TPU v7x, 32 devices: a whole 2x2x4 slice. The times are simulated.
32 devices in a mesh: src: 4 (over x, core), tgt: 8 (over z, y).
Axes of the slice: x: 2, y: 2, z: 4, core: 2. Of those that a mesh axis runs over, the one named last changes fastest.
Arguments:
- source_feat: bfloat16 [4096, 256], P(('src', 'tgt')), may hold values from -40 to 40
- target_feat: bfloat16 [14400, 256], P('tgt', 'src'), may hold values from -4 to 4
- proj: bfloat16 [256, 256], replicated, may hold values from -0.375 to 0.375
Outputs:
- flow: float32 [2, 4096], P(None, ('src', 'tgt'))
- matched: bfloat16 [4096, 256], P(('src', 'tgt'))
All inputs are finite; a program needn't handle non-finite values.
Results may differ from a plain program's by a relative error of at most 0.0075.
Values may be sent and summed in bfloat16 or wider, within the bound.
No kernel may reach another device: no remote copies, remote signals or barrier semaphores. Data moves between devices by JAX's collectives and lax.ppermute only.
A program may use at most 256 MiB of HBM per device.

v0:
```python
import jax
import jax.numpy as jnp
from jax import lax
from jax.sharding import PartitionSpec as P

W_GRID = 320


def grid_coords(pos):
    return (
        (pos % W_GRID).astype(jnp.float32) / W_GRID,
        (pos // W_GRID).astype(jnp.float32) / W_GRID,
    )


def partial_block(queries, keys, key_start):
    width = queries.shape[1]
    scores = jnp.einsum("qc,kc->qk", queries, keys, preferred_element_type=jnp.float32) * width ** (
        -0.5
    )
    top = jnp.max(scores, axis=1)
    weights = jnp.exp(scores - top[:, None])
    total = jnp.sum(weights, axis=1)
    pos = key_start + jnp.arange(keys.shape[0], dtype=jnp.int32)
    grid_x, grid_y = grid_coords(pos)
    coord_sum = jnp.stack(
        [jnp.sum(weights * grid_x[None, :], axis=1), jnp.sum(weights * grid_y[None, :], axis=1)],
        axis=0,
    )
    feat_sum = jnp.dot(weights.astype(jnp.bfloat16), keys, preferred_element_type=jnp.float32)
    return (top, total, coord_sum, feat_sum)


def per_device(source_feat, target_feat, proj):
    width = proj.shape[1]
    own_rows = source_feat.shape[0]
    tgt_rows = target_feat.shape[0]
    strips = lax.axis_size("tgt")
    queries = jnp.dot(source_feat, proj, preferred_element_type=jnp.float32).astype(jnp.bfloat16)
    keys = jnp.dot(
        lax.all_gather(target_feat, "src", axis=1, tiled=True),
        proj,
        preferred_element_type=jnp.float32,
    ).astype(jnp.bfloat16)
    own_start = (lax.axis_index("src") * strips + lax.axis_index("tgt")) * own_rows
    strip = lax.all_gather(queries, "tgt", axis=0, tiled=True)
    strip_rows = strip.shape[0]
    block = min(256, strip_rows)
    key_start = lax.axis_index("tgt") * tgt_rows

    def one_block(qblock):
        return partial_block(qblock, keys, key_start)

    top, total, coord_sum, feat_sum = lax.map(
        one_block, strip.reshape(strip_rows // block, block, width)
    )
    top = top.reshape(strip_rows)
    total = total.reshape(strip_rows)
    coord_sum = jnp.moveaxis(coord_sum, 1, 0).reshape(2, strip_rows)
    feat_sum = feat_sum.reshape(strip_rows, width)
    largest = lax.pmax(top, "tgt")
    rescale = jnp.exp(top - largest)
    total, coord_sum, feat_sum = (
        lax.psum_scatter(total * rescale, "tgt", scatter_dimension=0, tiled=True),
        lax.psum_scatter(coord_sum * rescale[None, :], "tgt", scatter_dimension=1, tiled=True),
        lax.psum_scatter(feat_sum * rescale[:, None], "tgt", scatter_dimension=0, tiled=True),
    )
    own_pos = own_start + jnp.arange(own_rows, dtype=jnp.int32)
    own_x, own_y = grid_coords(own_pos)
    flow = jnp.stack([coord_sum[0] / total - own_x, coord_sum[1] / total - own_y], axis=0)
    matched = (feat_sum / total[:, None]).astype(jnp.bfloat16)
    return (flow, matched)


def solution(mesh):
    in_specs = (P(("src", "tgt"), None), P("tgt", "src"), P())
    out_specs = (P(None, ("src", "tgt")), P(("src", "tgt"), None))
    return jax.shard_map(
        per_device, mesh=mesh, in_specs=in_specs, out_specs=out_specs, check_vma=False
    )
```

profile of v0, /device:TPU:0, one launch (start us, length us, event | category | flops | bytes accessed | tf_op | source)
XLA Modules:
  0.0 219.3 jit_solution(3305022111221268667)
XLA Ops:
  7.2 0.0 reduce-scatter.7.cloned.1.call-start
  7.3 11.3 %all_gather.7 = bf16[1800,256]{0,1:T(8,128)(2,1)S(1)} all-gather(bf16[1800,64]{0,1:T(8,128)(2,1)} %param.6), channel_id=1, replica_groups=mesh['src'=4,'tgt'=8] {'src'}, dimensions={1}, use_global_device_ids=true | all-gather | bytes 1152000 | tf_op jit(solution)/shard_map/all_gather | solution.py:41
  18.6 0.4 convolution_convert_fusion
  19.1 0.2 convolution_convert_fusion.1
  19.2 31.9 %all_gather.6 = bf16[1024,256]{1,0:T(8,128)(2,1)S(1)} all-gather(bf16[128,256]{1,0:T(8,128)(2,1)S(1)} %convolution_convert_fusion.1), channel_id=1, replica_groups=mesh['src'=4,'tgt'=8] {'tgt'}, dimensions={0}, use_global_device_ids=true | all-gather | bytes 589824 | tf_op jit(solution)/shard_map/all_gather | solution.py:46
  51.1 11.8 %while.18 = (s32[]{:T(128)}, f32[4,256]{1,0:T(4,128)S(1)}, f32[4,256]{1,0:T(4,128)S(1)}, f32[4,2,256]{2,1,0:T(2,128)S(1)}, f32[4,256,256]{2,1,0:T(8,128)}, /*ind...) while((s32[]{:T(128)}, f32[4,256]{1,0:T(4,128)S(1)}, ...), condition=%wide.region_5.6_spmd, body=%wide.region_0.5_spmd.sunk | while | flops 476497280 | bytes 7809785 | solution.py:54
  51.1 0.5 fusion.44
  51.7 1.0 multiply_reduce_fusion.3
  52.8 1.2 fusion.47
  54.0 0.5 fusion.44
  54.6 1.0 multiply_reduce_fusion.3
  55.7 1.3 fusion.47
  57.0 0.5 fusion.44
  57.5 1.0 multiply_reduce_fusion.3
  58.6 1.3 fusion.47
  59.9 0.5 fusion.44
  60.5 1.0 multiply_reduce_fusion.3
  61.6 1.3 fusion.47
  62.9 21.3 %pmax.7 = f32[1024]{0:T(1024)S(1)} all-reduce(f32[1024]{0:T(1024)S(1)} %bitcast.77), channel_id=1, replica_groups=mesh['src'=4,'tgt'=8] {'tgt'}, use_global_device_ids=true, to_apply=%region_6.7 | all-reduce | flops 1024 | bytes 8192 | tf_op jit(solution)/shard_map/pmax | solution.py:61
  84.2 1.1 copy.5
  85.3 0.0 reduce-scatter.5.cloned.1.call-start
  85.4 1.2 bitcast_multiply_fusion
  86.6 0.6 dynamic-slice
  87.8 17.2 %all-reduce = f32[1024]{0:T(1024)S(1)} all-reduce(f32[1024]{0:T(1024)S(1)} %get-tuple-element.134), channel_id=3, replica_groups=mesh['src'=4,'tgt'=8] {'tgt'}, use_global_device_ids=true, to_apply=%region_8.9.clone | all-reduce | flops 1024 | bytes 8192
  105.1 39.2 %reduce-scatter.7.cloned.1.call-done = f32[128,2]{1,0:T(8,128)} async-done(((f32[1024,2]{1,0:T(8,128)}), f32[128,2]{1,0:T(8,128)}) %reduce-scatter.7.cloned.1.call-update) | async-done | bytes 1040
  144.2 1.0 fusion.27
  145.2 0.1 copy.7
  145.3 0.1 copy.8
  145.3 0.1 fusion.24
  145.5 0.6 pad_maximum_fusion
  146.0 64.8 %reduce-scatter.5.cloned.1.call-done = f32[128,256]{1,0:T(8,128)} async-done(((f32[1024,256]{1,0:T(8,128)}), f32[128,256]{1,0:T(8,128)}) %reduce-scatter.5.cloned.1.call-update) | async-done | bytes 131088 | tf_op jit(solution)/shard_map/reduce_scatter | solution.py:66
  210.9 1.6 divide_convert_fusion
  (35 shorter events, 0.5 us)
Async XLA Ops:
  7.2 11.4 %copy-start = (bf16[256,256]{1,0:T(8,128)(2,1)S(1)}, bf16[256,256]{1,0:T(8,128)(2,1)}, u32[]{:S(2)}) copy-start(bf16[256,256]{1,0:T(8,128)(2,1)} %param.7) | copy-start | bytes 393220
  7.2 11.9 %copy-start.2 = (bf16[128,256]{1,0:T(8,128)(2,1)S(1)}, bf16[128,256]{1,0:T(8,128)(2,1)}, u32[]{:S(2)}) copy-start(bf16[128,256]{1,0:T(8,128)(2,1)} %param.5) | copy-start | bytes 196612
  7.2 137.0 %reduce-scatter.7.cloned.1.call-start = ((), (), s32[]{:S(2)}) async-start(), calls=%async_computation.3 | async-start | bytes 589824
  62.9 22.5 %copy-start.1 = (f32[4,256,256]{2,1,0:T(8,128)S(1)}, f32[4,256,256]{2,1,0:T(8,128)}, u32[]{:S(2)}) copy-start(f32[4,256,256]{2,1,0:T(8,128)} %get-tuple-element.112) | copy-start | bytes 3145732
  85.3 1.3 copy-start.3
  85.3 125.6 %reduce-scatter.5.cloned.1.call-start = ((), (), s32[]{:S(2)}) async-start(), calls=%async_computation.2 | async-start | bytes 1179648 | tf_op jit(solution)/shard_map/reduce_scatter | solution.py:66
Sparse Core Ops, SparseCore 0:
  85.4 58.7 reduce-scatter.6
  148.0 62.8 reduce-scatter.4
where the time goes:
time: 220 us; the launch traced here: 219 us
  waiting for transfers between devices  104 us (47%)
  blocking collectives  81.7 us (37%)
  between operations  14.8 us (7%)
  other arithmetic  7.84 us (4%)
  matrix products  7.68 us (3%)
  local copies, waits for them, and re-layouts  3.1 us (1%)
    reduce_scatter x1, waiting for transfers between devices, per_device(): lax.psum_scatter(feat_sum * rescale[:, None], 'tgt', scatter_dimension=0,...  64.8 us
    unnamed x3, waiting for transfers between devices  39.2 us
    all_gather x1, blocking collectives, per_device(): strip = lax.all_gather(queries, 'tgt', axis=0, tiled=True)  31.9 us
    pmax x1, blocking collectives, per_device(): largest = lax.pmax(top, 'tgt')  21.3 us
    unnamed x1, blocking collectives  17.2 us
    all_gather x1, blocking collectives, per_device(): lax.all_gather(target_feat, 'src', axis=1, tiled=True)  11.3 us
    dot_general x4, matrix products, partial_block(): jnp.dot(weights.astype(jnp.bfloat16), keys, preferred_element_type=jnp.fl...  5.02 us
  transfers between devices with their start and end apart: 2, of which 2 were waited for; matrix products, arithmetic and copies ran while one was open for 2% of the time, Pallas kernels for 0%

commit v1 on v0

v1 whole, which is shorter than its diff:
```python
import functools
import math

import jax
import jax.numpy as jnp
from jax import lax
from jax.experimental import pallas as pl
from jax.experimental.pallas import tpu as pltpu
from jax.sharding import PartitionSpec as P

W_GRID = 320
STAT_ROWS = 16
F32, BF16 = jnp.float32, jnp.bfloat16


def grid_coords(pos):
    return (
        (pos % W_GRID).astype(F32) / W_GRID,
        (pos // W_GRID).astype(F32) / W_GRID,
    )


def coord_rows(start, count):
    pos = start + lax.broadcasted_iota(jnp.int32, (STAT_ROWS, count), 1)
    row = lax.broadcasted_iota(jnp.int32, (STAT_ROWS, count), 0)
    gx, gy = pos % W_GRID, pos // W_GRID
    rows = jnp.where(row == 0, 1, 0)
    for index, value in enumerate((gx // 16, gx % 16, gy // 16, gy % 16)):
        rows = jnp.where(row == index + 1, value, rows)
    return rows.astype(BF16)


def split3(value):
    high = value.astype(BF16)
    rest = value - high.astype(F32)
    mid = rest.astype(BF16)
    low = (rest - mid.astype(F32)).astype(BF16)
    return [high.astype(F32), mid.astype(F32), low.astype(F32)]


def attend(pieces, projt, rows, queries, scale, kext):
    width = projt.shape[0]
    strip = jnp.concatenate([p[...] for p in pieces], axis=0)
    kext[0:width, :] = jnp.dot(projt[...], strip, preferred_element_type=F32).astype(BF16)
    kext[width:, :] = rows[...]
    raw = jnp.dot(queries, kext[0:width, :], preferred_element_type=F32)
    top = jnp.max(raw, axis=1, keepdims=True)
    weights = jnp.exp2((raw - top) * scale).astype(BF16)
    sums = lax.dot_general(
        kext[...], weights, (((1,), (1,)), ((), ())), preferred_element_type=F32
    )
    return top, sums


def as_row(column):
    return jnp.transpose(jnp.broadcast_to(column, (column.shape[0], 128)))[0:1, :]


def first_kernel(n_src, scale, *refs):
    pieces, (projt, proj, rows), refs = refs[:n_src], refs[n_src : n_src + 3], refs[n_src + 3 :]
    *sources, top_ref, sums_ref, query_ref, kext = refs
    source = jnp.concatenate([s[...] for s in sources], axis=0)
    queries = jnp.dot(source, proj[...], preferred_element_type=F32).astype(BF16)
    query_ref[...] = queries
    top, sums = attend(pieces, projt, rows, queries, scale, kext)
    top_ref[...] = as_row(top)
    sums_ref[...] = sums


def second_kernel(n_src, scale, *refs):
    pieces = refs[:n_src]
    projt, rows, query_ref, top_ref, sums_ref, out_ref, kext = refs[n_src:]
    top2, sums2 = attend(pieces, projt, rows, query_ref[...], scale, kext)
    top1, top2 = top_ref[...], as_row(top2)
    top = jnp.maximum(top1, top2)
    sums = sums_ref[...] * jnp.exp2((top1 - top) * scale) + sums2 * jnp.exp2((top2 - top) * scale)
    width = sums.shape[0] - STAT_ROWS
    stats = sums[width:]
    coord_x = stats[1:2] * 16.0 + stats[2:3]
    coord_y = stats[3:4] * 16.0 + stats[4:5]
    parts = split3(top) + split3(stats[0:1]) + split3(coord_x) + split3(coord_y)
    parts.append(jnp.zeros((STAT_ROWS - len(parts), top.shape[1]), F32))
    tail = jnp.concatenate(parts, axis=0).astype(BF16)
    blocks, _, lanes = out_ref.shape
    for index in range(blocks):
        cols = slice(index * lanes, (index + 1) * lanes)
        out_ref[index, 0:width, :] = sums[0:width, cols].astype(BF16)
        out_ref[index, width:, :] = tail[:, cols]


def merge_kernel(scale, *refs):
    *parts, own_ref, flow_ref, matched_ref = refs
    width = matched_ref.shape[1]
    stats = [p[width:, :].astype(F32) for p in parts]
    join = lambda s, k: s[3 * k : 3 * k + 1] + s[3 * k + 1 : 3 * k + 2] + s[3 * k + 2 : 3 * k + 3]
    tops = [join(s, 0) for s in stats]
    top = functools.reduce(jnp.maximum, tops)
    factors = [jnp.exp2((t - top) * scale) for t in tops]
    total, coord_x, coord_y = (
        sum(f * join(s, k) for f, s in zip(factors, stats)) for k in (1, 2, 3)
    )
    feat = sum(f * p[0:width, :].astype(F32) for f, p in zip(factors, parts))
    flow_ref[0:1, :] = coord_x / (total * W_GRID) - own_ref[0:1, :]
    flow_ref[1:2, :] = coord_y / (total * W_GRID) - own_ref[1:2, :]
    matched_ref[...] = jnp.transpose(feat / total).astype(matched_ref.dtype)


def call(kernel, outs, scratch, flops, args):
    size = lambda a: math.prod(a.shape) * a.dtype.itemsize
    return pl.pallas_call(
        kernel,
        out_shape=outs,
        scratch_shapes=scratch,
        compiler_params=pltpu.CompilerParams(vmem_limit_bytes=40 * 2**20),
        cost_estimate=pl.CostEstimate(
            flops=flops,
            bytes_accessed=sum(map(size, args)) + sum(map(size, jax.tree.leaves(outs))),
            transcendentals=0,
        ),
    )(*args)


def per_device(source_feat, target_feat, proj):
    width = proj.shape[1]
    own_rows = source_feat.shape[0]
    count, depth = target_feat.shape
    n_src, n_tgt = lax.axis_size("src"), lax.axis_size("tgt")
    src, tgt = lax.axis_index("src"), lax.axis_index("tgt")
    scale = math.log2(math.e) * width ** (-0.5)
    axes = ("src", "tgt")

    def swap(x, s=0, t=0):
        pairs = [
            (a * n_tgt + b, (a ^ s) * n_tgt + (b ^ t)) for a in range(n_src) for b in range(n_tgt)
        ]
        return lax.ppermute(x, axes, pairs)

    strip = target_feat.T
    far = [swap(strip, s=2), swap(strip, t=1), swap(strip, s=2, t=1)]
    near = swap(strip, s=1)
    sources = [source_feat] + [swap(source_feat, t=2 * k) for k in range(1, n_tgt // 2)]
    near_far = [swap(x, s=1) for x in far]
    first = [strip, near, far[0], near_far[0]]
    second = [far[1], near_far[1], far[2], near_far[2]]

    order = src ^ jnp.arange(n_src, dtype=jnp.int32)
    projt = jnp.take(proj.reshape(n_src, depth, width), order, axis=0).reshape(width, width).T
    rows = [coord_rows((tgt ^ k) * count, count) for k in (0, 1)]

    n_q = own_rows * len(sources)
    ext = width + STAT_ROWS
    shape = jax.ShapeDtypeStruct
    flops = 2 * count * width * (width + 2 * n_q)
    kext = [pltpu.VMEM((ext, count), BF16)]
    top, sums, queries = call(
        functools.partial(first_kernel, n_src, scale),
        (shape((1, n_q), F32), shape((ext, n_q), F32), shape((n_q, width), BF16)),
        kext,
        flops,
        (*first, projt, proj, rows[0], *sources),
    )
    message = call(
        functools.partial(second_kernel, n_src, scale),
        shape((len(sources), ext, own_rows), BF16),
        kext,
        flops,
        (*second, projt, rows[1], queries, top, sums),
    )
    parts = [message[0]] + [swap(message[k], t=2 * k) for k in range(1, len(sources))]
    own_pos = (src * n_tgt + tgt) * own_rows + jnp.arange(own_rows, dtype=jnp.int32)
    own = jnp.stack(grid_coords(own_pos), axis=0)
    return call(
        functools.partial(merge_kernel, scale),
        (shape((2, own_rows), F32), shape((own_rows, width), BF16)),
        [],
        4 * ext * own_rows * len(parts),
        (*parts, own),
    )


def solution(mesh):
    in_specs = (P(("src", "tgt"), None), P("tgt", "src"), P())
    out_specs = (P(None, ("src", "tgt")), P(("src", "tgt"), None))
    return jax.shard_map(
        per_device, mesh=mesh, in_specs=in_specs, out_specs=out_specs, check_vma=False
    )
```

time: 220 us -> 40.4 us (0.18)
  waiting for transfers between devices: 104 us -> 19.1 us
  blocking collectives: 81.7 us -> 0 us
  between operations: 14.8 us -> 0.8 us
  starting transfers between devices: 0.08 us -> 13.9 us
  matrix products: 7.68 us -> 0 us
  other arithmetic: 7.84 us -> 0.46 us
  Pallas kernels: 0 us -> 4.49 us
    reduce_scatter x1 -> x0, waiting for transfers between devices: 64.8 us -> none  [per_device(): lax.psum_scatter(feat_sum * rescale[:, None], 'tgt', scatter_dimension=0,...]
    all_gather x2 -> x0, blocking collectives: 43.2 us -> none  [the longest x1 31.9 us: per_device(): strip = lax.all_gather(queries, 'tgt', axis=0, tiled=True)]
    unnamed x3 -> x0, waiting for transfers between devices: 39.2 us -> none
    pmax x1 -> x0, blocking collectives: 21.3 us -> none  [per_device(): largest = lax.pmax(top, 'tgt')]
    ppermute x0 -> x13, waiting for transfers between devices: none -> 19.1 us  [swap(): return lax.ppermute(x, axes, pairs)]
    unnamed x1 -> x0, blocking collectives: 17.2 us -> none
    ppermute x0 -> x13, starting transfers between devices: none -> 13.9 us  [swap(): return lax.ppermute(x, axes, pairs)]
    dot_general x10 -> x0, matrix products: 7.68 us -> none  [the longest x4 5.02 us: partial_block(): jnp.dot(weights.astype(jnp.bfloat16), keys, preferred_element_type=jnp.fl...]
  transfers between devices with their start and end apart: 2 -> 13, of which waited for: 2 -> 7; matrix products, arithmetic and copies ran while one was open for 2% -> 3% of each run, Pallas kernels for 0% -> 5%
where the time goes in v1:
time: 40.4 us; the launch traced here: 40.2 us
  waiting for transfers between devices  19.1 us (47%)
  starting transfers between devices  13.9 us (34%)
  Pallas kernels  4.49 us (11%)
  local copies, waits for them, and re-layouts  1.48 us (4%)
  between operations  0.8 us (2%)
  other arithmetic  0.46 us (1%)
    ppermute x13, waiting for transfers between devices, swap(): return lax.ppermute(x, axes, pairs)  19.1 us
    ppermute x13, starting transfers between devices, swap(): return lax.ppermute(x, axes, pairs)  13.9 us
    pallas_call x3, Pallas kernels, call(): pl.pallas_call(kernel, out_shape=outs, scratch_shapes=scratch, compiler_p...  4.49 us
  transfers between devices with their start and end apart: 13, of which 7 were waited for; matrix products, arithmetic and copies ran while one was open for 3% of the time, Pallas kernels for 5%

profile of v1, /device:TPU:0, one launch (start us, length us, event | category | flops | bytes accessed | tf_op | source)
XLA Modules:
  0.0 40.2 jit_solution(6111619160571223499)
XLA Ops:
  0.6 4.1 %collective-permute-start.8 = (bf16[128,256]{1,0:T(8,128)(2,1)}, bf16[128,256]{1,0:T(8,128)(2,1)S(1)}, u32[]{:S(2)}, u32[]{:S(2)}) collective-permute-start(bf16[128,256]{1,0:T(8,128)(2,1)} %refs_7_.1), channel_id=1, source_target_pairs={{0,4},{1,5},{2,6},{3,7},{4,0},{5,1},{6,2},{7,3},{8,12},{9,13},{10,... | collective-permute-start | bytes 196616 | tf_op jit(solution)/shard_map/ppermute | solution.py:136
  4.7 1.6 %collective-permute-start.7 = (bf16[128,256]{1,0:T(8,128)(2,1)}, bf16[128,256]{1,0:T(8,128)(2,1)S(1)}, u32[]{:S(2)}, u32[]{:S(2)}) collective-permute-start(bf16[128,256]{1,0:T(8,128)(2,1)} %refs_7_.1), channel_id=1, source_target_pairs={{0,2},{1,3},{2,0},{3,1},{4,6},{5,7},{6,4},{7,5},{8,10},{9,11},{10,... | collective-permute-start | bytes 196616 | tf_op jit(solution)/shard_map/ppermute | solution.py:136
  6.3 1.5 %collective-permute-start.5 = (bf16[64,1800]{1,0:T(8,128)(2,1)}, bf16[64,1800]{1,0:T(8,128)(2,1)S(1)}, u32[]{:S(2)}, u32[]{:S(2)}) collective-permute-start(bf16[64,1800]{1,0:T(8,128)(2,1)} %bitcast.16), channel_id=1, source_target_pairs={{0,16},{1,17},{2,18},{3,19},{4,20},{5,21},{6,22},{7,23},{8,24},{9,... | collective-permute-start | bytes 691208 | tf_op jit(solution)/shard_map/ppermute | solution.py:136
  7.8 1.5 %collective-permute-start.2 = (bf16[64,1800]{1,0:T(8,128)(2,1)}, bf16[64,1800]{1,0:T(8,128)(2,1)S(1)}, u32[]{:S(2)}, u32[]{:S(2)}) collective-permute-start(bf16[64,1800]{1,0:T(8,128)(2,1)} %bitcast.17), channel_id=1, source_target_pairs={{0,17},{1,16},{2,19},{3,18},{4,21},{5,20},{6,23},{7,22},{8,25},{9,... | collective-permute-start | bytes 691208 | tf_op jit(solution)/shard_map/ppermute | solution.py:136
  9.3 0.5 %collective-permute-start = (bf16[64,1800]{1,0:T(8,128)(2,1)}, bf16[64,1800]{1,0:T(8,128)(2,1)S(1)}, u32[]{:S(2)}, u32[]{:S(2)}) collective-permute-start(bf16[64,1800]{1,0:T(8,128)(2,1)} %bitcast.18), channel_id=1, source_target_pairs={{0,1},{1,0},{2,3},{3,2},{4,5},{5,4},{6,7},{7,6},{8,9},{9,8},{10,11... | collective-permute-start | bytes 691208 | tf_op jit(solution)/shard_map/ppermute | solution.py:136
  9.9 0.0 copy-start
  10.0 0.3 fusion.6
  10.3 0.1 broadcast_in_dim.20
  10.3 0.1 broadcast_in_dim.21
  10.4 0.4 copy-done
  10.8 0.6 %gather_fusion = bf16[4,64,256]{2,1,0:T(8,128)(2,1)S(1)} fusion(bf16[4,64,256]{2,1,0:T(8,128)(2,1)S(1)} %bitcast.15, s32[1024]{0:T(1024)S(1)} %pad_clamp_fusion), kind=kCustom, calls=%fused_computation | custom fusion | bytes 262160 | tf_op jit(solution)/shard_map/jit(_take)/gather | solution.py:147
  11.4 0.1 copy.5
  11.5 0.0 copy-start.2
  11.5 0.0 collective-permute-done.8.refs_9_
  11.5 0.3 copy-done.1
  11.8 0.0 collective-permute-start.4
  11.8 3.6 %collective-permute-done.5.refs_2_ = bf16[64,1800]{1,0:T(8,128)(2,1)S(1)} collective-permute-done((bf16[64,1800]{1,0:T(8,128)(2,1)}, bf16[64,1800]{1,0:T(8,128)(2,1)S(1)}, u32[]{:S(2)}, u32[]{:S(2)}) %collective-permute-start.5) | collective-permute-done | bytes 230432 | tf_op jit(solution)/shard_map/ppermute | solution.py:136
  15.4 4.6 %collective-permute-done.2.refs_2_ = bf16[64,1800]{1,0:T(8,128)(2,1)S(1)} collective-permute-done((bf16[64,1800]{1,0:T(8,128)(2,1)}, bf16[64,1800]{1,0:T(8,128)(2,1)S(1)}, u32[]{:S(2)}, u32[]{:S(2)}) %collective-permute-start.2) | collective-permute-done | bytes 230432 | tf_op jit(solution)/shard_map/ppermute | solution.py:136
  20.0 0.0 collective-permute-start.3
  20.0 1.4 %collective-permute-done.refs_0_ = bf16[64,1800]{1,0:T(8,128)(2,1)S(1)} collective-permute-done((bf16[64,1800]{1,0:T(8,128)(2,1)}, bf16[64,1800]{1,0:T(8,128)(2,1)S(1)}, u32[]{:S(2)}, u32[]{:S(2)}) %collective-permute-start) | collective-permute-done | bytes 230432 | tf_op jit(solution)/shard_map/ppermute | solution.py:136
  21.4 0.3 collective-permute-start.9
  21.7 6.0 %collective-permute-done.9.refs_10_ = bf16[128,256]{1,0:T(8,128)(2,1)S(1)} collective-permute-done((bf16[128,256]{1,0:T(8,128)(2,1)S(1)}, bf16[128,256]{1,0:T(8,128)(2,1)S(1)}, u32[]{:S(2)}, u32[]{:S(2)}) %collective-permute-start.9) | collective-permute-done | bytes 65568 | tf_op jit(solution)/shard_map/ppermute | solution.py:136
  27.8 1.9 %shard_map.50 = (f32[1,512]{1,0:T(1,128)S(1)}, f32[272,512]{1,0:T(8,128)S(1)}, bf16[512,256]{1,0:T(8,128)(2,1)S(1)}) custom-call(bf16[64,1800]{1,0:T(8,128)(2,1)S(1)} %bitcast.20, bf16[64,1800]{1,0:T(8,128)(2,1)S(1)} %collective-permute-done.4.refs_1_, bf16[64,1800]{1,0:T(8,128)(2,1)S(1)} %collective-permute-done.5.refs_2_, ...), custom_call_target="tpu_custom_call" | custom-call | flops 1179648000 | bytes 2324736 | tf_op jit(solution)/shard_map/pallas_call | solution.py:110
  29.7 0.0 collective-permute-done.3.refs_3_
  29.7 1.8 %shard_map.51 = bf16[4,272,128]{2,1,0:T(8,128)(2,1)S(1)} custom-call(bf16[64,1800]{1,0:T(8,128)(2,1)S(1)} %collective-permute-done.refs_0_, bf16[64,1800]{1,0:T(8,128)(2,1)S(1)} %collective-permute-done.1.refs_1_, bf16[64,1800]{1,0:T(8,128)(2,1)S(1)} %collective-permute-done.2.refs_2_, bf16[64,1800]{1,0:T(8,128)(2,1)S(1)} %collective-permute-done.3.refs_3_, ...), custom_call_target="tpu_custom_call" | custom-call | flops 1179648000 | bytes 2210048 | tf_op jit(solution)/shard_map/pallas_call | solution.py:110
  31.5 0.5 %collective-permute-start.12 = (bf16[272,128]{1,0:T(8,128)(2,1)S(1)}, bf16[272,128]{1,0:T(8,128)(2,1)S(1)}, u32[]{:S(2)}, u32[]{:S(2)}) collective-permute-start(bf16[272,128]{1,0:T(8,128)(2,1)S(1)} %get-tuple-element.8), channel_id=1, source_target_pairs={{0,6},{1,7},{2,4},{3,5},{4,2},{5,3},{6,0},{7,1},{8,14},{9,15},{10,... | collective-permute-start | bytes 208904 | tf_op jit(solution)/shard_map/ppermute | solution.py:136
  32.0 0.0 collective-permute-start.11
  32.0 4.0 %collective-permute-start.10 = (bf16[272,128]{1,0:T(8,128)(2,1)S(1)}, bf16[272,128]{1,0:T(8,128)(2,1)S(1)}, u32[]{:S(2)}, u32[]{:S(2)}) collective-permute-start(bf16[272,128]{1,0:T(8,128)(2,1)S(1)} %get-tuple-element.10), channel_id=1, source_target_pairs={{0,2},{1,3},{2,0},{3,1},{4,6},{5,7},{6,4},{7,5},{8,10},{9,11},{10,... | collective-permute-start | bytes 208904 | tf_op jit(solution)/shard_map/ppermute | solution.py:136
  36.0 2.5 %collective-permute-done.12.refs_3_ = bf16[272,128]{1,0:T(8,128)(2,1)S(1)} collective-permute-done((bf16[272,128]{1,0:T(8,128)(2,1)S(1)}, bf16[272,128]{1,0:T(8,128)(2,1)S(1)}, u32[]{:S(2)}, u32[]{:S(2)}) %collective-permute-start.12) | collective-permute-done | bytes 69664 | tf_op jit(solution)/shard_map/ppermute | solution.py:136
  38.5 0.4 collective-permute-done.11.refs_2_
  38.9 0.5 %collective-permute-done.10.refs_1_ = bf16[272,128]{1,0:T(8,128)(2,1)S(1)} collective-permute-done((bf16[272,128]{1,0:T(8,128)(2,1)S(1)}, bf16[272,128]{1,0:T(8,128)(2,1)S(1)}, u32[]{:S(2)}, u32[]{:S(2)}) %collective-permute-start.10) | collective-permute-done | bytes 69664 | tf_op jit(solution)/shard_map/ppermute | solution.py:136
  39.5 0.8 %shard_map.52 = (f32[2,128]{1,0:T(2,128)}, bf16[128,256]{1,0:T(8,128)(2,1)}) custom-call(bf16[272,128]{1,0:T(8,128)(2,1)S(1)} %get-tuple-element.11.refs_0_, bf16[272,128]{1,0:T(8,128)(2,1)S(1)} %collective-permute-done.10.refs_1_, bf16[272,128]{1,0:T(8,128)(2,1)S(1)} %collective-permute-done.11.refs_2_, ...), custom_call_target="tpu_custom_call" | custom-call | flops 557056 | bytes 346112 | tf_op jit(solution)/shard_map/pallas_call | solution.py:110
  (24 shorter events, 0.2 us)
Async XLA Ops:
  0.6 10.9 %collective-permute-start.8 = (bf16[128,256]{1,0:T(8,128)(2,1)}, bf16[128,256]{1,0:T(8,128)(2,1)S(1)}, u32[]{:S(2)}, u32[]{:S(2)}) collective-permute-start(bf16[128,256]{1,0:T(8,128)(2,1)} %refs_7_.1), channel_id=1, source_target_pairs={{0,4},{1,5},{2,6},{3,7},{4,0},{5,1},{6,2},{7,3},{8,12},{9,13},{10,... | collective-permute-start | bytes 196616 | tf_op jit(solution)/shard_map/ppermute | solution.py:136
  4.7 16.6 %collective-permute-start.7 = (bf16[128,256]{1,0:T(8,128)(2,1)}, bf16[128,256]{1,0:T(8,128)(2,1)S(1)}, u32[]{:S(2)}, u32[]{:S(2)}) collective-permute-start(bf16[128,256]{1,0:T(8,128)(2,1)} %refs_7_.1), channel_id=1, source_target_pairs={{0,2},{1,3},{2,0},{3,1},{4,6},{5,7},{6,4},{7,5},{8,10},{9,11},{10,... | collective-permute-start | bytes 196616 | tf_op jit(solution)/shard_map/ppermute | solution.py:136
  6.3 9.1 %collective-permute-start.5 = (bf16[64,1800]{1,0:T(8,128)(2,1)}, bf16[64,1800]{1,0:T(8,128)(2,1)S(1)}, u32[]{:S(2)}, u32[]{:S(2)}) collective-permute-start(bf16[64,1800]{1,0:T(8,128)(2,1)} %bitcast.16), channel_id=1, source_target_pairs={{0,16},{1,17},{2,18},{3,19},{4,20},{5,21},{6,22},{7,23},{8,24},{9,... | collective-permute-start | bytes 691208 | tf_op jit(solution)/shard_map/ppermute | solution.py:136
  7.8 12.2 %collective-permute-start.2 = (bf16[64,1800]{1,0:T(8,128)(2,1)}, bf16[64,1800]{1,0:T(8,128)(2,1)S(1)}, u32[]{:S(2)}, u32[]{:S(2)}) collective-permute-start(bf16[64,1800]{1,0:T(8,128)(2,1)} %bitcast.17), channel_id=1, source_target_pairs={{0,17},{1,16},{2,19},{3,18},{4,21},{5,20},{6,23},{7,22},{8,25},{9,... | collective-permute-start | bytes 691208 | tf_op jit(solution)/shard_map/ppermute | solution.py:136
  9.3 12.1 %collective-permute-start = (bf16[64,1800]{1,0:T(8,128)(2,1)}, bf16[64,1800]{1,0:T(8,128)(2,1)S(1)}, u32[]{:S(2)}, u32[]{:S(2)}) collective-permute-start(bf16[64,1800]{1,0:T(8,128)(2,1)} %bitcast.18), channel_id=1, source_target_pairs={{0,1},{1,0},{2,3},{3,2},{4,5},{5,4},{6,7},{7,6},{8,9},{9,8},{10,11... | collective-permute-start | bytes 691208 | tf_op jit(solution)/shard_map/ppermute | solution.py:136
  9.9 0.9 %copy-start = (bf16[256,256]{1,0:T(8,128)(2,1)S(1)}, bf16[256,256]{1,0:T(8,128)(2,1)}, u32[]{:S(2)}) copy-start(bf16[256,256]{1,0:T(8,128)(2,1)} %refs_5_.1) | copy-start | bytes 393220
  10.8 0.9 %copy-start.1 = (bf16[1800,64]{0,1:T(8,128)(2,1)S(1)}, bf16[1800,64]{0,1:T(8,128)(2,1)}, u32[]{:S(2)}) copy-start(bf16[1800,64]{0,1:T(8,128)(2,1)} %param.4) | copy-start | bytes 691204
  11.5 9.9 %copy-start.2 = (bf16[128,256]{1,0:T(8,128)(2,1)S(1)}, bf16[128,256]{1,0:T(8,128)(2,1)}, u32[]{:S(2)}) copy-start(bf16[128,256]{1,0:T(8,128)(2,1)} %refs_7_.1) | copy-start | bytes 196612
  11.8 16.0 %collective-permute-start.4 = (bf16[64,1800]{1,0:T(8,128)(2,1)S(1)}, bf16[64,1800]{1,0:T(8,128)(2,1)S(1)}, u32[]{:S(2)}, u32[]{:S(2)}) collective-permute-start(bf16[64,1800]{1,0:T(8,128)(2,1)S(1)} %bitcast.19), channel_id=1, source_target_pairs={{0,8},{1,9},{2,10},{3,11},{4,12},{5,13},{6,14},{7,15},{8,0},{9,1},... | collective-permute-start | bytes 691208 | tf_op jit(solution)/shard_map/ppermute | solution.py:136
  15.4 12.4 %collective-permute-start.6 = (bf16[64,1800]{1,0:T(8,128)(2,1)S(1)}, bf16[64,1800]{1,0:T(8,128)(2,1)S(1)}, u32[]{:S(2)}, u32[]{:S(2)}) collective-permute-start(bf16[64,1800]{1,0:T(8,128)(2,1)S(1)} %collective-permute-done.5.refs_2_), channel_id=1, source_target_pairs={{0,8},{1,9},{2,10},{3,11},{4,12},{5,13},{6,14},{7,15},{8,0},{9,1},... | collective-permute-start | bytes 691208 | tf_op jit(solution)/shard_map/ppermute | solution.py:136
  20.0 9.7 %collective-permute-start.3 = (bf16[64,1800]{1,0:T(8,128)(2,1)S(1)}, bf16[64,1800]{1,0:T(8,128)(2,1)S(1)}, u32[]{:S(2)}, u32[]{:S(2)}) collective-permute-start(bf16[64,1800]{1,0:T(8,128)(2,1)S(1)} %collective-permute-done.2.refs_2_), channel_id=1, source_target_pairs={{0,8},{1,9},{2,10},{3,11},{4,12},{5,13},{6,14},{7,15},{8,0},{9,1},... | collective-permute-start | bytes 691208 | tf_op jit(solution)/shard_map/ppermute | solution.py:136
  21.3 8.3 %collective-permute-start.1 = (bf16[64,1800]{1,0:T(8,128)(2,1)S(1)}, bf16[64,1800]{1,0:T(8,128)(2,1)S(1)}, u32[]{:S(2)}, u32[]{:S(2)}) collective-permute-start(bf16[64,1800]{1,0:T(8,128)(2,1)S(1)} %collective-permute-done.refs_0_), channel_id=1, source_target_pairs={{0,8},{1,9},{2,10},{3,11},{4,12},{5,13},{6,14},{7,15},{8,0},{9,1},... | collective-permute-start | bytes 691208 | tf_op jit(solution)/shard_map/ppermute | solution.py:136
  21.4 6.4 %collective-permute-start.9 = (bf16[128,256]{1,0:T(8,128)(2,1)S(1)}, bf16[128,256]{1,0:T(8,128)(2,1)S(1)}, u32[]{:S(2)}, u32[]{:S(2)}) collective-permute-start(bf16[128,256]{1,0:T(8,128)(2,1)S(1)} %copy-done.2), channel_id=1, source_target_pairs={{0,6},{1,7},{2,4},{3,5},{4,2},{5,3},{6,0},{7,1},{8,14},{9,15},{10,... | collective-permute-start | bytes 196616 | tf_op jit(solution)/shard_map/ppermute | solution.py:136
  31.5 7.0 %collective-permute-start.12 = (bf16[272,128]{1,0:T(8,128)(2,1)S(1)}, bf16[272,128]{1,0:T(8,128)(2,1)S(1)}, u32[]{:S(2)}, u32[]{:S(2)}) collective-permute-start(bf16[272,128]{1,0:T(8,128)(2,1)S(1)} %get-tuple-element.8), channel_id=1, source_target_pairs={{0,6},{1,7},{2,4},{3,5},{4,2},{5,3},{6,0},{7,1},{8,14},{9,15},{10,... | collective-permute-start | bytes 208904 | tf_op jit(solution)/shard_map/ppermute | solution.py:136
  32.0 6.9 %collective-permute-start.11 = (bf16[272,128]{1,0:T(8,128)(2,1)S(1)}, bf16[272,128]{1,0:T(8,128)(2,1)S(1)}, u32[]{:S(2)}, u32[]{:S(2)}) collective-permute-start(bf16[272,128]{1,0:T(8,128)(2,1)S(1)} %get-tuple-element.9), channel_id=1, source_target_pairs={{0,4},{1,5},{2,6},{3,7},{4,0},{5,1},{6,2},{7,3},{8,12},{9,13},{10,... | collective-permute-start | bytes 208904 | tf_op jit(solution)/shard_map/ppermute | solution.py:136
  32.0 7.4 %collective-permute-start.10 = (bf16[272,128]{1,0:T(8,128)(2,1)S(1)}, bf16[272,128]{1,0:T(8,128)(2,1)S(1)}, u32[]{:S(2)}, u32[]{:S(2)}) collective-permute-start(bf16[272,128]{1,0:T(8,128)(2,1)S(1)} %get-tuple-element.10), channel_id=1, source_target_pairs={{0,2},{1,3},{2,0},{3,1},{4,6},{5,7},{6,4},{7,5},{8,10},{9,11},{10,... | collective-permute-start | bytes 208904 | tf_op jit(solution)/shard_map/ppermute | solution.py:136

commit v2 on v1

v2 whole, which is shorter than its diff:
```python
import functools
import math

import jax
import jax.numpy as jnp
from jax import lax
from jax.experimental import pallas as pl
from jax.experimental.pallas import tpu as pltpu
from jax.sharding import PartitionSpec as P

W_GRID = 320
STAT_ROWS = 16
F32, BF16 = jnp.float32, jnp.bfloat16


def grid_coords(pos):
    return (
        (pos % W_GRID).astype(F32) / W_GRID,
        (pos // W_GRID).astype(F32) / W_GRID,
    )


def coord_rows(start, count):
    pos = start + lax.broadcasted_iota(jnp.int32, (STAT_ROWS, count), 1)
    row = lax.broadcasted_iota(jnp.int32, (STAT_ROWS, count), 0)
    gx, gy = pos % W_GRID, pos // W_GRID
    rows = jnp.where(row == 0, 1, 0)
    for index, value in enumerate((gx // 16, gx % 16, gy // 16, gy % 16)):
        rows = jnp.where(row == index + 1, value, rows)
    return rows.astype(BF16)


def split3(value):
    high = value.astype(BF16)
    rest = value - high.astype(F32)
    mid = rest.astype(BF16)
    low = (rest - mid.astype(F32)).astype(BF16)
    return [high.astype(F32), mid.astype(F32), low.astype(F32)]


def project(pieces, projt, rows, strip, kext):
    depth, width = pieces[0].shape[0], projt.shape[0]
    src = lax.axis_index("src")
    for step, piece in enumerate(pieces):
        strip[pl.ds(pl.multiple_of((src ^ step) * depth, depth), depth), :] = piece
    kext[0:width, :] = jnp.dot(projt[...], strip[...], preferred_element_type=F32).astype(BF16)
    kext[width:, :] = rows[...]


def attend(queries, kext, scale):
    width = queries.shape[1]
    raw = jnp.dot(queries, kext[0:width, :], preferred_element_type=F32)
    top = jnp.max(raw, axis=1, keepdims=True)
    weights = jnp.exp2((raw - top) * scale).astype(BF16)
    sums = lax.dot_general(
        kext[...], weights, (((1,), (1,)), ((), ())), preferred_element_type=F32
    )
    return as_row(top), sums


def as_row(column):
    return jnp.transpose(jnp.broadcast_to(column, (column.shape[0], 128)))[0:1, :]


def pick(even, odd):
    return jnp.where(lax.axis_index("src") % 2 == 0, even[...], odd[...])


def first_kernel(scale, *refs):
    own, near, one, near_one, two, near_two, projt, proj, rows, source, *refs = refs
    top_ref, sums_ref, query_ref, kext, strip = refs
    queries = jnp.dot(source[...], proj[...], preferred_element_type=F32).astype(BF16)
    query_ref[...] = queries
    pieces = [own[...], near[...], pick(one, near_two), pick(two, near_one)]
    project(pieces, projt, rows, strip, kext)
    top_ref[...], sums_ref[...] = attend(queries[0 : top_ref.shape[1]], kext, scale)


def rest_kernel(scale, query_ref, kext, top_ref, sums_ref):
    count = top_ref.shape[1]
    top_ref[...], sums_ref[...] = attend(query_ref[count:, :], kext, scale)


def emit(queries, kext, top1, sums1, scale):
    top2, sums2 = attend(queries, kext, scale)
    top = jnp.maximum(top1, top2)
    sums = sums1 * jnp.exp2((top1 - top) * scale) + sums2 * jnp.exp2((top2 - top) * scale)
    stats = sums[queries.shape[1] :]
    coord_x = stats[1:2] * 16.0 + stats[2:3]
    coord_y = stats[3:4] * 16.0 + stats[4:5]
    parts = split3(top) + split3(stats[0:1]) + split3(coord_x) + split3(coord_y)
    parts.append(jnp.zeros((STAT_ROWS - len(parts), top.shape[1]), F32))
    return jnp.concatenate([sums[0 : queries.shape[1]], *parts], axis=0).astype(BF16)


def second_kernel(scale, *refs):
    one, near_one, two, near_two, cross, near_cross, projt, rows, *refs = refs
    query_ref, top_near, sums_near, top_far, sums_far, out_ref, kext, strip = refs
    pieces = [pick(near_two, one), pick(near_one, two), cross[...], near_cross[...]]
    project(pieces, projt, rows, strip, kext)
    lanes = out_ref.shape[2]
    top1 = jnp.concatenate([top_near[:, lanes:], top_far[...]], axis=1)
    sums1 = jnp.concatenate([sums_near[:, lanes:], sums_far[...]], axis=1)
    out = emit(query_ref[lanes:, :], kext, top1, sums1, scale)
    for index in range(out_ref.shape[0]):
        out_ref[index] = out[:, index * lanes : (index + 1) * lanes]


def last_kernel(scale, query_ref, kext, top_ref, sums_ref, out_ref):
    lanes = out_ref.shape[1]
    out_ref[...] = emit(
        query_ref[0:lanes, :], kext, top_ref[:, 0:lanes], sums_ref[:, 0:lanes], scale
    )


def merge_kernel(scale, *refs):
    *parts, own_ref, flow_ref, matched_ref = refs
    width = matched_ref.shape[1]
    stats = [p[width:, :].astype(F32) for p in parts]
    join = lambda s, k: s[3 * k : 3 * k + 1] + s[3 * k + 1 : 3 * k + 2] + s[3 * k + 2 : 3 * k + 3]
    tops = [join(s, 0) for s in stats]
    top = functools.reduce(jnp.maximum, tops)
    factors = [jnp.exp2((t - top) * scale) for t in tops]
    total, coord_x, coord_y = (
        sum(f * join(s, k) for f, s in zip(factors, stats)) for k in (1, 2, 3)
    )
    feat = sum(f * p[0:width, :].astype(F32) for f, p in zip(factors, parts))
    flow_ref[0:1, :] = coord_x / (total * W_GRID) - own_ref[0:1, :]
    flow_ref[1:2, :] = coord_y / (total * W_GRID) - own_ref[1:2, :]
    matched_ref[...] = jnp.transpose(feat / total).astype(matched_ref.dtype)


def call(kernel, outs, scratch, flops, args):
    size = lambda a: math.prod(a.shape) * a.dtype.itemsize
    return pl.pallas_call(
        kernel,
        out_shape=outs,
        scratch_shapes=scratch,
        compiler_params=pltpu.CompilerParams(vmem_limit_bytes=40 * 2**20),
        cost_estimate=pl.CostEstimate(
            flops=flops,
            bytes_accessed=sum(map(size, args)) + sum(map(size, jax.tree.leaves(outs))),
            transcendentals=0,
        ),
    )(*args)


def after(value, other):
    def kernel(value_ref, other_ref, out_ref):
        out_ref[...] = value_ref[...]

    return pl.pallas_call(
        kernel,
        out_shape=jax.ShapeDtypeStruct(value.shape, value.dtype),
        compiler_params=pltpu.CompilerParams(vmem_limit_bytes=8 * 2**20),
    )(value, other)


def per_device(source_feat, target_feat, proj):
    width = proj.shape[1]
    own_rows = source_feat.shape[0]
    count, depth = target_feat.shape
    n_src, n_tgt = lax.axis_size("src"), lax.axis_size("tgt")
    src, tgt = lax.axis_index("src"), lax.axis_index("tgt")
    scale = math.log2(math.e) * width ** (-0.5)
    axes = ("src", "tgt")

    def permute(x, move):
        pairs = []
        for a in range(n_src):
            for b in range(n_tgt):
                s, t = move(a)
                pairs.append((a * n_tgt + b, (a ^ s) * n_tgt + (b ^ t)))
        return lax.ppermute(x, axes, pairs)

    def swap(x, s=0, t=0):
        return permute(x, lambda a: (s, t))

    turn_one = lambda a: (2, 0) if a % 2 == 0 else (0, 1)
    turn_two = lambda a: (0, 1) if a % 2 == 0 else (2, 0)
    own = target_feat.T
    near = swap(own, s=1)
    one = permute(own, turn_one)
    two = permute(near, turn_one)
    sources, offsets = source_feat, [0]
    for bit in reversed(range(1, n_tgt.bit_length() - 1)):
        sources = jnp.concatenate([sources, swap(sources, t=1 << bit)], axis=0)
        offsets += [offset ^ (1 << bit) for offset in offsets]
    cross = permute(one, turn_two)
    near_one, near_two = swap(one, s=1), swap(two, s=1)

    projt = proj.T
    rows = [coord_rows((tgt ^ k) * count, count) for k in (0, 1)]

    n_q = sources.shape[0]
    blocks = n_q // own_rows
    half = n_q // 2
    ext = width + STAT_ROWS
    shape = jax.ShapeDtypeStruct
    flops = 2 * count * width * (width + 2 * n_q)
    kext = shape((ext, count), BF16)
    strip = [pltpu.VMEM((width, count), BF16)]
    top, sums, queries, keys = call(
        functools.partial(first_kernel, scale),
        (shape((1, half), F32), shape((ext, half), F32), shape((n_q, width), BF16), kext),
        strip,
        flops,
        (own, near, one, near_one, two, near_two, projt, proj, rows[0], sources),
    )
    near_cross = swap(after(cross, top), s=1)
    far_top, far_sums = call(
        functools.partial(rest_kernel, scale),
        (shape((1, half), F32), shape((ext, half), F32)),
        [],
        flops,
        (queries, keys),
    )
    out, keys = call(
        functools.partial(second_kernel, scale),
        (shape((blocks - 1, ext, own_rows), BF16), kext),
        strip,
        flops,
        (one, near_one, two, near_two, cross, near_cross, projt, rows[1], queries)
        + (top, sums, far_top, far_sums),
    )
    kept = call(
        functools.partial(last_kernel, scale),
        shape((ext, own_rows), BF16),
        [],
        flops,
        (queries, keys, top, sums),
    )
    parts = [kept] + [swap(out[k - 1], t=offsets[k]) for k in range(1, blocks)]
    own_pos = (src * n_tgt + tgt) * own_rows + jnp.arange(own_rows, dtype=jnp.int32)
    own = jnp.stack(grid_coords(own_pos), axis=0)
    return call(
        functools.partial(merge_kernel, scale),
        (shape((2, own_rows), F32), shape((own_rows, width), BF16)),
        [],
        4 * ext * own_rows * len(parts),
        (*parts, own),
    )


def solution(mesh):
    in_specs = (P(("src", "tgt"), None), P("tgt", "src"), P())
    out_specs = (P(None, ("src", "tgt")), P(("src", "tgt"), None))
    return jax.shard_map(
        per_device, mesh=mesh, in_specs=in_specs, out_specs=out_specs, check_vma=False
    )
```

time: 40.4 us -> 31.9 us (0.79)
  waiting for transfers between devices: 19.1 us -> 10.2 us
  Pallas kernels: 4.49 us -> 6.04 us
  local copies, waits for them, and re-layouts: 1.48 us -> 0.13 us
    ppermute x13 -> x12, waiting for transfers between devices: 19.1 us -> 10.2 us  [permute(): return lax.ppermute(x, axes, pairs)]
    pallas_call x3 -> x5, Pallas kernels: 4.49 us -> 6.02 us  [call(): pl.pallas_call(kernel, out_shape=outs, scratch_shapes=scratch, compiler_p...]
    gather x2 -> x0, local copies, waits for them, and re-layouts: 0.65 us -> none  [per_device(): jnp.take(proj.reshape(n_src, depth, width), order, axis=0)]
    unnamed x6 -> x7, local copies, waits for them, and re-layouts: 0.65 us -> 0.12 us
    ppermute x13 -> x12, starting transfers between devices: 13.9 us -> 14.1 us  [permute(): return lax.ppermute(x, axes, pairs)]
  transfers between devices with their start and end apart: 13 -> 12, of which waited for: 7 -> 7; matrix products, arithmetic and copies ran while one was open for 3% -> 2% of each run, Pallas kernels for 5% -> 11%
where the time goes in v2:
time: 31.9 us; the launch traced here: 31.7 us
  starting transfers between devices  14.1 us (44%)
  waiting for transfers between devices  10.2 us (32%)
  Pallas kernels  6.04 us (19%)
  between operations  0.82 us (3%)
  other arithmetic  0.45 us (1%)
    ppermute x12, starting transfers between devices, permute(): return lax.ppermute(x, axes, pairs)  14.1 us
    ppermute x12, waiting for transfers between devices, permute(): return lax.ppermute(x, axes, pairs)  10.2 us
    pallas_call x5, Pallas kernels, call(): pl.pallas_call(kernel, out_shape=outs, scratch_shapes=scratch, compiler_p...  6.02 us
  transfers between devices with their start and end apart: 12, of which 7 were waited for; matrix products, arithmetic and copies ran while one was open for 2% of the time, Pallas kernels for 11%

profile of v2, /device:TPU:0, one launch (start us, length us, event | category | flops | bytes accessed | tf_op | source)
XLA Modules:
  0.0 31.7 jit_solution(8498184687553263985)
XLA Ops:
  0.6 3.0 %collective-permute-start.1 = (bf16[64,1800]{1,0:T(8,128)(2,1)}, bf16[64,1800]{1,0:T(8,128)(2,1)S(1)}, u32[]{:S(2)}, u32[]{:S(2)}) collective-permute-start(bf16[64,1800]{1,0:T(8,128)(2,1)} %bitcast.10), channel_id=1, source_target_pairs={{0,16},{1,17},{2,18},{3,19},{4,20},{5,21},{6,22},{7,23},{8,9},{9,8... | collective-permute-start | bytes 691208 | tf_op jit(solution)/shard_map/ppermute | solution.py:174
  3.6 0.0 collective-permute-start
  3.6 2.6 %collective-permute-start.5 = (bf16[128,256]{1,0:T(8,128)(2,1)}, bf16[128,256]{1,0:T(8,128)(2,1)S(1)}, u32[]{:S(2)}, u32[]{:S(2)}) collective-permute-start(bf16[128,256]{1,0:T(8,128)(2,1)} %param.3), channel_id=1, source_target_pairs={{0,4},{1,5},{2,6},{3,7},{4,0},{5,1},{6,2},{7,3},{8,12},{9,13},{10,... | collective-permute-start | bytes 196616 | tf_op jit(solution)/shard_map/ppermute | solution.py:174
  6.4 0.0 collective-permute-done.refs_1_
  6.4 1.1 %collective-permute-start.3 = (bf16[64,1800]{1,0:T(8,128)(2,1)S(1)}, bf16[64,1800]{1,0:T(8,128)(2,1)S(1)}, u32[]{:S(2)}, u32[]{:S(2)}) collective-permute-start(bf16[64,1800]{1,0:T(8,128)(2,1)S(1)} %collective-permute-done.refs_1_), channel_id=1, source_target_pairs={{0,16},{1,17},{2,18},{3,19},{4,20},{5,21},{6,22},{7,23},{8,9},{9,8... | collective-permute-start | bytes 691208 | tf_op jit(solution)/shard_map/ppermute | solution.py:174
  7.5 3.1 %collective-permute-done.5 = bf16[128,256]{1,0:T(8,128)(2,1)S(1)} collective-permute-done((bf16[128,256]{1,0:T(8,128)(2,1)}, bf16[128,256]{1,0:T(8,128)(2,1)S(1)}, u32[]{:S(2)}, u32[]{:S(2)}) %collective-permute-start.5) | collective-permute-done | bytes 65568 | tf_op jit(solution)/shard_map/ppermute | solution.py:174
  10.7 0.0 copy-start
  10.7 0.8 %collective-permute-start.6 = (bf16[256,256]{1,0:T(8,128)(2,1)S(1)}, bf16[256,256]{1,0:T(8,128)(2,1)S(1)}, u32[]{:S(2)}, u32[]{:S(2)}) collective-permute-start(bf16[256,256]{1,0:T(8,128)(2,1)S(1)} %pad_maximum_fusion.1), channel_id=1, source_target_pairs={{0,2},{1,3},{2,0},{3,1},{4,6},{5,7},{6,4},{7,5},{8,10},{9,11},{10,... | collective-permute-start | bytes 393224 | tf_op jit(solution)/shard_map/ppermute | solution.py:174
  11.5 0.0 collective-permute-done.1.refs_2_.refs_0_
  11.5 1.5 %collective-permute-start.7 = (bf16[64,1800]{1,0:T(8,128)(2,1)S(1)}, bf16[64,1800]{1,0:T(8,128)(2,1)S(1)}, u32[]{:S(2)}, u32[]{:S(2)}) collective-permute-start(bf16[64,1800]{1,0:T(8,128)(2,1)S(1)} %collective-permute-done.1.refs_2_.refs_0_), channel_id=1, source_target_pairs={{0,1},{1,0},{2,3},{3,2},{4,5},{5,4},{6,7},{7,6},{8,24},{9,25},{10,... | collective-permute-start | bytes 691208 | tf_op jit(solution)/shard_map/ppermute | solution.py:174
  13.1 0.0 collective-permute-start.2
  13.1 0.0 collective-permute-done.3.refs_4_.refs_2_
  13.1 0.5 %collective-permute-start.4 = (bf16[64,1800]{1,0:T(8,128)(2,1)S(1)}, bf16[64,1800]{1,0:T(8,128)(2,1)S(1)}, u32[]{:S(2)}, u32[]{:S(2)}) collective-permute-start(bf16[64,1800]{1,0:T(8,128)(2,1)S(1)} %collective-permute-done.3.refs_4_.refs_2_), channel_id=1, source_target_pairs={{0,8},{1,9},{2,10},{3,11},{4,12},{5,13},{6,14},{7,15},{8,0},{9,1},... | collective-permute-start | bytes 691208 | tf_op jit(solution)/shard_map/ppermute | solution.py:174
  13.6 0.3 fusion.6
  13.9 0.1 copy.5
  14.0 0.0 copy-start.1
  14.0 1.7 %collective-permute-done.6 = bf16[256,256]{1,0:T(8,128)(2,1)S(1)} collective-permute-done((bf16[256,256]{1,0:T(8,128)(2,1)S(1)}, bf16[256,256]{1,0:T(8,128)(2,1)S(1)}, u32[]{:S(2)}, u32[]{:S(2)}) %collective-permute-start.6) | collective-permute-done | bytes 131104 | tf_op jit(solution)/shard_map/ppermute | solution.py:174
  15.7 0.0 collective-permute-done.2.refs_3_.refs_1_
  15.8 1.6 %shard_map.50 = (f32[1,256]{1,0:T(1,128)S(1)}, f32[272,256]{1,0:T(8,128)S(1)}, bf16[512,256]{1,0:T(8,128)(2,1)S(1)}, bf16[272,1800]{1,0:T(8,128)(2,1)S(1)}) custom-call(bf16[64,1800]{1,0:T(8,128)(2,1)S(1)} %bitcast.12, bf16[64,1800]{1,0:T(8,128)(2,1)S(1)} %collective-permute-done.refs_1_, bf16[64,1800]{1,0:T(8,128)(2,1)S(1)} %collective-permute-done.1.refs_2_.refs_0_, ...), custom_call_target="tpu_custom_call" | custom-call | flops 1179648000 | bytes 3485184 | tf_op jit(solution)/shard_map/pallas_call | solution.py:135
  17.4 0.3 collective-permute-done.7.value_ref.refs_4_
  17.8 0.1 collective-permute-start.8
  17.9 1.0 %shard_map.52 = (f32[1,256]{1,0:T(1,128)S(1)}, f32[272,256]{1,0:T(8,128)S(1)}) custom-call(bf16[512,256]{1,0:T(8,128)(2,1)S(1)} %get-tuple-element.10.query_ref.refs_8_, bf16[272,1800]{1,0:T(8,128)(2,1)S(1)} %get-tuple-element.13.kext), custom_call_target="tpu_custom_call" | custom-call | flops 1179648000 | bytes 1520896 | tf_op jit(solution)/shard_map/pallas_call | solution.py:135
  18.8 0.5 %collective-permute-done.8.refs_5_ = bf16[64,1800]{1,0:T(8,128)(2,1)S(1)} collective-permute-done((bf16[64,1800]{1,0:T(8,128)(2,1)S(1)}, bf16[64,1800]{1,0:T(8,128)(2,1)S(1)}, u32[]{:S(2)}, u32[]{:S(2)}) %collective-permute-start.8) | collective-permute-done | bytes 230432 | tf_op jit(solution)/shard_map/ppermute | solution.py:174
  19.3 1.8 %shard_map.53 = (bf16[3,272,128]{2,1,0:T(8,128)(2,1)S(1)}, bf16[272,1800]{1,0:T(8,128)(2,1)S(1)}) custom-call(bf16[64,1800]{1,0:T(8,128)(2,1)S(1)} %collective-permute-done.1.refs_2_.refs_0_, bf16[64,1800]{1,0:T(8,128)(2,1)S(1)} %collective-permute-done.2.refs_3_.refs_1_, bf16[64,1800]{1,0:T(8,128)(2,1)S(1)} %collective-permute-done.3.refs_4_.refs_2_, ...), custom_call_target="tpu_custom_call" | custom-call | flops 1179648000 | bytes 3580416 | tf_op jit(solution)/shard_map/pallas_call | solution.py:135
  21.2 3.8 %collective-permute-start.11 = (bf16[272,128]{1,0:T(8,128)(2,1)S(1)}, bf16[272,128]{1,0:T(8,128)(2,1)S(1)}, u32[]{:S(2)}, u32[]{:S(2)}) collective-permute-start(bf16[272,128]{1,0:T(8,128)(2,1)S(1)} %get-tuple-element.18), channel_id=1, source_target_pairs={{0,6},{1,7},{2,4},{3,5},{4,2},{5,3},{6,0},{7,1},{8,14},{9,15},{10,... | collective-permute-start | bytes 208904 | tf_op jit(solution)/shard_map/ppermute | solution.py:174
  24.9 0.1 collective-permute-start.10
  25.1 0.5 %collective-permute-start.9 = (bf16[272,128]{1,0:T(8,128)(2,1)S(1)}, bf16[272,128]{1,0:T(8,128)(2,1)S(1)}, u32[]{:S(2)}, u32[]{:S(2)}) collective-permute-start(bf16[272,128]{1,0:T(8,128)(2,1)S(1)} %get-tuple-element.20), channel_id=1, source_target_pairs={{0,4},{1,5},{2,6},{3,7},{4,0},{5,1},{6,2},{7,3},{8,12},{9,13},{10,... | collective-permute-start | bytes 208904 | tf_op jit(solution)/shard_map/ppermute | solution.py:174
  25.6 0.9 %shard_map.54.refs_0_ = bf16[272,128]{1,0:T(8,128)(2,1)S(1)} custom-call(bf16[512,256]{1,0:T(8,128)(2,1)S(1)} %get-tuple-element.10.query_ref.refs_8_, bf16[272,1800]{1,0:T(8,128)(2,1)S(1)} %get-tuple-element.16.kext, f32[1,256]{1,0:T(1,128)S(1)} %get-tuple-element.11.other_ref.refs_9_.top_ref, f32[272,256]{1,0:T(8,128)S(1)} %get-tuple-element.12.refs_10_.sums_ref), custom_call_target="tpu_custom_call" | custom-call | flops 1179648000 | bytes 1590528 | tf_op jit(solution)/shard_map/pallas_call | solution.py:135
  26.5 1.6 %collective-permute-done.11.refs_3_ = bf16[272,128]{1,0:T(8,128)(2,1)S(1)} collective-permute-done((bf16[272,128]{1,0:T(8,128)(2,1)S(1)}, bf16[272,128]{1,0:T(8,128)(2,1)S(1)}, u32[]{:S(2)}, u32[]{:S(2)}) %collective-permute-start.11) | collective-permute-done | bytes 69664 | tf_op jit(solution)/shard_map/ppermute | solution.py:174
  28.0 1.9 %collective-permute-done.10.refs_2_ = bf16[272,128]{1,0:T(8,128)(2,1)S(1)} collective-permute-done((bf16[272,128]{1,0:T(8,128)(2,1)S(1)}, bf16[272,128]{1,0:T(8,128)(2,1)S(1)}, u32[]{:S(2)}, u32[]{:S(2)}) %collective-permute-start.10) | collective-permute-done | bytes 69664 | tf_op jit(solution)/shard_map/ppermute | solution.py:174
  30.0 1.0 %collective-permute-done.9.refs_1_ = bf16[272,128]{1,0:T(8,128)(2,1)S(1)} collective-permute-done((bf16[272,128]{1,0:T(8,128)(2,1)S(1)}, bf16[272,128]{1,0:T(8,128)(2,1)S(1)}, u32[]{:S(2)}, u32[]{:S(2)}) %collective-permute-start.9) | collective-permute-done | bytes 69664 | tf_op jit(solution)/shard_map/ppermute | solution.py:174
  30.9 0.8 %shard_map.55 = (f32[2,128]{1,0:T(2,128)}, bf16[128,256]{1,0:T(8,128)(2,1)}) custom-call(bf16[272,128]{1,0:T(8,128)(2,1)S(1)} %shard_map.54.refs_0_, bf16[272,128]{1,0:T(8,128)(2,1)S(1)} %collective-permute-done.9.refs_1_, bf16[272,128]{1,0:T(8,128)(2,1)S(1)} %collective-permute-done.10.refs_2_, bf16[272,128]{1,0:T(8,128)(2,1)S(1)} %collective-permute-done.11.refs_3_, ...), custom_call_target="tpu_custom_call" | custom-call | flops 557056 | bytes 346112 | tf_op jit(solution)/shard_map/pallas_call | solution.py:135
  (20 shorter events, 0.2 us)
Async XLA Ops:
  0.6 10.0 %copy-start.2 = (bf16[128,256]{1,0:T(8,128)(2,1)S(1)}, bf16[128,256]{1,0:T(8,128)(2,1)}, u32[]{:S(2)}) copy-start(bf16[128,256]{1,0:T(8,128)(2,1)} %param.3) | copy-start | bytes 196612
  0.6 10.9 %collective-permute-start.1 = (bf16[64,1800]{1,0:T(8,128)(2,1)}, bf16[64,1800]{1,0:T(8,128)(2,1)S(1)}, u32[]{:S(2)}, u32[]{:S(2)}) collective-permute-start(bf16[64,1800]{1,0:T(8,128)(2,1)} %bitcast.10), channel_id=1, source_target_pairs={{0,16},{1,17},{2,18},{3,19},{4,20},{5,21},{6,22},{7,23},{8,9},{9,8... | collective-permute-start | bytes 691208 | tf_op jit(solution)/shard_map/ppermute | solution.py:174
  3.6 2.7 %collective-permute-start = (bf16[64,1800]{1,0:T(8,128)(2,1)}, bf16[64,1800]{1,0:T(8,128)(2,1)S(1)}, u32[]{:S(2)}, u32[]{:S(2)}) collective-permute-start(bf16[64,1800]{1,0:T(8,128)(2,1)} %bitcast.11), channel_id=1, source_target_pairs={{0,8},{1,9},{2,10},{3,11},{4,12},{5,13},{6,14},{7,15},{8,0},{9,1},... | collective-permute-start | bytes 691208 | tf_op jit(solution)/shard_map/ppermute | solution.py:174
  3.6 7.0 %collective-permute-start.5 = (bf16[128,256]{1,0:T(8,128)(2,1)}, bf16[128,256]{1,0:T(8,128)(2,1)S(1)}, u32[]{:S(2)}, u32[]{:S(2)}) collective-permute-start(bf16[128,256]{1,0:T(8,128)(2,1)} %param.3), channel_id=1, source_target_pairs={{0,4},{1,5},{2,6},{3,7},{4,0},{5,1},{6,2},{7,3},{8,12},{9,13},{10,... | collective-permute-start | bytes 196616 | tf_op jit(solution)/shard_map/ppermute | solution.py:174
  6.4 6.7 %collective-permute-start.3 = (bf16[64,1800]{1,0:T(8,128)(2,1)S(1)}, bf16[64,1800]{1,0:T(8,128)(2,1)S(1)}, u32[]{:S(2)}, u32[]{:S(2)}) collective-permute-start(bf16[64,1800]{1,0:T(8,128)(2,1)S(1)} %collective-permute-done.refs_1_), channel_id=1, source_target_pairs={{0,16},{1,17},{2,18},{3,19},{4,20},{5,21},{6,22},{7,23},{8,9},{9,8... | collective-permute-start | bytes 691208 | tf_op jit(solution)/shard_map/ppermute | solution.py:174
  10.7 3.2 %copy-start = (bf16[256,256]{1,0:T(8,128)(2,1)S(1)}, bf16[256,256]{1,0:T(8,128)(2,1)}, u32[]{:S(2)}) copy-start(bf16[256,256]{1,0:T(8,128)(2,1)} %refs_7_.1) | copy-start | bytes 393220
  10.7 5.0 %collective-permute-start.6 = (bf16[256,256]{1,0:T(8,128)(2,1)S(1)}, bf16[256,256]{1,0:T(8,128)(2,1)S(1)}, u32[]{:S(2)}, u32[]{:S(2)}) collective-permute-start(bf16[256,256]{1,0:T(8,128)(2,1)S(1)} %pad_maximum_fusion.1), channel_id=1, source_target_pairs={{0,2},{1,3},{2,0},{3,1},{4,6},{5,7},{6,4},{7,5},{8,10},{9,11},{10,... | collective-permute-start | bytes 393224 | tf_op jit(solution)/shard_map/ppermute | solution.py:174
  11.5 6.2 %collective-permute-start.7 = (bf16[64,1800]{1,0:T(8,128)(2,1)S(1)}, bf16[64,1800]{1,0:T(8,128)(2,1)S(1)}, u32[]{:S(2)}, u32[]{:S(2)}) collective-permute-start(bf16[64,1800]{1,0:T(8,128)(2,1)S(1)} %collective-permute-done.1.refs_2_.refs_0_), channel_id=1, source_target_pairs={{0,1},{1,0},{2,3},{3,2},{4,5},{5,4},{6,7},{7,6},{8,24},{9,25},{10,... | collective-permute-start | bytes 691208 | tf_op jit(solution)/shard_map/ppermute | solution.py:174
  13.1 2.7 %collective-permute-start.2 = (bf16[64,1800]{1,0:T(8,128)(2,1)S(1)}, bf16[64,1800]{1,0:T(8,128)(2,1)S(1)}, u32[]{:S(2)}, u32[]{:S(2)}) collective-permute-start(bf16[64,1800]{1,0:T(8,128)(2,1)S(1)} %collective-permute-done.1.refs_2_.refs_0_), channel_id=1, source_target_pairs={{0,8},{1,9},{2,10},{3,11},{4,12},{5,13},{6,14},{7,15},{8,0},{9,1},... | collective-permute-start | bytes 691208 | tf_op jit(solution)/shard_map/ppermute | solution.py:174
  13.1 2.7 %collective-permute-start.4 = (bf16[64,1800]{1,0:T(8,128)(2,1)S(1)}, bf16[64,1800]{1,0:T(8,128)(2,1)S(1)}, u32[]{:S(2)}, u32[]{:S(2)}) collective-permute-start(bf16[64,1800]{1,0:T(8,128)(2,1)S(1)} %collective-permute-done.3.refs_4_.refs_2_), channel_id=1, source_target_pairs={{0,8},{1,9},{2,10},{3,11},{4,12},{5,13},{6,14},{7,15},{8,0},{9,1},... | collective-permute-start | bytes 691208 | tf_op jit(solution)/shard_map/ppermute | solution.py:174
  14.0 1.8 %copy-start.1 = (bf16[1800,64]{0,1:T(8,128)(2,1)S(1)}, bf16[1800,64]{0,1:T(8,128)(2,1)}, u32[]{:S(2)}) copy-start(bf16[1800,64]{0,1:T(8,128)(2,1)} %param.4) | copy-start | bytes 691204
  17.8 1.6 %collective-permute-start.8 = (bf16[64,1800]{1,0:T(8,128)(2,1)S(1)}, bf16[64,1800]{1,0:T(8,128)(2,1)S(1)}, u32[]{:S(2)}, u32[]{:S(2)}) collective-permute-start(bf16[64,1800]{1,0:T(8,128)(2,1)S(1)} %shard_map.51), channel_id=1, source_target_pairs={{0,8},{1,9},{2,10},{3,11},{4,12},{5,13},{6,14},{7,15},{8,0},{9,1},... | collective-permute-start | bytes 691208 | tf_op jit(solution)/shard_map/ppermute | solution.py:174
  21.2 6.9 %collective-permute-start.11 = (bf16[272,128]{1,0:T(8,128)(2,1)S(1)}, bf16[272,128]{1,0:T(8,128)(2,1)S(1)}, u32[]{:S(2)}, u32[]{:S(2)}) collective-permute-start(bf16[272,128]{1,0:T(8,128)(2,1)S(1)} %get-tuple-element.18), channel_id=1, source_target_pairs={{0,6},{1,7},{2,4},{3,5},{4,2},{5,3},{6,0},{7,1},{8,14},{9,15},{10,... | collective-permute-start | bytes 208904 | tf_op jit(solution)/shard_map/ppermute | solution.py:174
  24.9 5.1 %collective-permute-start.10 = (bf16[272,128]{1,0:T(8,128)(2,1)S(1)}, bf16[272,128]{1,0:T(8,128)(2,1)S(1)}, u32[]{:S(2)}, u32[]{:S(2)}) collective-permute-start(bf16[272,128]{1,0:T(8,128)(2,1)S(1)} %get-tuple-element.19), channel_id=1, source_target_pairs={{0,2},{1,3},{2,0},{3,1},{4,6},{5,7},{6,4},{7,5},{8,10},{9,11},{10,... | collective-permute-start | bytes 208904 | tf_op jit(solution)/shard_map/ppermute | solution.py:174
  25.1 5.9 %collective-permute-start.9 = (bf16[272,128]{1,0:T(8,128)(2,1)S(1)}, bf16[272,128]{1,0:T(8,128)(2,1)S(1)}, u32[]{:S(2)}, u32[]{:S(2)}) collective-permute-start(bf16[272,128]{1,0:T(8,128)(2,1)S(1)} %get-tuple-element.20), channel_id=1, source_target_pairs={{0,4},{1,5},{2,6},{3,7},{4,0},{5,1},{6,2},{7,3},{8,12},{9,13},{10,... | collective-permute-start | bytes 208904 | tf_op jit(solution)/shard_map/ppermute | solution.py:174

commit v3 on v2

v3 whole, which is shorter than its diff:
```python
import functools
import math

import jax
import jax.numpy as jnp
from jax import lax
from jax.experimental import pallas as pl
from jax.experimental.pallas import tpu as pltpu
from jax.sharding import PartitionSpec as P

W_GRID = 320
STAT_ROWS = 16
CHUNK = 512
F32, BF16 = jnp.float32, jnp.bfloat16


def grid_coords(pos):
    return (
        (pos % W_GRID).astype(F32) / W_GRID,
        (pos // W_GRID).astype(F32) / W_GRID,
    )


def coord_rows(start, count):
    pos = start + lax.broadcasted_iota(jnp.int32, (STAT_ROWS, count), 1)
    row = lax.broadcasted_iota(jnp.int32, (STAT_ROWS, count), 0)
    gx, gy = pos % W_GRID, pos // W_GRID
    rows = jnp.where(row == 0, 1, 0)
    for index, value in enumerate((gx // 16, gx % 16, gy // 16, gy % 16)):
        rows = jnp.where(row == index + 1, value, rows)
    return rows.astype(BF16)


def split3(value):
    high = value.astype(BF16)
    rest = value - high.astype(F32)
    mid = rest.astype(BF16)
    low = (rest - mid.astype(F32)).astype(BF16)
    return [high.astype(F32), mid.astype(F32), low.astype(F32)]


def as_row(column):
    return jnp.transpose(jnp.broadcast_to(column, (column.shape[0], 128)))[0:1, :]


def either(even, odd):
    return jnp.where(lax.axis_index("src") % 2 == 0, even[...], odd[...])


def project(pieces, projt, rows, strip, kext):
    depth, width = pieces[0].shape[0], projt.shape[0]
    src = lax.axis_index("src")
    for step, piece in enumerate(pieces):
        strip[pl.ds(pl.multiple_of((src ^ step) * depth, depth), depth), :] = piece
    kext[0:width, :] = jnp.dot(projt[...], strip[...], preferred_element_type=F32).astype(BF16)
    kext[width:, :] = rows[...]


def attend(queries, kext, scale):
    tops, totals = [], []
    for first in range(0, queries.shape[0], CHUNK):
        part = queries[first : first + CHUNK]
        raw = jnp.dot(part, kext[0 : part.shape[1], :], preferred_element_type=F32)
        top = jnp.max(raw, axis=1, keepdims=True)
        weights = jnp.exp2((raw - top) * scale).astype(BF16)
        tops.append(as_row(top))
        totals.append(
            lax.dot_general(
                kext[...], weights, (((1,), (1,)), ((), ())), preferred_element_type=F32
            )
        )
    return jnp.concatenate(tops, axis=1), jnp.concatenate(totals, axis=1)


def first_kernel(scale, *refs):
    own, near, one, near_one, two, near_two, projt, proj, rows, *refs = refs
    *sources, top_ref, sums_ref, query_ref, kext, strip = refs
    pieces = [own[...], near[...], either(one, near_two), either(two, near_one)]
    project(pieces, projt, rows, strip, kext)
    source = jnp.concatenate([ref[...] for ref in sources], axis=0)
    queries = jnp.dot(source, proj[...], preferred_element_type=F32).astype(BF16)
    query_ref[...] = queries
    top_ref[...], sums_ref[...] = attend(queries, kext, scale)


def emit(first, state, kext, out_refs, scale):
    lanes = out_refs[0].shape[1]
    span = slice(first * lanes, (first + len(out_refs)) * lanes)
    top_ref, sums_ref, query_ref = state
    queries = query_ref[span, :]
    top1, (top2, sums2) = top_ref[:, span], attend(queries, kext, scale)
    top = jnp.maximum(top1, top2)
    sums = sums_ref[:, span] * jnp.exp2((top1 - top) * scale) + sums2 * jnp.exp2(
        (top2 - top) * scale
    )
    width = queries.shape[1]
    stats = sums[width:]
    coord_x = stats[1:2] * 16.0 + stats[2:3]
    coord_y = stats[3:4] * 16.0 + stats[4:5]
    parts = split3(top) + split3(stats[0:1]) + split3(coord_x) + split3(coord_y)
    parts.append(jnp.zeros((STAT_ROWS - len(parts), top.shape[1]), F32))
    out = jnp.concatenate([sums[0:width], *parts], axis=0).astype(BF16)
    for index, out_ref in enumerate(out_refs):
        out_ref[...] = out[:, index * lanes : (index + 1) * lanes]


def second_kernel(first, scale, *refs):
    one, near_one, two, near_two, cross, near_cross, projt, rows, *refs = refs
    state, (*out_refs, kext, strip) = refs[:3], refs[3:]
    pieces = [either(near_two, one), either(near_one, two), cross[...], near_cross[...]]
    project(pieces, projt, rows, strip, kext)
    emit(first, state, kext, out_refs, scale)


def third_kernel(first, scale, *refs):
    state, kext, out_refs = refs[:3], refs[3], refs[4:]
    emit(first, state, kext, out_refs, scale)


def joined(stats, index):
    rows = stats[3 * index : 3 * index + 3]
    return rows[0:1] + rows[1:2] + rows[2:3]


def merged(scale, parts):
    top = functools.reduce(jnp.maximum, [t for t, _ in parts])
    return top, sum(jnp.exp2((t - top) * scale) * sums for t, sums in parts)


def unpacked(ref):
    width = ref.shape[0] - STAT_ROWS
    stats = ref[width:, :].astype(F32)
    rows = [ref[0:width, :].astype(F32), *(joined(stats, k) for k in (1, 2, 3))]
    return joined(stats, 0), jnp.concatenate([*rows, jnp.zeros((5, ref.shape[1]), F32)], axis=0)


def gather_kernel(scale, *refs):
    *parts, top_ref, sums_ref = refs
    top_ref[...], sums_ref[...] = merged(scale, [unpacked(p) for p in parts])


def merge_kernel(scale, *refs):
    *parts, top_ref, sums_ref, own_ref, flow_ref, matched_ref = refs
    _, sums = merged(scale, [(top_ref[...], sums_ref[...]), *(unpacked(p) for p in parts)])
    width = matched_ref.shape[1]
    total = sums[width : width + 1]
    flow_ref[...] = sums[width + 1 : width + 3] / (total * W_GRID) - own_ref[...]
    matched_ref[...] = jnp.transpose(sums[0:width] / total).astype(matched_ref.dtype)


def call(kernel, outs, scratch, flops, args):
    size = lambda a: math.prod(a.shape) * a.dtype.itemsize
    return pl.pallas_call(
        kernel,
        out_shape=outs,
        scratch_shapes=scratch,
        compiler_params=pltpu.CompilerParams(vmem_limit_bytes=32 * 2**20),
        cost_estimate=pl.CostEstimate(
            flops=flops,
            bytes_accessed=sum(map(size, args)) + sum(map(size, jax.tree.leaves(outs))),
            transcendentals=0,
        ),
    )(*args)


def after(value, *others):
    def kernel(value_ref, *refs):
        refs[-1][...] = value_ref[...]

    return pl.pallas_call(
        kernel,
        out_shape=jax.ShapeDtypeStruct(value.shape, value.dtype),
        compiler_params=pltpu.CompilerParams(vmem_limit_bytes=8 * 2**20),
    )(value, *others)


def per_device(source_feat, target_feat, proj):
    width = proj.shape[1]
    own_rows = source_feat.shape[0]
    count = target_feat.shape[0]
    n_src, n_tgt = lax.axis_size("src"), lax.axis_size("tgt")
    src, tgt = lax.axis_index("src"), lax.axis_index("tgt")
    scale = math.log2(math.e) * width ** (-0.5)
    axes = ("src", "tgt")

    def permute(x, move):
        pairs = []
        for a in range(n_src):
            for b in range(n_tgt):
                s, t = move(a)
                pairs.append((a * n_tgt + b, (a ^ s) * n_tgt + (b ^ t)))
        return lax.ppermute(x, axes, pairs)

    def swap(x, s=0, t=0):
        return permute(x, lambda a: (s, t))

    turn_one = lambda a: (2, 0) if a % 2 == 0 else (0, 1)
    turn_two = lambda a: (0, 1) if a % 2 == 0 else (2, 0)
    own = target_feat.T
    near = swap(own, s=1)
    one = permute(own, turn_one)
    two = permute(near, turn_one)
    cross = permute(one, turn_two)
    near_one, near_two = swap(one, s=1), swap(two, s=1)

    blocks = n_tgt // 2
    half = blocks // 2
    offsets = [0, *range(2 * half, n_tgt - 2, 2), n_tgt - 2, *range(2, 2 * half, 2)]
    late = after(source_feat, near)
    sources = [source_feat]
    sources += [swap(source_feat if t == 2 * half else late, t=t) for t in offsets[1:]]

    projt = proj.T
    rows = [coord_rows((tgt ^ k) * count, count) for k in (0, 1)]
    n_q = blocks * own_rows
    ext = width + STAT_ROWS
    shape = jax.ShapeDtypeStruct
    flops = 2 * count * width * (width + 2 * n_q)
    kext = shape((ext, count), BF16)
    strip = pltpu.VMEM((width, count), BF16)
    message = [shape((ext, own_rows), BF16)] * half
    state = call(
        functools.partial(first_kernel, scale),
        (shape((1, n_q), F32), shape((ext, n_q), F32), shape((n_q, width), BF16)),
        [pltpu.VMEM(kext.shape, BF16), strip],
        flops,
        (own, near, one, near_one, two, near_two, projt, proj, rows[0], *sources),
    )
    near_cross = swap(after(cross, state[0]), s=1)
    *sent, keys = call(
        functools.partial(second_kernel, half, scale),
        (*message, kext),
        [strip],
        flops,
        (one, near_one, two, near_two, cross, near_cross, projt, rows[1], *state),
    )
    kept, *rest = call(
        functools.partial(third_kernel, 0, scale), message, [], flops, (*state, keys)
    )
    sent = [swap(x, t=t) for x, t in zip(sent, offsets[half:])]
    rest = [swap(x, t=t) for x, t in zip(rest, offsets[1:half])]
    top, sums = call(
        functools.partial(gather_kernel, scale),
        (shape((1, own_rows), F32), shape((width + 8, own_rows), F32)),
        [],
        2 * 10**9,
        (kept, *sent),
    )
    own_pos = (src * n_tgt + tgt) * own_rows + jnp.arange(own_rows, dtype=jnp.int32)
    own_coords = jnp.stack(grid_coords(own_pos), axis=0)
    return call(
        functools.partial(merge_kernel, scale),
        (shape((2, own_rows), F32), shape((own_rows, width), BF16)),
        [],
        4 * ext * own_rows * half,
        (*rest, top, sums, own_coords),
    )


def solution(mesh):
    in_specs = (P(("src", "tgt"), None), P("tgt", "src"), P())
    out_specs = (P(None, ("src", "tgt")), P(("src", "tgt"), None))
    return jax.shard_map(
        per_device, mesh=mesh, in_specs=in_specs, out_specs=out_specs, check_vma=False
    )
```

time: 31.9 us -> 30.2 us (0.947)
  waiting for transfers between devices: 10.2 us -> 8.18 us
  starting transfers between devices: 14.1 us -> 15.4 us
  Pallas kernels: 6.04 us -> 5.16 us
    ppermute x12 -> x13, waiting for transfers between devices: 10.2 us -> 8.18 us  [permute(): return lax.ppermute(x, axes, pairs)]
    ppermute x12 -> x13, starting transfers between devices: 14.1 us -> 15.4 us  [permute(): return lax.ppermute(x, axes, pairs)]
    pallas_call x5, Pallas kernels: 6.02 us -> 5.13 us  [call(): pl.pallas_call(kernel, out_shape=outs, scratch_shapes=scratch, compiler_p...]
  transfers between devices with their start and end apart: 12 -> 13, of which waited for: 7 -> 6; matrix products, arithmetic and copies ran while one was open for 2% -> 2% of each run, Pallas kernels for 11% -> 10%
where the time goes in v3:
time: 30.2 us; the launch traced here: 30.1 us
  starting transfers between devices  15.4 us (51%)
  waiting for transfers between devices  8.18 us (27%)
  Pallas kernels  5.16 us (17%)
  between operations  0.82 us (3%)
  other arithmetic  0.42 us (1%)
    ppermute x13, starting transfers between devices, permute(): return lax.ppermute(x, axes, pairs)  15.4 us
    ppermute x13, waiting for transfers between devices, permute(): return lax.ppermute(x, axes, pairs)  8.18 us
    pallas_call x5, Pallas kernels, call(): pl.pallas_call(kernel, out_shape=outs, scratch_shapes=scratch, compiler_p...  5.13 us
  transfers between devices with their start and end apart: 13, of which 6 were waited for; matrix products, arithmetic and copies ran while one was open for 2% of the time, Pallas kernels for 10%

profile of v3, /device:TPU:0, one launch (start us, length us, event | category | flops | bytes accessed | tf_op | source)
XLA Modules:
  0.0 30.1 jit_solution(4388595405477492689)
XLA Ops:
  0.6 3.0 %collective-permute-start.1 = (bf16[64,1800]{1,0:T(8,128)(2,1)}, bf16[64,1800]{1,0:T(8,128)(2,1)S(1)}, u32[]{:S(2)}, u32[]{:S(2)}) collective-permute-start(bf16[64,1800]{1,0:T(8,128)(2,1)} %bitcast.4), channel_id=1, source_target_pairs={{0,16},{1,17},{2,18},{3,19},{4,20},{5,21},{6,22},{7,23},{8,9},{9,8... | collective-permute-start | bytes 691208 | tf_op jit(solution)/shard_map/ppermute | solution.py:192
  3.6 0.0 collective-permute-start
  3.6 2.6 %collective-permute-start.5 = (bf16[128,256]{1,0:T(8,128)(2,1)}, bf16[128,256]{1,0:T(8,128)(2,1)S(1)}, u32[]{:S(2)}, u32[]{:S(2)}) collective-permute-start(bf16[128,256]{1,0:T(8,128)(2,1)} %refs_9_.1), channel_id=1, source_target_pairs={{0,4},{1,5},{2,6},{3,7},{4,0},{5,1},{6,2},{7,3},{8,12},{9,13},{10,... | collective-permute-start | bytes 196616 | tf_op jit(solution)/shard_map/ppermute | solution.py:192
  6.3 0.0 collective-permute-done.refs_0_.refs_1_
  6.4 1.1 %collective-permute-start.3 = (bf16[64,1800]{1,0:T(8,128)(2,1)S(1)}, bf16[64,1800]{1,0:T(8,128)(2,1)S(1)}, u32[]{:S(2)}, u32[]{:S(2)}) collective-permute-start(bf16[64,1800]{1,0:T(8,128)(2,1)S(1)} %collective-permute-done.refs_0_.refs_1_), channel_id=1, source_target_pairs={{0,16},{1,17},{2,18},{3,19},{4,20},{5,21},{6,22},{7,23},{8,9},{9,8... | collective-permute-start | bytes 691208 | tf_op jit(solution)/shard_map/ppermute | solution.py:192
  7.5 0.0 copy-start
  7.6 1.6 %collective-permute-start.7 = (bf16[128,256]{1,0:T(8,128)(2,1)S(1)}, bf16[128,256]{1,0:T(8,128)(2,1)S(1)}, u32[]{:S(2)}, u32[]{:S(2)}) collective-permute-start(bf16[128,256]{1,0:T(8,128)(2,1)S(1)} %shard_map.50), channel_id=1, source_target_pairs={{0,2},{1,3},{2,0},{3,1},{4,6},{5,7},{6,4},{7,5},{8,10},{9,11},{10,... | collective-permute-start | bytes 196616 | tf_op jit(solution)/shard_map/ppermute | solution.py:192
  9.2 1.0 %collective-permute-start.6 = (bf16[128,256]{1,0:T(8,128)(2,1)S(1)}, bf16[128,256]{1,0:T(8,128)(2,1)S(1)}, u32[]{:S(2)}, u32[]{:S(2)}) collective-permute-start(bf16[128,256]{1,0:T(8,128)(2,1)S(1)} %shard_map.50), channel_id=1, source_target_pairs={{0,6},{1,7},{2,4},{3,5},{4,2},{5,3},{6,0},{7,1},{8,14},{9,15},{10,... | collective-permute-start | bytes 196616 | tf_op jit(solution)/shard_map/ppermute | solution.py:192
  10.3 0.0 collective-permute-done.1.refs_2_.refs_0_
  10.3 1.4 %collective-permute-start.8 = (bf16[64,1800]{1,0:T(8,128)(2,1)S(1)}, bf16[64,1800]{1,0:T(8,128)(2,1)S(1)}, u32[]{:S(2)}, u32[]{:S(2)}) collective-permute-start(bf16[64,1800]{1,0:T(8,128)(2,1)S(1)} %collective-permute-done.1.refs_2_.refs_0_), channel_id=1, source_target_pairs={{0,1},{1,0},{2,3},{3,2},{4,5},{5,4},{6,7},{7,6},{8,24},{9,25},{10,... | collective-permute-start | bytes 691208 | tf_op jit(solution)/shard_map/ppermute | solution.py:192
  11.6 0.0 collective-permute-done.5.refs_10_
  11.6 0.0 collective-permute-start.2
  11.6 1.0 %collective-permute-done.3.refs_4_.refs_2_ = bf16[64,1800]{1,0:T(8,128)(2,1)S(1)} collective-permute-done((bf16[64,1800]{1,0:T(8,128)(2,1)S(1)}, bf16[64,1800]{1,0:T(8,128)(2,1)S(1)}, u32[]{:S(2)}, u32[]{:S(2)}) %collective-permute-start.3) | collective-permute-done | bytes 230432 | tf_op jit(solution)/shard_map/ppermute | solution.py:192
  12.6 0.0 collective-permute-start.4
  12.6 0.3 fusion.6
  12.9 0.1 copy.5
  13.0 0.0 collective-permute-done.7.refs_12_
  13.0 2.2 %collective-permute-done.6.refs_11_ = bf16[128,256]{1,0:T(8,128)(2,1)S(1)} collective-permute-done((bf16[128,256]{1,0:T(8,128)(2,1)S(1)}, bf16[128,256]{1,0:T(8,128)(2,1)S(1)}, u32[]{:S(2)}, u32[]{:S(2)}) %collective-permute-start.6) | collective-permute-done | bytes 65568 | tf_op jit(solution)/shard_map/ppermute | solution.py:192
  15.3 0.0 collective-permute-done.2.refs_3_.refs_1_
  15.3 0.0 collective-permute-done.4.refs_5_.refs_3_
  15.3 2.0 %shard_map.51 = (f32[1,512]{1,0:T(1,128)S(1)}, f32[272,512]{1,0:T(8,128)S(1)}, bf16[512,256]{1,0:T(8,128)(2,1)S(1)}) custom-call(bf16[64,1800]{1,0:T(8,128)(2,1)S(1)} %bitcast.6, bf16[64,1800]{1,0:T(8,128)(2,1)S(1)} %collective-permute-done.refs_0_.refs_1_, bf16[64,1800]{1,0:T(8,128)(2,1)S(1)} %collective-permute-done.1.refs_2_.refs_0_, ...), custom_call_target="tpu_custom_call" | custom-call | flops 1179648000 | bytes 2785536 | tf_op jit(solution)/shard_map/pallas_call | solution.py:153
  17.3 0.1 collective-permute-start.9
  17.4 1.5 %collective-permute-done.9.refs_5_ = bf16[64,1800]{1,0:T(8,128)(2,1)S(1)} collective-permute-done((bf16[64,1800]{1,0:T(8,128)(2,1)S(1)}, bf16[64,1800]{1,0:T(8,128)(2,1)S(1)}, u32[]{:S(2)}, u32[]{:S(2)}) %collective-permute-start.9) | collective-permute-done | bytes 230432 | tf_op jit(solution)/shard_map/ppermute | solution.py:192
  18.9 1.4 %shard_map.53 = (bf16[272,128]{1,0:T(8,128)(2,1)S(1)}, bf16[272,128]{1,0:T(8,128)(2,1)S(1)}, bf16[272,1800]{1,0:T(8,128)(2,1)S(1)}) custom-call(bf16[64,1800]{1,0:T(8,128)(2,1)S(1)} %collective-permute-done.1.refs_2_.refs_0_, bf16[64,1800]{1,0:T(8,128)(2,1)S(1)} %collective-permute-done.2.refs_3_.refs_1_, ...), custom_call_target="tpu_custom_call" | custom-call | flops 1179648000 | bytes 3510784 | tf_op jit(solution)/shard_map/pallas_call | solution.py:153
  20.2 2.0 %collective-permute-start.11 = (bf16[272,128]{1,0:T(8,128)(2,1)S(1)}, bf16[272,128]{1,0:T(8,128)(2,1)S(1)}, u32[]{:S(2)}, u32[]{:S(2)}) collective-permute-start(bf16[272,128]{1,0:T(8,128)(2,1)S(1)} %get-tuple-element.18), channel_id=1, source_target_pairs={{0,6},{1,7},{2,4},{3,5},{4,2},{5,3},{6,0},{7,1},{8,14},{9,15},{10,... | collective-permute-start | bytes 208904 | tf_op jit(solution)/shard_map/ppermute | solution.py:192
  22.3 1.0 %shard_map.54 = (bf16[272,128]{1,0:T(8,128)(2,1)S(1)}, bf16[272,128]{1,0:T(8,128)(2,1)S(1)}) custom-call(f32[1,512]{1,0:T(1,128)S(1)} %get-tuple-element.12.refs_0_.refs_8_, f32[272,512]{1,0:T(8,128)S(1)} %get-tuple-element.13.refs_9_.refs_1_, bf16[512,256]{1,0:T(8,128)(2,1)S(1)} %get-tuple-element.14.refs_10_.refs_2_, ...), custom_call_target="tpu_custom_call" | custom-call | flops 1179648000 | bytes 1939712 | tf_op jit(solution)/shard_map/pallas_call | solution.py:153
  23.3 2.5 %collective-permute-start.10 = (bf16[272,128]{1,0:T(8,128)(2,1)S(1)}, bf16[272,128]{1,0:T(8,128)(2,1)S(1)}, u32[]{:S(2)}, u32[]{:S(2)}) collective-permute-start(bf16[272,128]{1,0:T(8,128)(2,1)S(1)} %get-tuple-element.16), channel_id=1, source_target_pairs={{0,4},{1,5},{2,6},{3,7},{4,0},{5,1},{6,2},{7,3},{8,12},{9,13},{10,... | collective-permute-start | bytes 208904 | tf_op jit(solution)/shard_map/ppermute | solution.py:192
  25.7 1.4 %collective-permute-done.11.refs_1_ = bf16[272,128]{1,0:T(8,128)(2,1)S(1)} collective-permute-done((bf16[272,128]{1,0:T(8,128)(2,1)S(1)}, bf16[272,128]{1,0:T(8,128)(2,1)S(1)}, u32[]{:S(2)}, u32[]{:S(2)}) %collective-permute-start.11) | collective-permute-done | bytes 69664 | tf_op jit(solution)/shard_map/ppermute | solution.py:192
  27.1 1.5 %collective-permute-done.12.refs_2_ = bf16[272,128]{1,0:T(8,128)(2,1)S(1)} collective-permute-done((bf16[272,128]{1,0:T(8,128)(2,1)S(1)}, bf16[272,128]{1,0:T(8,128)(2,1)S(1)}, u32[]{:S(2)}, u32[]{:S(2)}) %collective-permute-start.12) | collective-permute-done | bytes 69664 | tf_op jit(solution)/shard_map/ppermute | solution.py:192
  28.6 0.1 shard_map.55
  28.7 0.6 %collective-permute-done.10.refs_0_ = bf16[272,128]{1,0:T(8,128)(2,1)S(1)} collective-permute-done((bf16[272,128]{1,0:T(8,128)(2,1)S(1)}, bf16[272,128]{1,0:T(8,128)(2,1)S(1)}, u32[]{:S(2)}, u32[]{:S(2)}) %collective-permute-start.10) | collective-permute-done | bytes 69664 | tf_op jit(solution)/shard_map/ppermute | solution.py:192
  29.3 0.8 %shard_map.56 = (f32[2,128]{1,0:T(2,128)}, bf16[128,256]{1,0:T(8,128)(2,1)}) custom-call(bf16[272,128]{1,0:T(8,128)(2,1)S(1)} %collective-permute-done.10.refs_0_, f32[1,128]{1,0:T(1,128)S(1)} %get-tuple-element.20.refs_1_, f32[264,128]{1,0:T(8,128)S(1)} %get-tuple-element.21.refs_2_, f32[2,128]{1,0:T(2,128)S(1)} %pad_maximum_fusion.refs_3_), custom_call_target="tpu_custom_call" | custom-call | flops 278528 | bytes 272896 | tf_op jit(solution)/shard_map/pallas_call | solution.py:153
  (20 shorter events, 0.2 us)
Async XLA Ops:
  0.6 6.9 %copy-start.1 = (bf16[128,256]{1,0:T(8,128)(2,1)S(1)}, bf16[128,256]{1,0:T(8,128)(2,1)}, u32[]{:S(2)}) copy-start(bf16[128,256]{1,0:T(8,128)(2,1)} %refs_9_.1) | copy-start | bytes 196612
  0.6 9.6 %collective-permute-start.1 = (bf16[64,1800]{1,0:T(8,128)(2,1)}, bf16[64,1800]{1,0:T(8,128)(2,1)S(1)}, u32[]{:S(2)}, u32[]{:S(2)}) collective-permute-start(bf16[64,1800]{1,0:T(8,128)(2,1)} %bitcast.4), channel_id=1, source_target_pairs={{0,16},{1,17},{2,18},{3,19},{4,20},{5,21},{6,22},{7,23},{8,9},{9,8... | collective-permute-start | bytes 691208 | tf_op jit(solution)/shard_map/ppermute | solution.py:192
  3.6 2.7 %collective-permute-start = (bf16[64,1800]{1,0:T(8,128)(2,1)}, bf16[64,1800]{1,0:T(8,128)(2,1)S(1)}, u32[]{:S(2)}, u32[]{:S(2)}) collective-permute-start(bf16[64,1800]{1,0:T(8,128)(2,1)} %bitcast.5), channel_id=1, source_target_pairs={{0,8},{1,9},{2,10},{3,11},{4,12},{5,13},{6,14},{7,15},{8,0},{9,1},... | collective-permute-start | bytes 691208 | tf_op jit(solution)/shard_map/ppermute | solution.py:192
  3.6 8.0 %collective-permute-start.5 = (bf16[128,256]{1,0:T(8,128)(2,1)}, bf16[128,256]{1,0:T(8,128)(2,1)S(1)}, u32[]{:S(2)}, u32[]{:S(2)}) collective-permute-start(bf16[128,256]{1,0:T(8,128)(2,1)} %refs_9_.1), channel_id=1, source_target_pairs={{0,4},{1,5},{2,6},{3,7},{4,0},{5,1},{6,2},{7,3},{8,12},{9,13},{10,... | collective-permute-start | bytes 196616 | tf_op jit(solution)/shard_map/ppermute | solution.py:192
  6.4 6.3 %collective-permute-start.3 = (bf16[64,1800]{1,0:T(8,128)(2,1)S(1)}, bf16[64,1800]{1,0:T(8,128)(2,1)S(1)}, u32[]{:S(2)}, u32[]{:S(2)}) collective-permute-start(bf16[64,1800]{1,0:T(8,128)(2,1)S(1)} %collective-permute-done.refs_0_.refs_1_), channel_id=1, source_target_pairs={{0,16},{1,17},{2,18},{3,19},{4,20},{5,21},{6,22},{7,23},{8,9},{9,8... | collective-permute-start | bytes 691208 | tf_op jit(solution)/shard_map/ppermute | solution.py:192
  7.5 5.4 %copy-start = (bf16[256,256]{1,0:T(8,128)(2,1)S(1)}, bf16[256,256]{1,0:T(8,128)(2,1)}, u32[]{:S(2)}) copy-start(bf16[256,256]{1,0:T(8,128)(2,1)} %refs_7_.1) | copy-start | bytes 393220
  7.6 5.5 %collective-permute-start.7 = (bf16[128,256]{1,0:T(8,128)(2,1)S(1)}, bf16[128,256]{1,0:T(8,128)(2,1)S(1)}, u32[]{:S(2)}, u32[]{:S(2)}) collective-permute-start(bf16[128,256]{1,0:T(8,128)(2,1)S(1)} %shard_map.50), channel_id=1, source_target_pairs={{0,2},{1,3},{2,0},{3,1},{4,6},{5,7},{6,4},{7,5},{8,10},{9,11},{10,... | collective-permute-start | bytes 196616 | tf_op jit(solution)/shard_map/ppermute | solution.py:192
  9.2 6.1 %collective-permute-start.6 = (bf16[128,256]{1,0:T(8,128)(2,1)S(1)}, bf16[128,256]{1,0:T(8,128)(2,1)S(1)}, u32[]{:S(2)}, u32[]{:S(2)}) collective-permute-start(bf16[128,256]{1,0:T(8,128)(2,1)S(1)} %shard_map.50), channel_id=1, source_target_pairs={{0,6},{1,7},{2,4},{3,5},{4,2},{5,3},{6,0},{7,1},{8,14},{9,15},{10,... | collective-permute-start | bytes 196616 | tf_op jit(solution)/shard_map/ppermute | solution.py:192
  10.3 7.0 %collective-permute-start.8 = (bf16[64,1800]{1,0:T(8,128)(2,1)S(1)}, bf16[64,1800]{1,0:T(8,128)(2,1)S(1)}, u32[]{:S(2)}, u32[]{:S(2)}) collective-permute-start(bf16[64,1800]{1,0:T(8,128)(2,1)S(1)} %collective-permute-done.1.refs_2_.refs_0_), channel_id=1, source_target_pairs={{0,1},{1,0},{2,3},{3,2},{4,5},{5,4},{6,7},{7,6},{8,24},{9,25},{10,... | collective-permute-start | bytes 691208 | tf_op jit(solution)/shard_map/ppermute | solution.py:192
  11.6 3.7 %collective-permute-start.2 = (bf16[64,1800]{1,0:T(8,128)(2,1)S(1)}, bf16[64,1800]{1,0:T(8,128)(2,1)S(1)}, u32[]{:S(2)}, u32[]{:S(2)}) collective-permute-start(bf16[64,1800]{1,0:T(8,128)(2,1)S(1)} %collective-permute-done.1.refs_2_.refs_0_), channel_id=1, source_target_pairs={{0,8},{1,9},{2,10},{3,11},{4,12},{5,13},{6,14},{7,15},{8,0},{9,1},... | collective-permute-start | bytes 691208 | tf_op jit(solution)/shard_map/ppermute | solution.py:192
  12.6 2.7 %collective-permute-start.4 = (bf16[64,1800]{1,0:T(8,128)(2,1)S(1)}, bf16[64,1800]{1,0:T(8,128)(2,1)S(1)}, u32[]{:S(2)}, u32[]{:S(2)}) collective-permute-start(bf16[64,1800]{1,0:T(8,128)(2,1)S(1)} %collective-permute-done.3.refs_4_.refs_2_), channel_id=1, source_target_pairs={{0,8},{1,9},{2,10},{3,11},{4,12},{5,13},{6,14},{7,15},{8,0},{9,1},... | collective-permute-start | bytes 691208 | tf_op jit(solution)/shard_map/ppermute | solution.py:192
  12.6 2.7 %copy-start.2 = (bf16[1800,64]{0,1:T(8,128)(2,1)S(1)}, bf16[1800,64]{0,1:T(8,128)(2,1)}, u32[]{:S(2)}) copy-start(bf16[1800,64]{0,1:T(8,128)(2,1)} %param.4) | copy-start | bytes 691204
  17.3 1.6 %collective-permute-start.9 = (bf16[64,1800]{1,0:T(8,128)(2,1)S(1)}, bf16[64,1800]{1,0:T(8,128)(2,1)S(1)}, u32[]{:S(2)}, u32[]{:S(2)}) collective-permute-start(bf16[64,1800]{1,0:T(8,128)(2,1)S(1)} %shard_map.52), channel_id=1, source_target_pairs={{0,8},{1,9},{2,10},{3,11},{4,12},{5,13},{6,14},{7,15},{8,0},{9,1},... | collective-permute-start | bytes 691208 | tf_op jit(solution)/shard_map/ppermute | solution.py:192
  20.2 6.9 %collective-permute-start.11 = (bf16[272,128]{1,0:T(8,128)(2,1)S(1)}, bf16[272,128]{1,0:T(8,128)(2,1)S(1)}, u32[]{:S(2)}, u32[]{:S(2)}) collective-permute-start(bf16[272,128]{1,0:T(8,128)(2,1)S(1)} %get-tuple-element.18), channel_id=1, source_target_pairs={{0,6},{1,7},{2,4},{3,5},{4,2},{5,3},{6,0},{7,1},{8,14},{9,15},{10,... | collective-permute-start | bytes 208904 | tf_op jit(solution)/shard_map/ppermute | solution.py:192
  22.3 6.3 %collective-permute-start.12 = (bf16[272,128]{1,0:T(8,128)(2,1)S(1)}, bf16[272,128]{1,0:T(8,128)(2,1)S(1)}, u32[]{:S(2)}, u32[]{:S(2)}) collective-permute-start(bf16[272,128]{1,0:T(8,128)(2,1)S(1)} %get-tuple-element.19), channel_id=1, source_target_pairs={{0,2},{1,3},{2,0},{3,1},{4,6},{5,7},{6,4},{7,5},{8,10},{9,11},{10,... | collective-permute-start | bytes 208904 | tf_op jit(solution)/shard_map/ppermute | solution.py:192
  23.3 6.0 %collective-permute-start.10 = (bf16[272,128]{1,0:T(8,128)(2,1)S(1)}, bf16[272,128]{1,0:T(8,128)(2,1)S(1)}, u32[]{:S(2)}, u32[]{:S(2)}) collective-permute-start(bf16[272,128]{1,0:T(8,128)(2,1)S(1)} %get-tuple-element.16), channel_id=1, source_target_pairs={{0,4},{1,5},{2,6},{3,7},{4,0},{5,1},{6,2},{7,3},{8,12},{9,13},{10,... | collective-permute-start | bytes 208904 | tf_op jit(solution)/shard_map/ppermute | solution.py:192

commit v4 on v3

--- a/solution.py
+++ b/solution.py
@@ -72,27 +72,35 @@
     return jnp.concatenate(tops, axis=1), jnp.concatenate(totals, axis=1)
 
 
-def first_kernel(scale, *refs):
-    own, near, one, near_one, two, near_two, projt, proj, rows, *refs = refs
-    *sources, top_ref, sums_ref, query_ref, kext, strip = refs
-    pieces = [own[...], near[...], either(one, near_two), either(two, near_one)]
-    project(pieces, projt, rows, strip, kext)
+def start(sources, proj, kext, state, scale):
+    top_ref, sums_ref, query_ref = state
     source = jnp.concatenate([ref[...] for ref in sources], axis=0)
     queries = jnp.dot(source, proj[...], preferred_element_type=F32).astype(BF16)
     query_ref[...] = queries
     top_ref[...], sums_ref[...] = attend(queries, kext, scale)
 
 
-def emit(first, state, kext, out_refs, scale):
+def first_kernel(early, scale, *refs):
+    own, near, one, near_one, two, near_two, projt, proj, rows, *refs = refs
+    sources, state, (kext, strip) = refs[:early], refs[-5:-2], refs[-2:]
+    pieces = [own[...], near[...], either(one, near_two), either(two, near_one)]
+    project(pieces, projt, rows, strip, kext)
+    start(sources, proj, kext, state, scale)
+
+
+def rest_kernel(scale, *refs):
+    *sources, proj, kext = refs[:-3]
+    start(sources, proj, kext, refs[-3:], scale)
+
+
+def emit(states, kext, out_refs, scale):
     lanes = out_refs[0].shape[1]
-    span = slice(first * lanes, (first + len(out_refs)) * lanes)
-    top_ref, sums_ref, query_ref = state
-    queries = query_ref[span, :]
-    top1, (top2, sums2) = top_ref[:, span], attend(queries, kext, scale)
+    top1 = jnp.concatenate([top[:, first:end] for (top, _, _), first, end in states], axis=1)
+    sums1 = jnp.concatenate([sums[:, first:end] for (_, sums, _), first, end in states], axis=1)
+    queries = jnp.concatenate([q[first:end, :] for (_, _, q), first, end in states], axis=0)
+    top2, sums2 = attend(queries, kext, scale)
     top = jnp.maximum(top1, top2)
-    sums = sums_ref[:, span] * jnp.exp2((top1 - top) * scale) + sums2 * jnp.exp2(
-        (top2 - top) * scale
-    )
+    sums = sums1 * jnp.exp2((top1 - top) * scale) + sums2 * jnp.exp2((top2 - top) * scale)
     width = queries.shape[1]
     stats = sums[width:]
     coord_x = stats[1:2] * 16.0 + stats[2:3]
@@ -104,17 +112,21 @@
         out_ref[...] = out[:, index * lanes : (index + 1) * lanes]
 
 
-def second_kernel(first, scale, *refs):
+def second_kernel(scale, *refs):
     one, near_one, two, near_two, cross, near_cross, projt, rows, *refs = refs
     state, (*out_refs, kext, strip) = refs[:3], refs[3:]
     pieces = [either(near_two, one), either(near_one, two), cross[...], near_cross[...]]
     project(pieces, projt, rows, strip, kext)
-    emit(first, state, kext, out_refs, scale)
-
-
-def third_kernel(first, scale, *refs):
-    state, kext, out_refs = refs[:3], refs[3], refs[4:]
-    emit(first, state, kext, out_refs, scale)
+    n_q = state[2].shape[0]
+    emit([(state, n_q - len(out_refs) * out_refs[0].shape[1], n_q)], kext, out_refs, scale)
+
+
+def third_kernel(scale, *refs):
+    state, others, kext, out_refs = refs[:3], refs[3:6], refs[6], refs[7:]
+    n_q = state[2].shape[0]
+    n_others = len(out_refs) * out_refs[0].shape[1] - n_q
+    states = [(state, 0, n_q)] + ([(others, 0, n_others)] if n_others else [])
+    emit(states, kext, out_refs, scale)
 
 
 def joined(stats, index):
@@ -219,23 +231,31 @@
     kext = shape((ext, count), BF16)
     strip = pltpu.VMEM((width, count), BF16)
     message = [shape((ext, own_rows), BF16)] * half
-    state = call(
-        functools.partial(first_kernel, scale),
-        (shape((1, n_q), F32), shape((ext, n_q), F32), shape((n_q, width), BF16)),
-        [pltpu.VMEM(kext.shape, BF16), strip],
+    state = lambda n_q: (shape((1, n_q), F32), shape((ext, n_q), F32), shape((n_q, width), BF16))
+    *first, first_keys = call(
+        functools.partial(first_kernel, half, scale),
+        (*state(half * own_rows), kext),
+        [strip],
         flops,
         (own, near, one, near_one, two, near_two, projt, proj, rows[0], *sources),
     )
-    near_cross = swap(after(cross, state[0]), s=1)
+    near_cross = swap(after(cross, first[0]), s=1)
+    others = call(
+        functools.partial(rest_kernel, scale),
+        state(n_q - half * own_rows),
+        [],
+        flops,
+        (*sources[half:], proj, first_keys),
+    )
     *sent, keys = call(
-        functools.partial(second_kernel, half, scale),
+        functools.partial(second_kernel, scale),
         (*message, kext),
         [strip],
         flops,
-        (one, near_one, two, near_two, cross, near_cross, projt, rows[1], *state),
+        (one, near_one, two, near_two, cross, near_cross, projt, rows[1], *others),
     )
     kept, *rest = call(
-        functools.partial(third_kernel, 0, scale), message, [], flops, (*state, keys)
+        functools.partial(third_kernel, scale), message, [], flops, (*first, *others, keys)
     )
     sent = [swap(x, t=t) for x, t in zip(sent, offsets[half:])]
     rest = [swap(x, t=t) for x, t in zip(rest, offsets[1:half])]

time: 30.2 us -> 30.2 us (level)
  waiting for transfers between devices: 8.18 us -> 7.41 us
  Pallas kernels: 5.16 us -> 5.86 us
    ppermute x13, waiting for transfers between devices: 8.18 us -> 7.41 us  [permute(): return lax.ppermute(x, axes, pairs)]
    pallas_call x5 -> x6, Pallas kernels: 5.13 us -> 5.83 us  [call(): pl.pallas_call(kernel, out_shape=outs, scratch_shapes=scratch, compiler_p...]
  transfers between devices with their start and end apart: 13 -> 13, of which waited for: 6 -> 6; matrix products, arithmetic and copies ran while one was open for 2% -> 2% of each run, Pallas kernels for 10% -> 12%
where the time goes in v4:
time: 30.2 us; the launch traced here: 30 us
  starting transfers between devices  15.4 us (51%)
  waiting for transfers between devices  7.41 us (25%)
  Pallas kernels  5.86 us (19%)
  between operations  0.83 us (3%)
  other arithmetic  0.42 us (1%)
    ppermute x13, starting transfers between devices, permute(): return lax.ppermute(x, axes, pairs)  15.4 us
    ppermute x13, waiting for transfers between devices, permute(): return lax.ppermute(x, axes, pairs)  7.41 us
    pallas_call x6, Pallas kernels, call(): pl.pallas_call(kernel, out_shape=outs, scratch_shapes=scratch, compiler_p...  5.83 us
  transfers between devices with their start and end apart: 13, of which 6 were waited for; matrix products, arithmetic and copies ran while one was open for 2% of the time, Pallas kernels for 12%

profile of v4, /device:TPU:0, one launch (start us, length us, event | category | flops | bytes accessed | tf_op | source)
XLA Modules:
  0.0 30.0 jit_solution(4303680583766647165)
XLA Ops:
  0.6 3.0 %collective-permute-start.1 = (bf16[64,1800]{1,0:T(8,128)(2,1)}, bf16[64,1800]{1,0:T(8,128)(2,1)S(1)}, u32[]{:S(2)}, u32[]{:S(2)}) collective-permute-start(bf16[64,1800]{1,0:T(8,128)(2,1)} %bitcast.4), channel_id=1, source_target_pairs={{0,16},{1,17},{2,18},{3,19},{4,20},{5,21},{6,22},{7,23},{8,9},{9,8... | collective-permute-start | bytes 691208 | tf_op jit(solution)/shard_map/ppermute | solution.py:204
  3.6 0.0 collective-permute-start
  3.6 2.6 %collective-permute-start.5 = (bf16[128,256]{1,0:T(8,128)(2,1)}, bf16[128,256]{1,0:T(8,128)(2,1)S(1)}, u32[]{:S(2)}, u32[]{:S(2)}) collective-permute-start(bf16[128,256]{1,0:T(8,128)(2,1)} %refs_9_.1), channel_id=1, source_target_pairs={{0,4},{1,5},{2,6},{3,7},{4,0},{5,1},{6,2},{7,3},{8,12},{9,13},{10,... | collective-permute-start | bytes 196616 | tf_op jit(solution)/shard_map/ppermute | solution.py:204
  6.3 0.0 collective-permute-done.refs_0_.refs_1_
  6.4 1.1 %collective-permute-start.3 = (bf16[64,1800]{1,0:T(8,128)(2,1)S(1)}, bf16[64,1800]{1,0:T(8,128)(2,1)S(1)}, u32[]{:S(2)}, u32[]{:S(2)}) collective-permute-start(bf16[64,1800]{1,0:T(8,128)(2,1)S(1)} %collective-permute-done.refs_0_.refs_1_), channel_id=1, source_target_pairs={{0,16},{1,17},{2,18},{3,19},{4,20},{5,21},{6,22},{7,23},{8,9},{9,8... | collective-permute-start | bytes 691208 | tf_op jit(solution)/shard_map/ppermute | solution.py:204
  7.5 0.0 copy-start
  7.6 1.6 %collective-permute-start.7 = (bf16[128,256]{1,0:T(8,128)(2,1)S(1)}, bf16[128,256]{1,0:T(8,128)(2,1)S(1)}, u32[]{:S(2)}, u32[]{:S(2)}) collective-permute-start(bf16[128,256]{1,0:T(8,128)(2,1)S(1)} %shard_map.50), channel_id=1, source_target_pairs={{0,2},{1,3},{2,0},{3,1},{4,6},{5,7},{6,4},{7,5},{8,10},{9,11},{10,... | collective-permute-start | bytes 196616 | tf_op jit(solution)/shard_map/ppermute | solution.py:204
  9.2 1.0 %collective-permute-start.6 = (bf16[128,256]{1,0:T(8,128)(2,1)S(1)}, bf16[128,256]{1,0:T(8,128)(2,1)S(1)}, u32[]{:S(2)}, u32[]{:S(2)}) collective-permute-start(bf16[128,256]{1,0:T(8,128)(2,1)S(1)} %shard_map.50), channel_id=1, source_target_pairs={{0,6},{1,7},{2,4},{3,5},{4,2},{5,3},{6,0},{7,1},{8,14},{9,15},{10,... | collective-permute-start | bytes 196616 | tf_op jit(solution)/shard_map/ppermute | solution.py:204
  10.3 1.4 %collective-permute-start.8 = (bf16[64,1800]{1,0:T(8,128)(2,1)S(1)}, bf16[64,1800]{1,0:T(8,128)(2,1)S(1)}, u32[]{:S(2)}, u32[]{:S(2)}) collective-permute-start(bf16[64,1800]{1,0:T(8,128)(2,1)S(1)} %collective-permute-done.1.refs_2_.refs_0_), channel_id=1, source_target_pairs={{0,1},{1,0},{2,3},{3,2},{4,5},{5,4},{6,7},{7,6},{8,24},{9,25},{10,... | collective-permute-start | bytes 691208 | tf_op jit(solution)/shard_map/ppermute | solution.py:204
  11.6 0.0 collective-permute-done.5.refs_10_
  11.6 0.0 collective-permute-start.2
  11.6 1.0 %collective-permute-done.3.refs_4_.refs_2_ = bf16[64,1800]{1,0:T(8,128)(2,1)S(1)} collective-permute-done((bf16[64,1800]{1,0:T(8,128)(2,1)S(1)}, bf16[64,1800]{1,0:T(8,128)(2,1)S(1)}, u32[]{:S(2)}, u32[]{:S(2)}) %collective-permute-start.3) | collective-permute-done | bytes 230432 | tf_op jit(solution)/shard_map/ppermute | solution.py:204
  12.6 0.0 collective-permute-start.4
  12.6 0.3 fusion.6
  12.9 0.1 copy.5
  13.0 0.0 collective-permute-done.7.refs_12_.refs_1_
  13.1 2.2 %collective-permute-done.6.refs_11_.refs_0_ = bf16[128,256]{1,0:T(8,128)(2,1)S(1)} collective-permute-done((bf16[128,256]{1,0:T(8,128)(2,1)S(1)}, bf16[128,256]{1,0:T(8,128)(2,1)S(1)}, u32[]{:S(2)}, u32[]{:S(2)}) %collective-permute-start.6) | collective-permute-done | bytes 65568 | tf_op jit(solution)/shard_map/ppermute | solution.py:204
  15.3 0.0 collective-permute-done.2.refs_3_.refs_1_
  15.3 0.0 collective-permute-done.4.refs_5_.refs_3_
  15.3 1.6 %shard_map.51 = (f32[1,256]{1,0:T(1,128)S(1)}, f32[272,256]{1,0:T(8,128)S(1)}, bf16[256,256]{1,0:T(8,128)(2,1)S(1)}, bf16[272,1800]{1,0:T(8,128)(2,1)S(1)}) custom-call(bf16[64,1800]{1,0:T(8,128)(2,1)S(1)} %bitcast.6, bf16[64,1800]{1,0:T(8,128)(2,1)S(1)} %collective-permute-done.refs_0_.refs_1_, bf16[64,1800]{1,0:T(8,128)(2,1)S(1)} %collective-permute-done.1.refs_2_.refs_0_, ...), custom_call_target="tpu_custom_call" | custom-call | flops 1179648000 | bytes 3354112 | tf_op jit(solution)/shard_map/pallas_call | solution.py:165
  16.9 0.1 collective-permute-start.9
  17.0 1.1 %shard_map.52 = (f32[1,256]{1,0:T(1,128)S(1)}, f32[272,256]{1,0:T(8,128)S(1)}, bf16[256,256]{1,0:T(8,128)(2,1)S(1)}) custom-call(bf16[128,256]{1,0:T(8,128)(2,1)S(1)} %collective-permute-done.6.refs_11_.refs_0_, bf16[128,256]{1,0:T(8,128)(2,1)S(1)} %collective-permute-done.7.refs_12_.refs_1_, bf16[256,256]{1,0:T(8,128)(2,1)S(1)} %copy-done, ...), custom_call_target="tpu_custom_call" | custom-call | flops 1179648000 | bytes 1651968 | tf_op jit(solution)/shard_map/pallas_call | solution.py:165
  18.2 0.3 %collective-permute-done.9.refs_5_ = bf16[64,1800]{1,0:T(8,128)(2,1)S(1)} collective-permute-done((bf16[64,1800]{1,0:T(8,128)(2,1)S(1)}, bf16[64,1800]{1,0:T(8,128)(2,1)S(1)}, u32[]{:S(2)}, u32[]{:S(2)}) %collective-permute-start.9) | collective-permute-done | bytes 230432 | tf_op jit(solution)/shard_map/ppermute | solution.py:204
  18.5 1.3 %shard_map.54 = (bf16[272,128]{1,0:T(8,128)(2,1)S(1)}, bf16[272,128]{1,0:T(8,128)(2,1)S(1)}, bf16[272,1800]{1,0:T(8,128)(2,1)S(1)}) custom-call(bf16[64,1800]{1,0:T(8,128)(2,1)S(1)} %collective-permute-done.1.refs_2_.refs_0_, bf16[64,1800]{1,0:T(8,128)(2,1)S(1)} %collective-permute-done.2.refs_3_.refs_1_, ...), custom_call_target="tpu_custom_call" | custom-call | flops 1179648000 | bytes 3100160 | tf_op jit(solution)/shard_map/pallas_call | solution.py:165
  19.8 2.4 %collective-permute-start.11 = (bf16[272,128]{1,0:T(8,128)(2,1)S(1)}, bf16[272,128]{1,0:T(8,128)(2,1)S(1)}, u32[]{:S(2)}, u32[]{:S(2)}) collective-permute-start(bf16[272,128]{1,0:T(8,128)(2,1)S(1)} %get-tuple-element.26), channel_id=1, source_target_pairs={{0,6},{1,7},{2,4},{3,5},{4,2},{5,3},{6,0},{7,1},{8,14},{9,15},{10,... | collective-permute-start | bytes 208904 | tf_op jit(solution)/shard_map/ppermute | solution.py:204
  22.2 1.0 %shard_map.55 = (bf16[272,128]{1,0:T(8,128)(2,1)S(1)}, bf16[272,128]{1,0:T(8,128)(2,1)S(1)}) custom-call(f32[1,256]{1,0:T(1,128)S(1)} %get-tuple-element.16.refs_0_, f32[272,256]{1,0:T(8,128)S(1)} %get-tuple-element.17.refs_1_, bf16[256,256]{1,0:T(8,128)(2,1)S(1)} %get-tuple-element.18.refs_2_, f32[1,256]{1,0:T(1,128)S(1)} %get-tuple-element.20.refs_8_.refs_3_, ...), custom_call_target="tpu_custom_call" | custom-call | flops 1179648000 | bytes 1939712 | tf_op jit(solution)/shard_map/pallas_call | solution.py:165
  23.2 2.1 %collective-permute-start.10 = (bf16[272,128]{1,0:T(8,128)(2,1)S(1)}, bf16[272,128]{1,0:T(8,128)(2,1)S(1)}, u32[]{:S(2)}, u32[]{:S(2)}) collective-permute-start(bf16[272,128]{1,0:T(8,128)(2,1)S(1)} %get-tuple-element.24), channel_id=1, source_target_pairs={{0,4},{1,5},{2,6},{3,7},{4,0},{5,1},{6,2},{7,3},{8,12},{9,13},{10,... | collective-permute-start | bytes 208904 | tf_op jit(solution)/shard_map/ppermute | solution.py:204
  25.3 1.4 %collective-permute-done.11.refs_1_ = bf16[272,128]{1,0:T(8,128)(2,1)S(1)} collective-permute-done((bf16[272,128]{1,0:T(8,128)(2,1)S(1)}, bf16[272,128]{1,0:T(8,128)(2,1)S(1)}, u32[]{:S(2)}, u32[]{:S(2)}) %collective-permute-start.11) | collective-permute-done | bytes 69664 | tf_op jit(solution)/shard_map/ppermute | solution.py:204
  26.7 1.7 %collective-permute-done.12.refs_2_ = bf16[272,128]{1,0:T(8,128)(2,1)S(1)} collective-permute-done((bf16[272,128]{1,0:T(8,128)(2,1)S(1)}, bf16[272,128]{1,0:T(8,128)(2,1)S(1)}, u32[]{:S(2)}, u32[]{:S(2)}) %collective-permute-start.12) | collective-permute-done | bytes 69664 | tf_op jit(solution)/shard_map/ppermute | solution.py:204
  28.5 0.1 shard_map.56
  28.5 0.7 %collective-permute-done.10.refs_0_ = bf16[272,128]{1,0:T(8,128)(2,1)S(1)} collective-permute-done((bf16[272,128]{1,0:T(8,128)(2,1)S(1)}, bf16[272,128]{1,0:T(8,128)(2,1)S(1)}, u32[]{:S(2)}, u32[]{:S(2)}) %collective-permute-start.10) | collective-permute-done | bytes 69664 | tf_op jit(solution)/shard_map/ppermute | solution.py:204
  29.2 0.8 %shard_map.57 = (f32[2,128]{1,0:T(2,128)}, bf16[128,256]{1,0:T(8,128)(2,1)}) custom-call(bf16[272,128]{1,0:T(8,128)(2,1)S(1)} %collective-permute-done.10.refs_0_, f32[1,128]{1,0:T(1,128)S(1)} %get-tuple-element.28.refs_1_, f32[264,128]{1,0:T(8,128)S(1)} %get-tuple-element.29.refs_2_, f32[2,128]{1,0:T(2,128)S(1)} %pad_maximum_fusion.refs_3_), custom_call_target="tpu_custom_call" | custom-call | flops 278528 | bytes 272896 | tf_op jit(solution)/shard_map/pallas_call | solution.py:165
  (21 shorter events, 0.2 us)
Async XLA Ops:
  0.6 6.9 %copy-start.1 = (bf16[128,256]{1,0:T(8,128)(2,1)S(1)}, bf16[128,256]{1,0:T(8,128)(2,1)}, u32[]{:S(2)}) copy-start(bf16[128,256]{1,0:T(8,128)(2,1)} %refs_9_.1) | copy-start | bytes 196612
  0.6 9.6 %collective-permute-start.1 = (bf16[64,1800]{1,0:T(8,128)(2,1)}, bf16[64,1800]{1,0:T(8,128)(2,1)S(1)}, u32[]{:S(2)}, u32[]{:S(2)}) collective-permute-start(bf16[64,1800]{1,0:T(8,128)(2,1)} %bitcast.4), channel_id=1, source_target_pairs={{0,16},{1,17},{2,18},{3,19},{4,20},{5,21},{6,22},{7,23},{8,9},{9,8... | collective-permute-start | bytes 691208 | tf_op jit(solution)/shard_map/ppermute | solution.py:204
  3.6 2.7 %collective-permute-start = (bf16[64,1800]{1,0:T(8,128)(2,1)}, bf16[64,1800]{1,0:T(8,128)(2,1)S(1)}, u32[]{:S(2)}, u32[]{:S(2)}) collective-permute-start(bf16[64,1800]{1,0:T(8,128)(2,1)} %bitcast.5), channel_id=1, source_target_pairs={{0,8},{1,9},{2,10},{3,11},{4,12},{5,13},{6,14},{7,15},{8,0},{9,1},... | collective-permute-start | bytes 691208 | tf_op jit(solution)/shard_map/ppermute | solution.py:204
  3.6 8.0 %collective-permute-start.5 = (bf16[128,256]{1,0:T(8,128)(2,1)}, bf16[128,256]{1,0:T(8,128)(2,1)S(1)}, u32[]{:S(2)}, u32[]{:S(2)}) collective-permute-start(bf16[128,256]{1,0:T(8,128)(2,1)} %refs_9_.1), channel_id=1, source_target_pairs={{0,4},{1,5},{2,6},{3,7},{4,0},{5,1},{6,2},{7,3},{8,12},{9,13},{10,... | collective-permute-start | bytes 196616 | tf_op jit(solution)/shard_map/ppermute | solution.py:204
  6.4 6.3 %collective-permute-start.3 = (bf16[64,1800]{1,0:T(8,128)(2,1)S(1)}, bf16[64,1800]{1,0:T(8,128)(2,1)S(1)}, u32[]{:S(2)}, u32[]{:S(2)}) collective-permute-start(bf16[64,1800]{1,0:T(8,128)(2,1)S(1)} %collective-permute-done.refs_0_.refs_1_), channel_id=1, source_target_pairs={{0,16},{1,17},{2,18},{3,19},{4,20},{5,21},{6,22},{7,23},{8,9},{9,8... | collective-permute-start | bytes 691208 | tf_op jit(solution)/shard_map/ppermute | solution.py:204
  7.5 5.4 %copy-start = (bf16[256,256]{1,0:T(8,128)(2,1)S(1)}, bf16[256,256]{1,0:T(8,128)(2,1)}, u32[]{:S(2)}) copy-start(bf16[256,256]{1,0:T(8,128)(2,1)} %refs_2_.1) | copy-start | bytes 393220
  7.6 5.5 %collective-permute-start.7 = (bf16[128,256]{1,0:T(8,128)(2,1)S(1)}, bf16[128,256]{1,0:T(8,128)(2,1)S(1)}, u32[]{:S(2)}, u32[]{:S(2)}) collective-permute-start(bf16[128,256]{1,0:T(8,128)(2,1)S(1)} %shard_map.50), channel_id=1, source_target_pairs={{0,2},{1,3},{2,0},{3,1},{4,6},{5,7},{6,4},{7,5},{8,10},{9,11},{10,... | collective-permute-start | bytes 196616 | tf_op jit(solution)/shard_map/ppermute | solution.py:204
  9.2 6.1 %collective-permute-start.6 = (bf16[128,256]{1,0:T(8,128)(2,1)S(1)}, bf16[128,256]{1,0:T(8,128)(2,1)S(1)}, u32[]{:S(2)}, u32[]{:S(2)}) collective-permute-start(bf16[128,256]{1,0:T(8,128)(2,1)S(1)} %shard_map.50), channel_id=1, source_target_pairs={{0,6},{1,7},{2,4},{3,5},{4,2},{5,3},{6,0},{7,1},{8,14},{9,15},{10,... | collective-permute-start | bytes 196616 | tf_op jit(solution)/shard_map/ppermute | solution.py:204
  10.3 6.6 %collective-permute-start.8 = (bf16[64,1800]{1,0:T(8,128)(2,1)S(1)}, bf16[64,1800]{1,0:T(8,128)(2,1)S(1)}, u32[]{:S(2)}, u32[]{:S(2)}) collective-permute-start(bf16[64,1800]{1,0:T(8,128)(2,1)S(1)} %collective-permute-done.1.refs_2_.refs_0_), channel_id=1, source_target_pairs={{0,1},{1,0},{2,3},{3,2},{4,5},{5,4},{6,7},{7,6},{8,24},{9,25},{10,... | collective-permute-start | bytes 691208 | tf_op jit(solution)/shard_map/ppermute | solution.py:204
  11.6 3.7 %collective-permute-start.2 = (bf16[64,1800]{1,0:T(8,128)(2,1)S(1)}, bf16[64,1800]{1,0:T(8,128)(2,1)S(1)}, u32[]{:S(2)}, u32[]{:S(2)}) collective-permute-start(bf16[64,1800]{1,0:T(8,128)(2,1)S(1)} %collective-permute-done.1.refs_2_.refs_0_), channel_id=1, source_target_pairs={{0,8},{1,9},{2,10},{3,11},{4,12},{5,13},{6,14},{7,15},{8,0},{9,1},... | collective-permute-start | bytes 691208 | tf_op jit(solution)/shard_map/ppermute | solution.py:204
  12.6 2.7 %collective-permute-start.4 = (bf16[64,1800]{1,0:T(8,128)(2,1)S(1)}, bf16[64,1800]{1,0:T(8,128)(2,1)S(1)}, u32[]{:S(2)}, u32[]{:S(2)}) collective-permute-start(bf16[64,1800]{1,0:T(8,128)(2,1)S(1)} %collective-permute-done.3.refs_4_.refs_2_), channel_id=1, source_target_pairs={{0,8},{1,9},{2,10},{3,11},{4,12},{5,13},{6,14},{7,15},{8,0},{9,1},... | collective-permute-start | bytes 691208 | tf_op jit(solution)/shard_map/ppermute | solution.py:204
  12.6 2.7 %copy-start.2 = (bf16[1800,64]{0,1:T(8,128)(2,1)S(1)}, bf16[1800,64]{0,1:T(8,128)(2,1)}, u32[]{:S(2)}) copy-start(bf16[1800,64]{0,1:T(8,128)(2,1)} %param.4) | copy-start | bytes 691204
  16.9 1.6 %collective-permute-start.9 = (bf16[64,1800]{1,0:T(8,128)(2,1)S(1)}, bf16[64,1800]{1,0:T(8,128)(2,1)S(1)}, u32[]{:S(2)}, u32[]{:S(2)}) collective-permute-start(bf16[64,1800]{1,0:T(8,128)(2,1)S(1)} %shard_map.53), channel_id=1, source_target_pairs={{0,8},{1,9},{2,10},{3,11},{4,12},{5,13},{6,14},{7,15},{8,0},{9,1},... | collective-permute-start | bytes 691208 | tf_op jit(solution)/shard_map/ppermute | solution.py:204
  19.8 6.9 %collective-permute-start.11 = (bf16[272,128]{1,0:T(8,128)(2,1)S(1)}, bf16[272,128]{1,0:T(8,128)(2,1)S(1)}, u32[]{:S(2)}, u32[]{:S(2)}) collective-permute-start(bf16[272,128]{1,0:T(8,128)(2,1)S(1)} %get-tuple-element.26), channel_id=1, source_target_pairs={{0,6},{1,7},{2,4},{3,5},{4,2},{5,3},{6,0},{7,1},{8,14},{9,15},{10,... | collective-permute-start | bytes 208904 | tf_op jit(solution)/shard_map/ppermute | solution.py:204
  22.2 6.2 %collective-permute-start.12 = (bf16[272,128]{1,0:T(8,128)(2,1)S(1)}, bf16[272,128]{1,0:T(8,128)(2,1)S(1)}, u32[]{:S(2)}, u32[]{:S(2)}) collective-permute-start(bf16[272,128]{1,0:T(8,128)(2,1)S(1)} %get-tuple-element.27), channel_id=1, source_target_pairs={{0,2},{1,3},{2,0},{3,1},{4,6},{5,7},{6,4},{7,5},{8,10},{9,11},{10,... | collective-permute-start | bytes 208904 | tf_op jit(solution)/shard_map/ppermute | solution.py:204
  23.2 6.0 %collective-permute-start.10 = (bf16[272,128]{1,0:T(8,128)(2,1)S(1)}, bf16[272,128]{1,0:T(8,128)(2,1)S(1)}, u32[]{:S(2)}, u32[]{:S(2)}) collective-permute-start(bf16[272,128]{1,0:T(8,128)(2,1)S(1)} %get-tuple-element.24), channel_id=1, source_target_pairs={{0,4},{1,5},{2,6},{3,7},{4,0},{5,1},{6,2},{7,3},{8,12},{9,13},{10,... | collective-permute-start | bytes 208904 | tf_op jit(solution)/shard_map/ppermute | solution.py:204

commit v5 on v4

--- a/solution.py
+++ b/solution.py
@@ -157,7 +157,7 @@
     width = matched_ref.shape[1]
     total = sums[width : width + 1]
     flow_ref[...] = sums[width + 1 : width + 3] / (total * W_GRID) - own_ref[...]
-    matched_ref[...] = jnp.transpose(sums[0:width] / total).astype(matched_ref.dtype)
+    matched_ref[...] = jnp.transpose((sums[0:width] * (1.0 / total)).astype(matched_ref.dtype))
 
 
 def call(kernel, outs, scratch, flops, args):

time: 30.2 us -> 30.1 us (level)
  no operation moved by 1% of the time
where the time goes in v5:
time: 30.1 us; the launch traced here: 30 us
  starting transfers between devices  15.4 us (51%)
  waiting for transfers between devices  7.41 us (25%)
  Pallas kernels  5.83 us (19%)
  between operations  0.83 us (3%)
  other arithmetic  0.42 us (1%)
    ppermute x13, starting transfers between devices, permute(): return lax.ppermute(x, axes, pairs)  15.4 us
    ppermute x13, waiting for transfers between devices, permute(): return lax.ppermute(x, axes, pairs)  7.41 us
    pallas_call x6, Pallas kernels, call(): pl.pallas_call(kernel, out_shape=outs, scratch_shapes=scratch, compiler_p...  5.8 us
  transfers between devices with their start and end apart: 13, of which 6 were waited for; matrix products, arithmetic and copies ran while one was open for 2% of the time, Pallas kernels for 12%

profile of v5, /device:TPU:0, one launch (start us, length us, event | category | flops | bytes accessed | tf_op | source)
XLA Modules:
  0.0 30.0 jit_solution(10987772123486926681)
XLA Ops:
  0.6 3.0 %collective-permute-start.1 = (bf16[64,1800]{1,0:T(8,128)(2,1)}, bf16[64,1800]{1,0:T(8,128)(2,1)S(1)}, u32[]{:S(2)}, u32[]{:S(2)}) collective-permute-start(bf16[64,1800]{1,0:T(8,128)(2,1)} %bitcast.4), channel_id=1, source_target_pairs={{0,16},{1,17},{2,18},{3,19},{4,20},{5,21},{6,22},{7,23},{8,9},{9,8... | collective-permute-start | bytes 691208 | tf_op jit(solution)/shard_map/ppermute | solution.py:204
  3.6 0.0 collective-permute-start
  3.6 2.6 %collective-permute-start.5 = (bf16[128,256]{1,0:T(8,128)(2,1)}, bf16[128,256]{1,0:T(8,128)(2,1)S(1)}, u32[]{:S(2)}, u32[]{:S(2)}) collective-permute-start(bf16[128,256]{1,0:T(8,128)(2,1)} %refs_9_.1), channel_id=1, source_target_pairs={{0,4},{1,5},{2,6},{3,7},{4,0},{5,1},{6,2},{7,3},{8,12},{9,13},{10,... | collective-permute-start | bytes 196616 | tf_op jit(solution)/shard_map/ppermute | solution.py:204
  6.3 0.0 collective-permute-done.refs_0_.refs_1_
  6.4 1.1 %collective-permute-start.3 = (bf16[64,1800]{1,0:T(8,128)(2,1)S(1)}, bf16[64,1800]{1,0:T(8,128)(2,1)S(1)}, u32[]{:S(2)}, u32[]{:S(2)}) collective-permute-start(bf16[64,1800]{1,0:T(8,128)(2,1)S(1)} %collective-permute-done.refs_0_.refs_1_), channel_id=1, source_target_pairs={{0,16},{1,17},{2,18},{3,19},{4,20},{5,21},{6,22},{7,23},{8,9},{9,8... | collective-permute-start | bytes 691208 | tf_op jit(solution)/shard_map/ppermute | solution.py:204
  7.5 0.0 copy-start
  7.6 1.6 %collective-permute-start.7 = (bf16[128,256]{1,0:T(8,128)(2,1)S(1)}, bf16[128,256]{1,0:T(8,128)(2,1)S(1)}, u32[]{:S(2)}, u32[]{:S(2)}) collective-permute-start(bf16[128,256]{1,0:T(8,128)(2,1)S(1)} %shard_map.50), channel_id=1, source_target_pairs={{0,2},{1,3},{2,0},{3,1},{4,6},{5,7},{6,4},{7,5},{8,10},{9,11},{10,... | collective-permute-start | bytes 196616 | tf_op jit(solution)/shard_map/ppermute | solution.py:204
  9.2 1.0 %collective-permute-start.6 = (bf16[128,256]{1,0:T(8,128)(2,1)S(1)}, bf16[128,256]{1,0:T(8,128)(2,1)S(1)}, u32[]{:S(2)}, u32[]{:S(2)}) collective-permute-start(bf16[128,256]{1,0:T(8,128)(2,1)S(1)} %shard_map.50), channel_id=1, source_target_pairs={{0,6},{1,7},{2,4},{3,5},{4,2},{5,3},{6,0},{7,1},{8,14},{9,15},{10,... | collective-permute-start | bytes 196616 | tf_op jit(solution)/shard_map/ppermute | solution.py:204
  10.3 1.4 %collective-permute-start.8 = (bf16[64,1800]{1,0:T(8,128)(2,1)S(1)}, bf16[64,1800]{1,0:T(8,128)(2,1)S(1)}, u32[]{:S(2)}, u32[]{:S(2)}) collective-permute-start(bf16[64,1800]{1,0:T(8,128)(2,1)S(1)} %collective-permute-done.1.refs_2_.refs_0_), channel_id=1, source_target_pairs={{0,1},{1,0},{2,3},{3,2},{4,5},{5,4},{6,7},{7,6},{8,24},{9,25},{10,... | collective-permute-start | bytes 691208 | tf_op jit(solution)/shard_map/ppermute | solution.py:204
  11.6 0.0 collective-permute-done.5.refs_10_
  11.6 0.0 collective-permute-start.2
  11.6 1.0 %collective-permute-done.3.refs_4_.refs_2_ = bf16[64,1800]{1,0:T(8,128)(2,1)S(1)} collective-permute-done((bf16[64,1800]{1,0:T(8,128)(2,1)S(1)}, bf16[64,1800]{1,0:T(8,128)(2,1)S(1)}, u32[]{:S(2)}, u32[]{:S(2)}) %collective-permute-start.3) | collective-permute-done | bytes 230432 | tf_op jit(solution)/shard_map/ppermute | solution.py:204
  12.6 0.0 collective-permute-start.4
  12.6 0.3 fusion.6
  12.9 0.1 copy.5
  13.0 0.0 collective-permute-done.7.refs_12_.refs_1_
  13.1 2.2 %collective-permute-done.6.refs_11_.refs_0_ = bf16[128,256]{1,0:T(8,128)(2,1)S(1)} collective-permute-done((bf16[128,256]{1,0:T(8,128)(2,1)S(1)}, bf16[128,256]{1,0:T(8,128)(2,1)S(1)}, u32[]{:S(2)}, u32[]{:S(2)}) %collective-permute-start.6) | collective-permute-done | bytes 65568 | tf_op jit(solution)/shard_map/ppermute | solution.py:204
  15.3 0.0 collective-permute-done.2.refs_3_.refs_1_
  15.3 0.0 collective-permute-done.4.refs_5_.refs_3_
  15.3 1.6 %shard_map.51 = (f32[1,256]{1,0:T(1,128)S(1)}, f32[272,256]{1,0:T(8,128)S(1)}, bf16[256,256]{1,0:T(8,128)(2,1)S(1)}, bf16[272,1800]{1,0:T(8,128)(2,1)S(1)}) custom-call(bf16[64,1800]{1,0:T(8,128)(2,1)S(1)} %bitcast.6, bf16[64,1800]{1,0:T(8,128)(2,1)S(1)} %collective-permute-done.refs_0_.refs_1_, bf16[64,1800]{1,0:T(8,128)(2,1)S(1)} %collective-permute-done.1.refs_2_.refs_0_, ...), custom_call_target="tpu_custom_call" | custom-call | flops 1179648000 | bytes 3354112 | tf_op jit(solution)/shard_map/pallas_call | solution.py:165
  16.9 0.1 collective-permute-start.9
  17.0 1.1 %shard_map.52 = (f32[1,256]{1,0:T(1,128)S(1)}, f32[272,256]{1,0:T(8,128)S(1)}, bf16[256,256]{1,0:T(8,128)(2,1)S(1)}) custom-call(bf16[128,256]{1,0:T(8,128)(2,1)S(1)} %collective-permute-done.6.refs_11_.refs_0_, bf16[128,256]{1,0:T(8,128)(2,1)S(1)} %collective-permute-done.7.refs_12_.refs_1_, bf16[256,256]{1,0:T(8,128)(2,1)S(1)} %copy-done, ...), custom_call_target="tpu_custom_call" | custom-call | flops 1179648000 | bytes 1651968 | tf_op jit(solution)/shard_map/pallas_call | solution.py:165
  18.2 0.3 %collective-permute-done.9.refs_5_ = bf16[64,1800]{1,0:T(8,128)(2,1)S(1)} collective-permute-done((bf16[64,1800]{1,0:T(8,128)(2,1)S(1)}, bf16[64,1800]{1,0:T(8,128)(2,1)S(1)}, u32[]{:S(2)}, u32[]{:S(2)}) %collective-permute-start.9) | collective-permute-done | bytes 230432 | tf_op jit(solution)/shard_map/ppermute | solution.py:204
  18.5 1.3 %shard_map.54 = (bf16[272,128]{1,0:T(8,128)(2,1)S(1)}, bf16[272,128]{1,0:T(8,128)(2,1)S(1)}, bf16[272,1800]{1,0:T(8,128)(2,1)S(1)}) custom-call(bf16[64,1800]{1,0:T(8,128)(2,1)S(1)} %collective-permute-done.1.refs_2_.refs_0_, bf16[64,1800]{1,0:T(8,128)(2,1)S(1)} %collective-permute-done.2.refs_3_.refs_1_, ...), custom_call_target="tpu_custom_call" | custom-call | flops 1179648000 | bytes 3100160 | tf_op jit(solution)/shard_map/pallas_call | solution.py:165
  19.8 2.4 %collective-permute-start.11 = (bf16[272,128]{1,0:T(8,128)(2,1)S(1)}, bf16[272,128]{1,0:T(8,128)(2,1)S(1)}, u32[]{:S(2)}, u32[]{:S(2)}) collective-permute-start(bf16[272,128]{1,0:T(8,128)(2,1)S(1)} %get-tuple-element.26), channel_id=1, source_target_pairs={{0,6},{1,7},{2,4},{3,5},{4,2},{5,3},{6,0},{7,1},{8,14},{9,15},{10,... | collective-permute-start | bytes 208904 | tf_op jit(solution)/shard_map/ppermute | solution.py:204
  22.2 1.0 %shard_map.55 = (bf16[272,128]{1,0:T(8,128)(2,1)S(1)}, bf16[272,128]{1,0:T(8,128)(2,1)S(1)}) custom-call(f32[1,256]{1,0:T(1,128)S(1)} %get-tuple-element.16.refs_0_, f32[272,256]{1,0:T(8,128)S(1)} %get-tuple-element.17.refs_1_, bf16[256,256]{1,0:T(8,128)(2,1)S(1)} %get-tuple-element.18.refs_2_, f32[1,256]{1,0:T(1,128)S(1)} %get-tuple-element.20.refs_8_.refs_3_, ...), custom_call_target="tpu_custom_call" | custom-call | flops 1179648000 | bytes 1939712 | tf_op jit(solution)/shard_map/pallas_call | solution.py:165
  23.2 2.1 %collective-permute-start.10 = (bf16[272,128]{1,0:T(8,128)(2,1)S(1)}, bf16[272,128]{1,0:T(8,128)(2,1)S(1)}, u32[]{:S(2)}, u32[]{:S(2)}) collective-permute-start(bf16[272,128]{1,0:T(8,128)(2,1)S(1)} %get-tuple-element.24), channel_id=1, source_target_pairs={{0,4},{1,5},{2,6},{3,7},{4,0},{5,1},{6,2},{7,3},{8,12},{9,13},{10,... | collective-permute-start | bytes 208904 | tf_op jit(solution)/shard_map/ppermute | solution.py:204
  25.3 1.4 %collective-permute-done.11.refs_1_ = bf16[272,128]{1,0:T(8,128)(2,1)S(1)} collective-permute-done((bf16[272,128]{1,0:T(8,128)(2,1)S(1)}, bf16[272,128]{1,0:T(8,128)(2,1)S(1)}, u32[]{:S(2)}, u32[]{:S(2)}) %collective-permute-start.11) | collective-permute-done | bytes 69664 | tf_op jit(solution)/shard_map/ppermute | solution.py:204
  26.7 1.7 %collective-permute-done.12.refs_2_ = bf16[272,128]{1,0:T(8,128)(2,1)S(1)} collective-permute-done((bf16[272,128]{1,0:T(8,128)(2,1)S(1)}, bf16[272,128]{1,0:T(8,128)(2,1)S(1)}, u32[]{:S(2)}, u32[]{:S(2)}) %collective-permute-start.12) | collective-permute-done | bytes 69664 | tf_op jit(solution)/shard_map/ppermute | solution.py:204
  28.5 0.1 shard_map.56
  28.5 0.7 %collective-permute-done.10.refs_0_ = bf16[272,128]{1,0:T(8,128)(2,1)S(1)} collective-permute-done((bf16[272,128]{1,0:T(8,128)(2,1)S(1)}, bf16[272,128]{1,0:T(8,128)(2,1)S(1)}, u32[]{:S(2)}, u32[]{:S(2)}) %collective-permute-start.10) | collective-permute-done | bytes 69664 | tf_op jit(solution)/shard_map/ppermute | solution.py:204
  29.2 0.7 %shard_map.57 = (f32[2,128]{1,0:T(2,128)}, bf16[128,256]{1,0:T(8,128)(2,1)}) custom-call(bf16[272,128]{1,0:T(8,128)(2,1)S(1)} %collective-permute-done.10.refs_0_, f32[1,128]{1,0:T(1,128)S(1)} %get-tuple-element.28.refs_1_, f32[264,128]{1,0:T(8,128)S(1)} %get-tuple-element.29.refs_2_, f32[2,128]{1,0:T(2,128)S(1)} %pad_maximum_fusion.refs_3_), custom_call_target="tpu_custom_call" | custom-call | flops 278528 | bytes 272896 | tf_op jit(solution)/shard_map/pallas_call | solution.py:165
  (21 shorter events, 0.2 us)
Async XLA Ops:
  0.6 6.9 %copy-start.1 = (bf16[128,256]{1,0:T(8,128)(2,1)S(1)}, bf16[128,256]{1,0:T(8,128)(2,1)}, u32[]{:S(2)}) copy-start(bf16[128,256]{1,0:T(8,128)(2,1)} %refs_9_.1) | copy-start | bytes 196612
  0.6 9.6 %collective-permute-start.1 = (bf16[64,1800]{1,0:T(8,128)(2,1)}, bf16[64,1800]{1,0:T(8,128)(2,1)S(1)}, u32[]{:S(2)}, u32[]{:S(2)}) collective-permute-start(bf16[64,1800]{1,0:T(8,128)(2,1)} %bitcast.4), channel_id=1, source_target_pairs={{0,16},{1,17},{2,18},{3,19},{4,20},{5,21},{6,22},{7,23},{8,9},{9,8... | collective-permute-start | bytes 691208 | tf_op jit(solution)/shard_map/ppermute | solution.py:204
  3.6 2.7 %collective-permute-start = (bf16[64,1800]{1,0:T(8,128)(2,1)}, bf16[64,1800]{1,0:T(8,128)(2,1)S(1)}, u32[]{:S(2)}, u32[]{:S(2)}) collective-permute-start(bf16[64,1800]{1,0:T(8,128)(2,1)} %bitcast.5), channel_id=1, source_target_pairs={{0,8},{1,9},{2,10},{3,11},{4,12},{5,13},{6,14},{7,15},{8,0},{9,1},... | collective-permute-start | bytes 691208 | tf_op jit(solution)/shard_map/ppermute | solution.py:204
  3.6 8.0 %collective-permute-start.5 = (bf16[128,256]{1,0:T(8,128)(2,1)}, bf16[128,256]{1,0:T(8,128)(2,1)S(1)}, u32[]{:S(2)}, u32[]{:S(2)}) collective-permute-start(bf16[128,256]{1,0:T(8,128)(2,1)} %refs_9_.1), channel_id=1, source_target_pairs={{0,4},{1,5},{2,6},{3,7},{4,0},{5,1},{6,2},{7,3},{8,12},{9,13},{10,... | collective-permute-start | bytes 196616 | tf_op jit(solution)/shard_map/ppermute | solution.py:204
  6.4 6.3 %collective-permute-start.3 = (bf16[64,1800]{1,0:T(8,128)(2,1)S(1)}, bf16[64,1800]{1,0:T(8,128)(2,1)S(1)}, u32[]{:S(2)}, u32[]{:S(2)}) collective-permute-start(bf16[64,1800]{1,0:T(8,128)(2,1)S(1)} %collective-permute-done.refs_0_.refs_1_), channel_id=1, source_target_pairs={{0,16},{1,17},{2,18},{3,19},{4,20},{5,21},{6,22},{7,23},{8,9},{9,8... | collective-permute-start | bytes 691208 | tf_op jit(solution)/shard_map/ppermute | solution.py:204
  7.5 5.4 %copy-start = (bf16[256,256]{1,0:T(8,128)(2,1)S(1)}, bf16[256,256]{1,0:T(8,128)(2,1)}, u32[]{:S(2)}) copy-start(bf16[256,256]{1,0:T(8,128)(2,1)} %refs_2_.1) | copy-start | bytes 393220
  7.6 5.5 %collective-permute-start.7 = (bf16[128,256]{1,0:T(8,128)(2,1)S(1)}, bf16[128,256]{1,0:T(8,128)(2,1)S(1)}, u32[]{:S(2)}, u32[]{:S(2)}) collective-permute-start(bf16[128,256]{1,0:T(8,128)(2,1)S(1)} %shard_map.50), channel_id=1, source_target_pairs={{0,2},{1,3},{2,0},{3,1},{4,6},{5,7},{6,4},{7,5},{8,10},{9,11},{10,... | collective-permute-start | bytes 196616 | tf_op jit(solution)/shard_map/ppermute | solution.py:204
  9.2 6.1 %collective-permute-start.6 = (bf16[128,256]{1,0:T(8,128)(2,1)S(1)}, bf16[128,256]{1,0:T(8,128)(2,1)S(1)}, u32[]{:S(2)}, u32[]{:S(2)}) collective-permute-start(bf16[128,256]{1,0:T(8,128)(2,1)S(1)} %shard_map.50), channel_id=1, source_target_pairs={{0,6},{1,7},{2,4},{3,5},{4,2},{5,3},{6,0},{7,1},{8,14},{9,15},{10,... | collective-permute-start | bytes 196616 | tf_op jit(solution)/shard_map/ppermute | solution.py:204
  10.3 6.6 %collective-permute-start.8 = (bf16[64,1800]{1,0:T(8,128)(2,1)S(1)}, bf16[64,1800]{1,0:T(8,128)(2,1)S(1)}, u32[]{:S(2)}, u32[]{:S(2)}) collective-permute-start(bf16[64,1800]{1,0:T(8,128)(2,1)S(1)} %collective-permute-done.1.refs_2_.refs_0_), channel_id=1, source_target_pairs={{0,1},{1,0},{2,3},{3,2},{4,5},{5,4},{6,7},{7,6},{8,24},{9,25},{10,... | collective-permute-start | bytes 691208 | tf_op jit(solution)/shard_map/ppermute | solution.py:204
  11.6 3.7 %collective-permute-start.2 = (bf16[64,1800]{1,0:T(8,128)(2,1)S(1)}, bf16[64,1800]{1,0:T(8,128)(2,1)S(1)}, u32[]{:S(2)}, u32[]{:S(2)}) collective-permute-start(bf16[64,1800]{1,0:T(8,128)(2,1)S(1)} %collective-permute-done.1.refs_2_.refs_0_), channel_id=1, source_target_pairs={{0,8},{1,9},{2,10},{3,11},{4,12},{5,13},{6,14},{7,15},{8,0},{9,1},... | collective-permute-start | bytes 691208 | tf_op jit(solution)/shard_map/ppermute | solution.py:204
  12.6 2.7 %collective-permute-start.4 = (bf16[64,1800]{1,0:T(8,128)(2,1)S(1)}, bf16[64,1800]{1,0:T(8,128)(2,1)S(1)}, u32[]{:S(2)}, u32[]{:S(2)}) collective-permute-start(bf16[64,1800]{1,0:T(8,128)(2,1)S(1)} %collective-permute-done.3.refs_4_.refs_2_), channel_id=1, source_target_pairs={{0,8},{1,9},{2,10},{3,11},{4,12},{5,13},{6,14},{7,15},{8,0},{9,1},... | collective-permute-start | bytes 691208 | tf_op jit(solution)/shard_map/ppermute | solution.py:204
  12.6 2.7 %copy-start.2 = (bf16[1800,64]{0,1:T(8,128)(2,1)S(1)}, bf16[1800,64]{0,1:T(8,128)(2,1)}, u32[]{:S(2)}) copy-start(bf16[1800,64]{0,1:T(8,128)(2,1)} %param.4) | copy-start | bytes 691204
  16.9 1.6 %collective-permute-start.9 = (bf16[64,1800]{1,0:T(8,128)(2,1)S(1)}, bf16[64,1800]{1,0:T(8,128)(2,1)S(1)}, u32[]{:S(2)}, u32[]{:S(2)}) collective-permute-start(bf16[64,1800]{1,0:T(8,128)(2,1)S(1)} %shard_map.53), channel_id=1, source_target_pairs={{0,8},{1,9},{2,10},{3,11},{4,12},{5,13},{6,14},{7,15},{8,0},{9,1},... | collective-permute-start | bytes 691208 | tf_op jit(solution)/shard_map/ppermute | solution.py:204
  19.8 6.9 %collective-permute-start.11 = (bf16[272,128]{1,0:T(8,128)(2,1)S(1)}, bf16[272,128]{1,0:T(8,128)(2,1)S(1)}, u32[]{:S(2)}, u32[]{:S(2)}) collective-permute-start(bf16[272,128]{1,0:T(8,128)(2,1)S(1)} %get-tuple-element.26), channel_id=1, source_target_pairs={{0,6},{1,7},{2,4},{3,5},{4,2},{5,3},{6,0},{7,1},{8,14},{9,15},{10,... | collective-permute-start | bytes 208904 | tf_op jit(solution)/shard_map/ppermute | solution.py:204
  22.2 6.2 %collective-permute-start.12 = (bf16[272,128]{1,0:T(8,128)(2,1)S(1)}, bf16[272,128]{1,0:T(8,128)(2,1)S(1)}, u32[]{:S(2)}, u32[]{:S(2)}) collective-permute-start(bf16[272,128]{1,0:T(8,128)(2,1)S(1)} %get-tuple-element.27), channel_id=1, source_target_pairs={{0,2},{1,3},{2,0},{3,1},{4,6},{5,7},{6,4},{7,5},{8,10},{9,11},{10,... | collective-permute-start | bytes 208904 | tf_op jit(solution)/shard_map/ppermute | solution.py:204
  23.2 6.0 %collective-permute-start.10 = (bf16[272,128]{1,0:T(8,128)(2,1)S(1)}, bf16[272,128]{1,0:T(8,128)(2,1)S(1)}, u32[]{:S(2)}, u32[]{:S(2)}) collective-permute-start(bf16[272,128]{1,0:T(8,128)(2,1)S(1)} %get-tuple-element.24), channel_id=1, source_target_pairs={{0,4},{1,5},{2,6},{3,7},{4,0},{5,1},{6,2},{7,3},{8,12},{9,13},{10,... | collective-permute-start | bytes 208904 | tf_op jit(solution)/shard_map/ppermute | solution.py:204

commit v6 on v4

--- a/solution.py
+++ b/solution.py
@@ -217,10 +217,10 @@
 
     blocks = n_tgt // 2
     half = blocks // 2
-    offsets = [0, *range(2 * half, n_tgt - 2, 2), n_tgt - 2, *range(2, 2 * half, 2)]
+    offsets = list(range(0, n_tgt, 2))
     late = after(source_feat, near)
     sources = [source_feat]
-    sources += [swap(source_feat if t == 2 * half else late, t=t) for t in offsets[1:]]
+    sources += [swap(source_feat if t == offsets[-1] else late, t=t) for t in offsets[1:]]
 
     projt = proj.T
     rows = [coord_rows((tgt ^ k) * count, count) for k in (0, 1)]

time: 30.2 us -> 30.1 us (level)
  starting transfers between devices: 15.4 us -> 14.7 us
  waiting for transfers between devices: 7.41 us -> 8.08 us
    ppermute x13, waiting for transfers between devices: 7.41 us -> 8.08 us  [permute(): return lax.ppermute(x, axes, pairs)]
    ppermute x13, starting transfers between devices: 15.4 us -> 14.7 us  [permute(): return lax.ppermute(x, axes, pairs)]
where the time goes in v6:
time: 30.1 us; the launch traced here: 30 us
  starting transfers between devices  14.7 us (49%)
  waiting for transfers between devices  8.08 us (27%)
  Pallas kernels  5.86 us (19%)
  between operations  0.81 us (3%)
  other arithmetic  0.42 us (1%)
    ppermute x13, starting transfers between devices, permute(): return lax.ppermute(x, axes, pairs)  14.7 us
    ppermute x13, waiting for transfers between devices, permute(): return lax.ppermute(x, axes, pairs)  8.08 us
    pallas_call x6, Pallas kernels, call(): pl.pallas_call(kernel, out_shape=outs, scratch_shapes=scratch, compiler_p...  5.84 us
  transfers between devices with their start and end apart: 13, of which 6 were waited for; matrix products, arithmetic and copies ran while one was open for 2% of the time, Pallas kernels for 12%

profile of v6, /device:TPU:0, one launch (start us, length us, event | category | flops | bytes accessed | tf_op | source)
XLA Modules:
  0.0 30.0 jit_solution(803556466394651236)
XLA Ops:
  0.6 3.0 %collective-permute-start.1 = (bf16[64,1800]{1,0:T(8,128)(2,1)}, bf16[64,1800]{1,0:T(8,128)(2,1)S(1)}, u32[]{:S(2)}, u32[]{:S(2)}) collective-permute-start(bf16[64,1800]{1,0:T(8,128)(2,1)} %bitcast.4), channel_id=1, source_target_pairs={{0,16},{1,17},{2,18},{3,19},{4,20},{5,21},{6,22},{7,23},{8,9},{9,8... | collective-permute-start | bytes 691208 | tf_op jit(solution)/shard_map/ppermute | solution.py:204
  3.6 0.0 collective-permute-start
  3.6 3.6 %collective-permute-start.7 = (bf16[128,256]{1,0:T(8,128)(2,1)}, bf16[128,256]{1,0:T(8,128)(2,1)S(1)}, u32[]{:S(2)}, u32[]{:S(2)}) collective-permute-start(bf16[128,256]{1,0:T(8,128)(2,1)} %refs_9_.1), channel_id=1, source_target_pairs={{0,6},{1,7},{2,4},{3,5},{4,2},{5,3},{6,0},{7,1},{8,14},{9,15},{10,... | collective-permute-start | bytes 196616 | tf_op jit(solution)/shard_map/ppermute | solution.py:204
  7.4 0.0 collective-permute-done.refs_0_.refs_1_
  7.4 1.1 %collective-permute-start.3 = (bf16[64,1800]{1,0:T(8,128)(2,1)S(1)}, bf16[64,1800]{1,0:T(8,128)(2,1)S(1)}, u32[]{:S(2)}, u32[]{:S(2)}) collective-permute-start(bf16[64,1800]{1,0:T(8,128)(2,1)S(1)} %collective-permute-done.refs_0_.refs_1_), channel_id=1, source_target_pairs={{0,16},{1,17},{2,18},{3,19},{4,20},{5,21},{6,22},{7,23},{8,9},{9,8... | collective-permute-start | bytes 691208 | tf_op jit(solution)/shard_map/ppermute | solution.py:204
  8.6 0.0 copy-start
  8.6 0.2 collective-permute-start.6
  8.8 1.6 %collective-permute-start.5 = (bf16[128,256]{1,0:T(8,128)(2,1)S(1)}, bf16[128,256]{1,0:T(8,128)(2,1)S(1)}, u32[]{:S(2)}, u32[]{:S(2)}) collective-permute-start(bf16[128,256]{1,0:T(8,128)(2,1)S(1)} %shard_map.50), channel_id=1, source_target_pairs={{0,2},{1,3},{2,0},{3,1},{4,6},{5,7},{6,4},{7,5},{8,10},{9,11},{10,... | collective-permute-start | bytes 196616 | tf_op jit(solution)/shard_map/ppermute | solution.py:204
  10.4 0.0 collective-permute-done.1.refs_2_.refs_0_
  10.4 1.4 %collective-permute-start.8 = (bf16[64,1800]{1,0:T(8,128)(2,1)S(1)}, bf16[64,1800]{1,0:T(8,128)(2,1)S(1)}, u32[]{:S(2)}, u32[]{:S(2)}) collective-permute-start(bf16[64,1800]{1,0:T(8,128)(2,1)S(1)} %collective-permute-done.1.refs_2_.refs_0_), channel_id=1, source_target_pairs={{0,1},{1,0},{2,3},{3,2},{4,5},{5,4},{6,7},{7,6},{8,24},{9,25},{10,... | collective-permute-start | bytes 691208 | tf_op jit(solution)/shard_map/ppermute | solution.py:204
  11.7 0.0 collective-permute-done.7.refs_12_.refs_1_
  11.7 0.0 collective-permute-start.2
  11.7 2.4 %collective-permute-done.3.refs_4_.refs_2_ = bf16[64,1800]{1,0:T(8,128)(2,1)S(1)} collective-permute-done((bf16[64,1800]{1,0:T(8,128)(2,1)S(1)}, bf16[64,1800]{1,0:T(8,128)(2,1)S(1)}, u32[]{:S(2)}, u32[]{:S(2)}) %collective-permute-start.3) | collective-permute-done | bytes 230432 | tf_op jit(solution)/shard_map/ppermute | solution.py:204
  14.1 0.0 collective-permute-start.4
  14.1 0.3 fusion.6
  14.4 0.1 copy.5
  14.5 0.1 collective-permute-done.5.refs_10_
  14.6 1.0 %collective-permute-done.4.refs_5_.refs_3_ = bf16[64,1800]{1,0:T(8,128)(2,1)S(1)} collective-permute-done((bf16[64,1800]{1,0:T(8,128)(2,1)S(1)}, bf16[64,1800]{1,0:T(8,128)(2,1)S(1)}, u32[]{:S(2)}, u32[]{:S(2)}) %collective-permute-start.4) | collective-permute-done | bytes 230432 | tf_op jit(solution)/shard_map/ppermute | solution.py:204
  15.6 1.6 %shard_map.51 = (f32[1,256]{1,0:T(1,128)S(1)}, f32[272,256]{1,0:T(8,128)S(1)}, bf16[256,256]{1,0:T(8,128)(2,1)S(1)}, bf16[272,1800]{1,0:T(8,128)(2,1)S(1)}) custom-call(bf16[64,1800]{1,0:T(8,128)(2,1)S(1)} %bitcast.6, bf16[64,1800]{1,0:T(8,128)(2,1)S(1)} %collective-permute-done.refs_0_.refs_1_, bf16[64,1800]{1,0:T(8,128)(2,1)S(1)} %collective-permute-done.1.refs_2_.refs_0_, ...), custom_call_target="tpu_custom_call" | custom-call | flops 1179648000 | bytes 3354112 | tf_op jit(solution)/shard_map/pallas_call | solution.py:165
  17.2 0.2 collective-permute-start.9
  17.5 1.1 %shard_map.52 = (f32[1,256]{1,0:T(1,128)S(1)}, f32[272,256]{1,0:T(8,128)S(1)}, bf16[256,256]{1,0:T(8,128)(2,1)S(1)}) custom-call(bf16[128,256]{1,0:T(8,128)(2,1)S(1)} %collective-permute-done.6.refs_11_.refs_0_, bf16[128,256]{1,0:T(8,128)(2,1)S(1)} %collective-permute-done.7.refs_12_.refs_1_, bf16[256,256]{1,0:T(8,128)(2,1)S(1)} %copy-done, ...), custom_call_target="tpu_custom_call" | custom-call | flops 1179648000 | bytes 1651968 | tf_op jit(solution)/shard_map/pallas_call | solution.py:165
  18.6 0.2 collective-permute-done.9.refs_5_
  18.8 1.3 %shard_map.54 = (bf16[272,128]{1,0:T(8,128)(2,1)S(1)}, bf16[272,128]{1,0:T(8,128)(2,1)S(1)}, bf16[272,1800]{1,0:T(8,128)(2,1)S(1)}) custom-call(bf16[64,1800]{1,0:T(8,128)(2,1)S(1)} %collective-permute-done.1.refs_2_.refs_0_, bf16[64,1800]{1,0:T(8,128)(2,1)S(1)} %collective-permute-done.2.refs_3_.refs_1_, ...), custom_call_target="tpu_custom_call" | custom-call | flops 1179648000 | bytes 3100160 | tf_op jit(solution)/shard_map/pallas_call | solution.py:165
  20.1 0.6 %collective-permute-start.11 = (bf16[272,128]{1,0:T(8,128)(2,1)S(1)}, bf16[272,128]{1,0:T(8,128)(2,1)S(1)}, u32[]{:S(2)}, u32[]{:S(2)}) collective-permute-start(bf16[272,128]{1,0:T(8,128)(2,1)S(1)} %get-tuple-element.26), channel_id=1, source_target_pairs={{0,4},{1,5},{2,6},{3,7},{4,0},{5,1},{6,2},{7,3},{8,12},{9,13},{10,... | collective-permute-start | bytes 208904 | tf_op jit(solution)/shard_map/ppermute | solution.py:204
  20.8 1.6 %collective-permute-start.12 = (bf16[272,128]{1,0:T(8,128)(2,1)S(1)}, bf16[272,128]{1,0:T(8,128)(2,1)S(1)}, u32[]{:S(2)}, u32[]{:S(2)}) collective-permute-start(bf16[272,128]{1,0:T(8,128)(2,1)S(1)} %get-tuple-element.27), channel_id=1, source_target_pairs={{0,6},{1,7},{2,4},{3,5},{4,2},{5,3},{6,0},{7,1},{8,14},{9,15},{10,... | collective-permute-start | bytes 208904 | tf_op jit(solution)/shard_map/ppermute | solution.py:204
  22.4 1.0 %shard_map.55 = (bf16[272,128]{1,0:T(8,128)(2,1)S(1)}, bf16[272,128]{1,0:T(8,128)(2,1)S(1)}) custom-call(f32[1,256]{1,0:T(1,128)S(1)} %get-tuple-element.16.refs_0_, f32[272,256]{1,0:T(8,128)S(1)} %get-tuple-element.17.refs_1_, bf16[256,256]{1,0:T(8,128)(2,1)S(1)} %get-tuple-element.18.refs_2_, f32[1,256]{1,0:T(1,128)S(1)} %get-tuple-element.20.refs_8_.refs_3_, ...), custom_call_target="tpu_custom_call" | custom-call | flops 1179648000 | bytes 1939712 | tf_op jit(solution)/shard_map/pallas_call | solution.py:165
  23.4 1.4 %collective-permute-start.10 = (bf16[272,128]{1,0:T(8,128)(2,1)S(1)}, bf16[272,128]{1,0:T(8,128)(2,1)S(1)}, u32[]{:S(2)}, u32[]{:S(2)}) collective-permute-start(bf16[272,128]{1,0:T(8,128)(2,1)S(1)} %get-tuple-element.24), channel_id=1, source_target_pairs={{0,2},{1,3},{2,0},{3,1},{4,6},{5,7},{6,4},{7,5},{8,10},{9,11},{10,... | collective-permute-start | bytes 208904 | tf_op jit(solution)/shard_map/ppermute | solution.py:204
  24.8 3.1 %collective-permute-done.11.refs_1_ = bf16[272,128]{1,0:T(8,128)(2,1)S(1)} collective-permute-done((bf16[272,128]{1,0:T(8,128)(2,1)S(1)}, bf16[272,128]{1,0:T(8,128)(2,1)S(1)}, u32[]{:S(2)}, u32[]{:S(2)}) %collective-permute-start.11) | collective-permute-done | bytes 69664 | tf_op jit(solution)/shard_map/ppermute | solution.py:204
  27.9 0.0 collective-permute-done.12.refs_2_
  27.9 0.1 shard_map.56
  27.9 1.3 %collective-permute-done.10.refs_0_ = bf16[272,128]{1,0:T(8,128)(2,1)S(1)} collective-permute-done((bf16[272,128]{1,0:T(8,128)(2,1)S(1)}, bf16[272,128]{1,0:T(8,128)(2,1)S(1)}, u32[]{:S(2)}, u32[]{:S(2)}) %collective-permute-start.10) | collective-permute-done | bytes 69664 | tf_op jit(solution)/shard_map/ppermute | solution.py:204
  29.2 0.8 %shard_map.57 = (f32[2,128]{1,0:T(2,128)}, bf16[128,256]{1,0:T(8,128)(2,1)}) custom-call(bf16[272,128]{1,0:T(8,128)(2,1)S(1)} %collective-permute-done.10.refs_0_, f32[1,128]{1,0:T(1,128)S(1)} %get-tuple-element.28.refs_1_, f32[264,128]{1,0:T(8,128)S(1)} %get-tuple-element.29.refs_2_, f32[2,128]{1,0:T(2,128)S(1)} %pad_maximum_fusion.refs_3_), custom_call_target="tpu_custom_call" | custom-call | flops 278528 | bytes 272896 | tf_op jit(solution)/shard_map/pallas_call | solution.py:165
  (21 shorter events, 0.2 us)
Async XLA Ops:
  0.6 7.9 %copy-start.1 = (bf16[128,256]{1,0:T(8,128)(2,1)S(1)}, bf16[128,256]{1,0:T(8,128)(2,1)}, u32[]{:S(2)}) copy-start(bf16[128,256]{1,0:T(8,128)(2,1)} %refs_9_.1) | copy-start | bytes 196612
  0.6 9.7 %collective-permute-start.1 = (bf16[64,1800]{1,0:T(8,128)(2,1)}, bf16[64,1800]{1,0:T(8,128)(2,1)S(1)}, u32[]{:S(2)}, u32[]{:S(2)}) collective-permute-start(bf16[64,1800]{1,0:T(8,128)(2,1)} %bitcast.4), channel_id=1, source_target_pairs={{0,16},{1,17},{2,18},{3,19},{4,20},{5,21},{6,22},{7,23},{8,9},{9,8... | collective-permute-start | bytes 691208 | tf_op jit(solution)/shard_map/ppermute | solution.py:204
  3.6 3.7 %collective-permute-start = (bf16[64,1800]{1,0:T(8,128)(2,1)}, bf16[64,1800]{1,0:T(8,128)(2,1)S(1)}, u32[]{:S(2)}, u32[]{:S(2)}) collective-permute-start(bf16[64,1800]{1,0:T(8,128)(2,1)} %bitcast.5), channel_id=1, source_target_pairs={{0,8},{1,9},{2,10},{3,11},{4,12},{5,13},{6,14},{7,15},{8,0},{9,1},... | collective-permute-start | bytes 691208 | tf_op jit(solution)/shard_map/ppermute | solution.py:204
  3.6 8.1 %collective-permute-start.7 = (bf16[128,256]{1,0:T(8,128)(2,1)}, bf16[128,256]{1,0:T(8,128)(2,1)S(1)}, u32[]{:S(2)}, u32[]{:S(2)}) collective-permute-start(bf16[128,256]{1,0:T(8,128)(2,1)} %refs_9_.1), channel_id=1, source_target_pairs={{0,6},{1,7},{2,4},{3,5},{4,2},{5,3},{6,0},{7,1},{8,14},{9,15},{10,... | collective-permute-start | bytes 196616 | tf_op jit(solution)/shard_map/ppermute | solution.py:204
  7.4 6.7 %collective-permute-start.3 = (bf16[64,1800]{1,0:T(8,128)(2,1)S(1)}, bf16[64,1800]{1,0:T(8,128)(2,1)S(1)}, u32[]{:S(2)}, u32[]{:S(2)}) collective-permute-start(bf16[64,1800]{1,0:T(8,128)(2,1)S(1)} %collective-permute-done.refs_0_.refs_1_), channel_id=1, source_target_pairs={{0,16},{1,17},{2,18},{3,19},{4,20},{5,21},{6,22},{7,23},{8,9},{9,8... | collective-permute-start | bytes 691208 | tf_op jit(solution)/shard_map/ppermute | solution.py:204
  8.6 5.8 %copy-start = (bf16[256,256]{1,0:T(8,128)(2,1)S(1)}, bf16[256,256]{1,0:T(8,128)(2,1)}, u32[]{:S(2)}) copy-start(bf16[256,256]{1,0:T(8,128)(2,1)} %refs_2_.1) | copy-start | bytes 393220
  8.6 5.9 %collective-permute-start.6 = (bf16[128,256]{1,0:T(8,128)(2,1)S(1)}, bf16[128,256]{1,0:T(8,128)(2,1)S(1)}, u32[]{:S(2)}, u32[]{:S(2)}) collective-permute-start(bf16[128,256]{1,0:T(8,128)(2,1)S(1)} %shard_map.50), channel_id=1, source_target_pairs={{0,4},{1,5},{2,6},{3,7},{4,0},{5,1},{6,2},{7,3},{8,12},{9,13},{10,... | collective-permute-start | bytes 196616 | tf_op jit(solution)/shard_map/ppermute | solution.py:204
  8.8 5.8 %collective-permute-start.5 = (bf16[128,256]{1,0:T(8,128)(2,1)S(1)}, bf16[128,256]{1,0:T(8,128)(2,1)S(1)}, u32[]{:S(2)}, u32[]{:S(2)}) collective-permute-start(bf16[128,256]{1,0:T(8,128)(2,1)S(1)} %shard_map.50), channel_id=1, source_target_pairs={{0,2},{1,3},{2,0},{3,1},{4,6},{5,7},{6,4},{7,5},{8,10},{9,11},{10,... | collective-permute-start | bytes 196616 | tf_op jit(solution)/shard_map/ppermute | solution.py:204
  10.4 6.8 %collective-permute-start.8 = (bf16[64,1800]{1,0:T(8,128)(2,1)S(1)}, bf16[64,1800]{1,0:T(8,128)(2,1)S(1)}, u32[]{:S(2)}, u32[]{:S(2)}) collective-permute-start(bf16[64,1800]{1,0:T(8,128)(2,1)S(1)} %collective-permute-done.1.refs_2_.refs_0_), channel_id=1, source_target_pairs={{0,1},{1,0},{2,3},{3,2},{4,5},{5,4},{6,7},{7,6},{8,24},{9,25},{10,... | collective-permute-start | bytes 691208 | tf_op jit(solution)/shard_map/ppermute | solution.py:204
  11.7 2.9 %collective-permute-start.2 = (bf16[64,1800]{1,0:T(8,128)(2,1)S(1)}, bf16[64,1800]{1,0:T(8,128)(2,1)S(1)}, u32[]{:S(2)}, u32[]{:S(2)}) collective-permute-start(bf16[64,1800]{1,0:T(8,128)(2,1)S(1)} %collective-permute-done.1.refs_2_.refs_0_), channel_id=1, source_target_pairs={{0,8},{1,9},{2,10},{3,11},{4,12},{5,13},{6,14},{7,15},{8,0},{9,1},... | collective-permute-start | bytes 691208 | tf_op jit(solution)/shard_map/ppermute | solution.py:204
  14.1 1.5 %collective-permute-start.4 = (bf16[64,1800]{1,0:T(8,128)(2,1)S(1)}, bf16[64,1800]{1,0:T(8,128)(2,1)S(1)}, u32[]{:S(2)}, u32[]{:S(2)}) collective-permute-start(bf16[64,1800]{1,0:T(8,128)(2,1)S(1)} %collective-permute-done.3.refs_4_.refs_2_), channel_id=1, source_target_pairs={{0,8},{1,9},{2,10},{3,11},{4,12},{5,13},{6,14},{7,15},{8,0},{9,1},... | collective-permute-start | bytes 691208 | tf_op jit(solution)/shard_map/ppermute | solution.py:204
  14.1 1.5 %copy-start.2 = (bf16[1800,64]{0,1:T(8,128)(2,1)S(1)}, bf16[1800,64]{0,1:T(8,128)(2,1)}, u32[]{:S(2)}) copy-start(bf16[1800,64]{0,1:T(8,128)(2,1)} %param.4) | copy-start | bytes 691204
  17.2 1.6 %collective-permute-start.9 = (bf16[64,1800]{1,0:T(8,128)(2,1)S(1)}, bf16[64,1800]{1,0:T(8,128)(2,1)S(1)}, u32[]{:S(2)}, u32[]{:S(2)}) collective-permute-start(bf16[64,1800]{1,0:T(8,128)(2,1)S(1)} %shard_map.53), channel_id=1, source_target_pairs={{0,8},{1,9},{2,10},{3,11},{4,12},{5,13},{6,14},{7,15},{8,0},{9,1},... | collective-permute-start | bytes 691208 | tf_op jit(solution)/shard_map/ppermute | solution.py:204
  20.1 7.7 %collective-permute-start.11 = (bf16[272,128]{1,0:T(8,128)(2,1)S(1)}, bf16[272,128]{1,0:T(8,128)(2,1)S(1)}, u32[]{:S(2)}, u32[]{:S(2)}) collective-permute-start(bf16[272,128]{1,0:T(8,128)(2,1)S(1)} %get-tuple-element.26), channel_id=1, source_target_pairs={{0,4},{1,5},{2,6},{3,7},{4,0},{5,1},{6,2},{7,3},{8,12},{9,13},{10,... | collective-permute-start | bytes 208904 | tf_op jit(solution)/shard_map/ppermute | solution.py:204
  20.8 7.1 %collective-permute-start.12 = (bf16[272,128]{1,0:T(8,128)(2,1)S(1)}, bf16[272,128]{1,0:T(8,128)(2,1)S(1)}, u32[]{:S(2)}, u32[]{:S(2)}) collective-permute-start(bf16[272,128]{1,0:T(8,128)(2,1)S(1)} %get-tuple-element.27), channel_id=1, source_target_pairs={{0,6},{1,7},{2,4},{3,5},{4,2},{5,3},{6,0},{7,1},{8,14},{9,15},{10,... | collective-permute-start | bytes 208904 | tf_op jit(solution)/shard_map/ppermute | solution.py:204
  23.4 5.9 %collective-permute-start.10 = (bf16[272,128]{1,0:T(8,128)(2,1)S(1)}, bf16[272,128]{1,0:T(8,128)(2,1)S(1)}, u32[]{:S(2)}, u32[]{:S(2)}) collective-permute-start(bf16[272,128]{1,0:T(8,128)(2,1)S(1)} %get-tuple-element.24), channel_id=1, source_target_pairs={{0,2},{1,3},{2,0},{3,1},{4,6},{5,7},{6,4},{7,5},{8,10},{9,11},{10,... | collective-permute-start | bytes 208904 | tf_op jit(solution)/shard_map/ppermute | solution.py:204

commit v7 on v4

--- a/solution.py
+++ b/solution.py
@@ -43,8 +43,8 @@
     return jnp.transpose(jnp.broadcast_to(column, (column.shape[0], 128)))[0:1, :]
 
 
-def either(even, odd):
-    return jnp.where(lax.axis_index("src") % 2 == 0, even[...], odd[...])
+def either(odd_first, other):
+    return jnp.where(lax.axis_index("src") % 2 == 1, odd_first[...], other[...])
 
 
 def project(pieces, projt, rows, strip, kext):
@@ -206,8 +206,8 @@
     def swap(x, s=0, t=0):
         return permute(x, lambda a: (s, t))
 
-    turn_one = lambda a: (2, 0) if a % 2 == 0 else (0, 1)
-    turn_two = lambda a: (0, 1) if a % 2 == 0 else (2, 0)
+    turn_one = lambda a: (0, 1) if a % 2 == 0 else (2, 0)
+    turn_two = lambda a: (2, 0) if a % 2 == 0 else (0, 1)
     own = target_feat.T
     near = swap(own, s=1)
     one = permute(own, turn_one)

time: 30.2 us -> 30.2 us (level)
  no operation moved by 1% of the time
where the time goes in v7:
time: 30.2 us; the launch traced here: 30 us
  starting transfers between devices  15.3 us (51%)
  waiting for transfers between devices  7.44 us (25%)
  Pallas kernels  5.86 us (19%)
  between operations  0.83 us (3%)
  other arithmetic  0.42 us (1%)
    ppermute x13, starting transfers between devices, permute(): return lax.ppermute(x, axes, pairs)  15.3 us
    ppermute x13, waiting for transfers between devices, permute(): return lax.ppermute(x, axes, pairs)  7.44 us
    pallas_call x6, Pallas kernels, call(): pl.pallas_call(kernel, out_shape=outs, scratch_shapes=scratch, compiler_p...  5.83 us
  transfers between devices with their start and end apart: 13, of which 6 were waited for; matrix products, arithmetic and copies ran while one was open for 2% of the time, Pallas kernels for 12%

profile of v7, /device:TPU:0, one launch (start us, length us, event | category | flops | bytes accessed | tf_op | source)
XLA Modules:
  0.0 30.0 jit_solution(14804825780509917219)
XLA Ops:
  0.6 3.0 %collective-permute-start.1 = (bf16[64,1800]{1,0:T(8,128)(2,1)}, bf16[64,1800]{1,0:T(8,128)(2,1)S(1)}, u32[]{:S(2)}, u32[]{:S(2)}) collective-permute-start(bf16[64,1800]{1,0:T(8,128)(2,1)} %bitcast.4), channel_id=1, source_target_pairs={{0,1},{1,0},{2,3},{3,2},{4,5},{5,4},{6,7},{7,6},{8,24},{9,25},{10,... | collective-permute-start | bytes 691208 | tf_op jit(solution)/shard_map/ppermute | solution.py:204
  3.7 0.0 collective-permute-start
  3.7 2.6 %collective-permute-start.5 = (bf16[128,256]{1,0:T(8,128)(2,1)}, bf16[128,256]{1,0:T(8,128)(2,1)S(1)}, u32[]{:S(2)}, u32[]{:S(2)}) collective-permute-start(bf16[128,256]{1,0:T(8,128)(2,1)} %refs_9_.1), channel_id=1, source_target_pairs={{0,4},{1,5},{2,6},{3,7},{4,0},{5,1},{6,2},{7,3},{8,12},{9,13},{10,... | collective-permute-start | bytes 196616 | tf_op jit(solution)/shard_map/ppermute | solution.py:204
  6.4 0.0 collective-permute-done.refs_0_.refs_1_
  6.4 1.1 %collective-permute-start.3 = (bf16[64,1800]{1,0:T(8,128)(2,1)S(1)}, bf16[64,1800]{1,0:T(8,128)(2,1)S(1)}, u32[]{:S(2)}, u32[]{:S(2)}) collective-permute-start(bf16[64,1800]{1,0:T(8,128)(2,1)S(1)} %collective-permute-done.refs_0_.refs_1_), channel_id=1, source_target_pairs={{0,1},{1,0},{2,3},{3,2},{4,5},{5,4},{6,7},{7,6},{8,24},{9,25},{10,... | collective-permute-start | bytes 691208 | tf_op jit(solution)/shard_map/ppermute | solution.py:204
  7.5 0.0 copy-start
  7.6 1.6 %collective-permute-start.7 = (bf16[128,256]{1,0:T(8,128)(2,1)S(1)}, bf16[128,256]{1,0:T(8,128)(2,1)S(1)}, u32[]{:S(2)}, u32[]{:S(2)}) collective-permute-start(bf16[128,256]{1,0:T(8,128)(2,1)S(1)} %shard_map.50), channel_id=1, source_target_pairs={{0,2},{1,3},{2,0},{3,1},{4,6},{5,7},{6,4},{7,5},{8,10},{9,11},{10,... | collective-permute-start | bytes 196616 | tf_op jit(solution)/shard_map/ppermute | solution.py:204
  9.2 1.0 %collective-permute-start.6 = (bf16[128,256]{1,0:T(8,128)(2,1)S(1)}, bf16[128,256]{1,0:T(8,128)(2,1)S(1)}, u32[]{:S(2)}, u32[]{:S(2)}) collective-permute-start(bf16[128,256]{1,0:T(8,128)(2,1)S(1)} %shard_map.50), channel_id=1, source_target_pairs={{0,6},{1,7},{2,4},{3,5},{4,2},{5,3},{6,0},{7,1},{8,14},{9,15},{10,... | collective-permute-start | bytes 196616 | tf_op jit(solution)/shard_map/ppermute | solution.py:204
  10.3 0.0 collective-permute-done.1.refs_2_.refs_0_
  10.3 1.3 %collective-permute-start.8 = (bf16[64,1800]{1,0:T(8,128)(2,1)S(1)}, bf16[64,1800]{1,0:T(8,128)(2,1)S(1)}, u32[]{:S(2)}, u32[]{:S(2)}) collective-permute-start(bf16[64,1800]{1,0:T(8,128)(2,1)S(1)} %collective-permute-done.1.refs_2_.refs_0_), channel_id=1, source_target_pairs={{0,16},{1,17},{2,18},{3,19},{4,20},{5,21},{6,22},{7,23},{8,9},{9,8... | collective-permute-start | bytes 691208 | tf_op jit(solution)/shard_map/ppermute | solution.py:204
  11.6 0.0 collective-permute-done.5.refs_10_
  11.6 0.0 collective-permute-start.2
  11.6 1.1 %collective-permute-done.3.refs_4_.refs_2_ = bf16[64,1800]{1,0:T(8,128)(2,1)S(1)} collective-permute-done((bf16[64,1800]{1,0:T(8,128)(2,1)S(1)}, bf16[64,1800]{1,0:T(8,128)(2,1)S(1)}, u32[]{:S(2)}, u32[]{:S(2)}) %collective-permute-start.3) | collective-permute-done | bytes 230432 | tf_op jit(solution)/shard_map/ppermute | solution.py:204
  12.6 0.0 collective-permute-start.4
  12.7 0.3 fusion.6
  13.0 0.1 copy.5
  13.1 0.0 collective-permute-done.7.refs_12_.refs_1_
  13.1 2.2 %collective-permute-done.6.refs_11_.refs_0_ = bf16[128,256]{1,0:T(8,128)(2,1)S(1)} collective-permute-done((bf16[128,256]{1,0:T(8,128)(2,1)S(1)}, bf16[128,256]{1,0:T(8,128)(2,1)S(1)}, u32[]{:S(2)}, u32[]{:S(2)}) %collective-permute-start.6) | collective-permute-done | bytes 65568 | tf_op jit(solution)/shard_map/ppermute | solution.py:204
  15.3 1.6 %shard_map.51 = (f32[1,256]{1,0:T(1,128)S(1)}, f32[272,256]{1,0:T(8,128)S(1)}, bf16[256,256]{1,0:T(8,128)(2,1)S(1)}, bf16[272,1800]{1,0:T(8,128)(2,1)S(1)}) custom-call(bf16[64,1800]{1,0:T(8,128)(2,1)S(1)} %bitcast.6, bf16[64,1800]{1,0:T(8,128)(2,1)S(1)} %collective-permute-done.refs_0_.refs_1_, bf16[64,1800]{1,0:T(8,128)(2,1)S(1)} %collective-permute-done.1.refs_2_.refs_0_, ...), custom_call_target="tpu_custom_call" | custom-call | flops 1179648000 | bytes 3354112 | tf_op jit(solution)/shard_map/pallas_call | solution.py:165
  16.9 0.0 collective-permute-done.8.value_ref.refs_4_
  16.9 0.1 collective-permute-start.9
  17.0 1.1 %shard_map.52 = (f32[1,256]{1,0:T(1,128)S(1)}, f32[272,256]{1,0:T(8,128)S(1)}, bf16[256,256]{1,0:T(8,128)(2,1)S(1)}) custom-call(bf16[128,256]{1,0:T(8,128)(2,1)S(1)} %collective-permute-done.6.refs_11_.refs_0_, bf16[128,256]{1,0:T(8,128)(2,1)S(1)} %collective-permute-done.7.refs_12_.refs_1_, bf16[256,256]{1,0:T(8,128)(2,1)S(1)} %copy-done, ...), custom_call_target="tpu_custom_call" | custom-call | flops 1179648000 | bytes 1651968 | tf_op jit(solution)/shard_map/pallas_call | solution.py:165
  18.2 0.3 %collective-permute-done.9.refs_5_ = bf16[64,1800]{1,0:T(8,128)(2,1)S(1)} collective-permute-done((bf16[64,1800]{1,0:T(8,128)(2,1)S(1)}, bf16[64,1800]{1,0:T(8,128)(2,1)S(1)}, u32[]{:S(2)}, u32[]{:S(2)}) %collective-permute-start.9) | collective-permute-done | bytes 230432 | tf_op jit(solution)/shard_map/ppermute | solution.py:204
  18.5 1.3 %shard_map.54 = (bf16[272,128]{1,0:T(8,128)(2,1)S(1)}, bf16[272,128]{1,0:T(8,128)(2,1)S(1)}, bf16[272,1800]{1,0:T(8,128)(2,1)S(1)}) custom-call(bf16[64,1800]{1,0:T(8,128)(2,1)S(1)} %collective-permute-done.1.refs_2_.refs_0_, bf16[64,1800]{1,0:T(8,128)(2,1)S(1)} %collective-permute-done.2.refs_3_.refs_1_, ...), custom_call_target="tpu_custom_call" | custom-call | flops 1179648000 | bytes 3100160 | tf_op jit(solution)/shard_map/pallas_call | solution.py:165
  19.8 2.4 %collective-permute-start.11 = (bf16[272,128]{1,0:T(8,128)(2,1)S(1)}, bf16[272,128]{1,0:T(8,128)(2,1)S(1)}, u32[]{:S(2)}, u32[]{:S(2)}) collective-permute-start(bf16[272,128]{1,0:T(8,128)(2,1)S(1)} %get-tuple-element.26), channel_id=1, source_target_pairs={{0,6},{1,7},{2,4},{3,5},{4,2},{5,3},{6,0},{7,1},{8,14},{9,15},{10,... | collective-permute-start | bytes 208904 | tf_op jit(solution)/shard_map/ppermute | solution.py:204
  22.2 1.0 %shard_map.55 = (bf16[272,128]{1,0:T(8,128)(2,1)S(1)}, bf16[272,128]{1,0:T(8,128)(2,1)S(1)}) custom-call(f32[1,256]{1,0:T(1,128)S(1)} %get-tuple-element.16.refs_0_, f32[272,256]{1,0:T(8,128)S(1)} %get-tuple-element.17.refs_1_, bf16[256,256]{1,0:T(8,128)(2,1)S(1)} %get-tuple-element.18.refs_2_, f32[1,256]{1,0:T(1,128)S(1)} %get-tuple-element.20.refs_8_.refs_3_, ...), custom_call_target="tpu_custom_call" | custom-call | flops 1179648000 | bytes 1939712 | tf_op jit(solution)/shard_map/pallas_call | solution.py:165
  23.2 2.1 %collective-permute-start.10 = (bf16[272,128]{1,0:T(8,128)(2,1)S(1)}, bf16[272,128]{1,0:T(8,128)(2,1)S(1)}, u32[]{:S(2)}, u32[]{:S(2)}) collective-permute-start(bf16[272,128]{1,0:T(8,128)(2,1)S(1)} %get-tuple-element.24), channel_id=1, source_target_pairs={{0,4},{1,5},{2,6},{3,7},{4,0},{5,1},{6,2},{7,3},{8,12},{9,13},{10,... | collective-permute-start | bytes 208904 | tf_op jit(solution)/shard_map/ppermute | solution.py:204
  25.3 1.4 %collective-permute-done.11.refs_1_ = bf16[272,128]{1,0:T(8,128)(2,1)S(1)} collective-permute-done((bf16[272,128]{1,0:T(8,128)(2,1)S(1)}, bf16[272,128]{1,0:T(8,128)(2,1)S(1)}, u32[]{:S(2)}, u32[]{:S(2)}) %collective-permute-start.11) | collective-permute-done | bytes 69664 | tf_op jit(solution)/shard_map/ppermute | solution.py:204
  26.7 1.8 %collective-permute-done.12.refs_2_ = bf16[272,128]{1,0:T(8,128)(2,1)S(1)} collective-permute-done((bf16[272,128]{1,0:T(8,128)(2,1)S(1)}, bf16[272,128]{1,0:T(8,128)(2,1)S(1)}, u32[]{:S(2)}, u32[]{:S(2)}) %collective-permute-start.12) | collective-permute-done | bytes 69664 | tf_op jit(solution)/shard_map/ppermute | solution.py:204
  28.5 0.1 shard_map.56
  28.6 0.7 %collective-permute-done.10.refs_0_ = bf16[272,128]{1,0:T(8,128)(2,1)S(1)} collective-permute-done((bf16[272,128]{1,0:T(8,128)(2,1)S(1)}, bf16[272,128]{1,0:T(8,128)(2,1)S(1)}, u32[]{:S(2)}, u32[]{:S(2)}) %collective-permute-start.10) | collective-permute-done | bytes 69664 | tf_op jit(solution)/shard_map/ppermute | solution.py:204
  29.2 0.8 %shard_map.57 = (f32[2,128]{1,0:T(2,128)}, bf16[128,256]{1,0:T(8,128)(2,1)}) custom-call(bf16[272,128]{1,0:T(8,128)(2,1)S(1)} %collective-permute-done.10.refs_0_, f32[1,128]{1,0:T(1,128)S(1)} %get-tuple-element.28.refs_1_, f32[264,128]{1,0:T(8,128)S(1)} %get-tuple-element.29.refs_2_, f32[2,128]{1,0:T(2,128)S(1)} %pad_maximum_fusion.refs_3_), custom_call_target="tpu_custom_call" | custom-call | flops 278528 | bytes 272896 | tf_op jit(solution)/shard_map/pallas_call | solution.py:165
  (21 shorter events, 0.2 us)
Async XLA Ops:
  0.6 6.9 %copy-start.1 = (bf16[128,256]{1,0:T(8,128)(2,1)S(1)}, bf16[128,256]{1,0:T(8,128)(2,1)}, u32[]{:S(2)}) copy-start(bf16[128,256]{1,0:T(8,128)(2,1)} %refs_9_.1) | copy-start | bytes 196612
  0.6 9.6 %collective-permute-start.1 = (bf16[64,1800]{1,0:T(8,128)(2,1)}, bf16[64,1800]{1,0:T(8,128)(2,1)S(1)}, u32[]{:S(2)}, u32[]{:S(2)}) collective-permute-start(bf16[64,1800]{1,0:T(8,128)(2,1)} %bitcast.4), channel_id=1, source_target_pairs={{0,1},{1,0},{2,3},{3,2},{4,5},{5,4},{6,7},{7,6},{8,24},{9,25},{10,... | collective-permute-start | bytes 691208 | tf_op jit(solution)/shard_map/ppermute | solution.py:204
  3.7 2.7 %collective-permute-start = (bf16[64,1800]{1,0:T(8,128)(2,1)}, bf16[64,1800]{1,0:T(8,128)(2,1)S(1)}, u32[]{:S(2)}, u32[]{:S(2)}) collective-permute-start(bf16[64,1800]{1,0:T(8,128)(2,1)} %bitcast.5), channel_id=1, source_target_pairs={{0,8},{1,9},{2,10},{3,11},{4,12},{5,13},{6,14},{7,15},{8,0},{9,1},... | collective-permute-start | bytes 691208 | tf_op jit(solution)/shard_map/ppermute | solution.py:204
  3.7 7.9 %collective-permute-start.5 = (bf16[128,256]{1,0:T(8,128)(2,1)}, bf16[128,256]{1,0:T(8,128)(2,1)S(1)}, u32[]{:S(2)}, u32[]{:S(2)}) collective-permute-start(bf16[128,256]{1,0:T(8,128)(2,1)} %refs_9_.1), channel_id=1, source_target_pairs={{0,4},{1,5},{2,6},{3,7},{4,0},{5,1},{6,2},{7,3},{8,12},{9,13},{10,... | collective-permute-start | bytes 196616 | tf_op jit(solution)/shard_map/ppermute | solution.py:204
  6.4 6.3 %collective-permute-start.3 = (bf16[64,1800]{1,0:T(8,128)(2,1)S(1)}, bf16[64,1800]{1,0:T(8,128)(2,1)S(1)}, u32[]{:S(2)}, u32[]{:S(2)}) collective-permute-start(bf16[64,1800]{1,0:T(8,128)(2,1)S(1)} %collective-permute-done.refs_0_.refs_1_), channel_id=1, source_target_pairs={{0,1},{1,0},{2,3},{3,2},{4,5},{5,4},{6,7},{7,6},{8,24},{9,25},{10,... | collective-permute-start | bytes 691208 | tf_op jit(solution)/shard_map/ppermute | solution.py:204
  7.5 5.4 %copy-start = (bf16[256,256]{1,0:T(8,128)(2,1)S(1)}, bf16[256,256]{1,0:T(8,128)(2,1)}, u32[]{:S(2)}) copy-start(bf16[256,256]{1,0:T(8,128)(2,1)} %refs_2_.1) | copy-start | bytes 393220
  7.6 5.5 %collective-permute-start.7 = (bf16[128,256]{1,0:T(8,128)(2,1)S(1)}, bf16[128,256]{1,0:T(8,128)(2,1)S(1)}, u32[]{:S(2)}, u32[]{:S(2)}) collective-permute-start(bf16[128,256]{1,0:T(8,128)(2,1)S(1)} %shard_map.50), channel_id=1, source_target_pairs={{0,2},{1,3},{2,0},{3,1},{4,6},{5,7},{6,4},{7,5},{8,10},{9,11},{10,... | collective-permute-start | bytes 196616 | tf_op jit(solution)/shard_map/ppermute | solution.py:204
  9.2 6.1 %collective-permute-start.6 = (bf16[128,256]{1,0:T(8,128)(2,1)S(1)}, bf16[128,256]{1,0:T(8,128)(2,1)S(1)}, u32[]{:S(2)}, u32[]{:S(2)}) collective-permute-start(bf16[128,256]{1,0:T(8,128)(2,1)S(1)} %shard_map.50), channel_id=1, source_target_pairs={{0,6},{1,7},{2,4},{3,5},{4,2},{5,3},{6,0},{7,1},{8,14},{9,15},{10,... | collective-permute-start | bytes 196616 | tf_op jit(solution)/shard_map/ppermute | solution.py:204
  10.3 6.6 %collective-permute-start.8 = (bf16[64,1800]{1,0:T(8,128)(2,1)S(1)}, bf16[64,1800]{1,0:T(8,128)(2,1)S(1)}, u32[]{:S(2)}, u32[]{:S(2)}) collective-permute-start(bf16[64,1800]{1,0:T(8,128)(2,1)S(1)} %collective-permute-done.1.refs_2_.refs_0_), channel_id=1, source_target_pairs={{0,16},{1,17},{2,18},{3,19},{4,20},{5,21},{6,22},{7,23},{8,9},{9,8... | collective-permute-start | bytes 691208 | tf_op jit(solution)/shard_map/ppermute | solution.py:204
  11.6 3.7 %collective-permute-start.2 = (bf16[64,1800]{1,0:T(8,128)(2,1)S(1)}, bf16[64,1800]{1,0:T(8,128)(2,1)S(1)}, u32[]{:S(2)}, u32[]{:S(2)}) collective-permute-start(bf16[64,1800]{1,0:T(8,128)(2,1)S(1)} %collective-permute-done.1.refs_2_.refs_0_), channel_id=1, source_target_pairs={{0,8},{1,9},{2,10},{3,11},{4,12},{5,13},{6,14},{7,15},{8,0},{9,1},... | collective-permute-start | bytes 691208 | tf_op jit(solution)/shard_map/ppermute | solution.py:204
  12.6 2.6 %collective-permute-start.4 = (bf16[64,1800]{1,0:T(8,128)(2,1)S(1)}, bf16[64,1800]{1,0:T(8,128)(2,1)S(1)}, u32[]{:S(2)}, u32[]{:S(2)}) collective-permute-start(bf16[64,1800]{1,0:T(8,128)(2,1)S(1)} %collective-permute-done.3.refs_4_.refs_2_), channel_id=1, source_target_pairs={{0,8},{1,9},{2,10},{3,11},{4,12},{5,13},{6,14},{7,15},{8,0},{9,1},... | collective-permute-start | bytes 691208 | tf_op jit(solution)/shard_map/ppermute | solution.py:204
  12.6 2.6 %copy-start.2 = (bf16[1800,64]{0,1:T(8,128)(2,1)S(1)}, bf16[1800,64]{0,1:T(8,128)(2,1)}, u32[]{:S(2)}) copy-start(bf16[1800,64]{0,1:T(8,128)(2,1)} %param.4) | copy-start | bytes 691204
  16.9 1.6 %collective-permute-start.9 = (bf16[64,1800]{1,0:T(8,128)(2,1)S(1)}, bf16[64,1800]{1,0:T(8,128)(2,1)S(1)}, u32[]{:S(2)}, u32[]{:S(2)}) collective-permute-start(bf16[64,1800]{1,0:T(8,128)(2,1)S(1)} %shard_map.53), channel_id=1, source_target_pairs={{0,8},{1,9},{2,10},{3,11},{4,12},{5,13},{6,14},{7,15},{8,0},{9,1},... | collective-permute-start | bytes 691208 | tf_op jit(solution)/shard_map/ppermute | solution.py:204
  19.8 6.9 %collective-permute-start.11 = (bf16[272,128]{1,0:T(8,128)(2,1)S(1)}, bf16[272,128]{1,0:T(8,128)(2,1)S(1)}, u32[]{:S(2)}, u32[]{:S(2)}) collective-permute-start(bf16[272,128]{1,0:T(8,128)(2,1)S(1)} %get-tuple-element.26), channel_id=1, source_target_pairs={{0,6},{1,7},{2,4},{3,5},{4,2},{5,3},{6,0},{7,1},{8,14},{9,15},{10,... | collective-permute-start | bytes 208904 | tf_op jit(solution)/shard_map/ppermute | solution.py:204
  22.2 6.3 %collective-permute-start.12 = (bf16[272,128]{1,0:T(8,128)(2,1)S(1)}, bf16[272,128]{1,0:T(8,128)(2,1)S(1)}, u32[]{:S(2)}, u32[]{:S(2)}) collective-permute-start(bf16[272,128]{1,0:T(8,128)(2,1)S(1)} %get-tuple-element.27), channel_id=1, source_target_pairs={{0,2},{1,3},{2,0},{3,1},{4,6},{5,7},{6,4},{7,5},{8,10},{9,11},{10,... | collective-permute-start | bytes 208904 | tf_op jit(solution)/shard_map/ppermute | solution.py:204
  23.2 6.0 %collective-permute-start.10 = (bf16[272,128]{1,0:T(8,128)(2,1)S(1)}, bf16[272,128]{1,0:T(8,128)(2,1)S(1)}, u32[]{:S(2)}, u32[]{:S(2)}) collective-permute-start(bf16[272,128]{1,0:T(8,128)(2,1)S(1)} %get-tuple-element.24), channel_id=1, source_target_pairs={{0,4},{1,5},{2,6},{3,7},{4,0},{5,1},{6,2},{7,3},{8,12},{9,13},{10,... | collective-permute-start | bytes 208904 | tf_op jit(solution)/shard_map/ppermute | solution.py:204
